TPU v7x, 512 devices: a whole 4x4x16 slice. The times are simulated.
512 devices in a mesh: frames: 8 (over z_hi, y), pix: 64 (over x, z_lo, core).
Axes of the slice: x: 4, y: 4, z: 16 (z_hi: 2, z_lo: 8; z = z_hi * 8 + z_lo), core: 2. Of those that a mesh axis runs over, the one named last changes fastest.
Arguments:
- intensity: float32 [3072, 98304], P('frames', 'pix'), as said below
- circle_index: int32 [65536], P('pix'), may hold values from 0 to 1535
- pixel_mask: int32 [98304], P('pix'), may hold values 0 or 1
Outputs:
- correlation: float32 [5, 3072, 384], P(None, ('frames', 'pix'))
Inputs may be any that keep to these rules, and one draw needn't show every extreme that they name: `circle_index`: each device's entries name columns of that device's own shard of the band. `intensity`: Positive.
All inputs are finite; a program needn't handle non-finite values. No bound on the sum of `pixel_mask` on one device may be relied on, other than what follows from the above.
Results may differ from a plain program's by a relative error of at most 0.0003.
Values sent between devices are 32-bit elements; how exact they have to be, the bound alone decides.
No kernel may reach another device: no remote copies, remote signals or barrier semaphores. Data moves between devices by JAX's collectives and lax.ppermute only.
A program may use at most 64 MiB of HBM per device.

v0:
```python
import jax
import jax.numpy as jnp
from jax import lax
from jax.sharding import PartitionSpec as P


def passed_along(value, axis, by):
    length = lax.axis_size(axis)
    return lax.ppermute(value, axis, [(i, (i + by) % length) for i in range(length)])


def cross_rows(left, right):
    return lax.dot_general(
        left,
        right,
        (((1,), (1,)), ((), ())),
        precision=lax.Precision.HIGHEST,
        preferred_element_type=jnp.float32,
    )


def body(intensity, circle_index, pixel_mask):
    frame_block = jnp.take(intensity, circle_index, axis=1)
    weights = jnp.take(pixel_mask, circle_index).astype(jnp.float32)
    weighted = frame_block * weights[None, :]
    partial_sums = jnp.dot(frame_block, weights, precision=lax.Precision.HIGHEST)
    frame_sums, good_count = lax.psum((partial_sums, jnp.sum(weights)), "pix")
    half_loop = lax.axis_size("frames") // 2
    block_size = frame_block.shape[0]
    block_rows = block_size // lax.axis_size("pix")
    blocks = [frame_block]
    totals = [frame_sums]
    moving_block = frame_block
    moving_sums = frame_sums
    for shift_step in range(half_loop):
        moving_block, moving_sums = passed_along((moving_block, moving_sums), "frames", 1)
        blocks.append(moving_block)
        totals.append(moving_sums)
    own_sums = lax.dynamic_slice_in_dim(
        frame_sums, lax.axis_index("pix") * block_rows, block_rows, 0
    )
    results = []
    for other_block, other_sums in zip(blocks, totals):

        def tile_term(first_row, row_count, other_block=other_block):
            return cross_rows(weighted, other_block)

        summed = lax.psum_scatter(
            tile_term(jnp.int32(0), lax.axis_size("pix") * block_rows),
            "pix",
            scatter_dimension=0,
            tiled=True,
        )
        results.append(summed * good_count / (own_sums[:, None] * other_sums[None, :]))
    return jnp.stack(results)


def solution(mesh):
    return jax.shard_map(
        body,
        mesh=mesh,
        in_specs=(P("frames", "pix"), P("pix"), P("pix")),
        out_specs=P(None, ("frames", "pix"), None),
        check_vma=False,
    )
```

profile of v0, /device:TPU:1, one launch (start us, length us, event | category | flops | bytes accessed | tf_op | source)
XLA Modules:
  0.0 1443.7 jit_solution(17200751002357895159)
XLA Ops:
  7.3 6.2 gather_fusion.1
  14.0 2.0 copy.6
  16.0 5.4 gather_fusion
  21.6 4.0 collective-permute-start
  25.7 69.9 %collective-permute-done = f32[384,1024]{0,1:T(8,128)S(1)} collective-permute-done((f32[384,1024]{0,1:T(8,128)S(1)}, f32[384,1024]{0,1:T(8,128)S(1)}, u32[]{:S(2)}, u32[]{:S(2)}) %collective-permute-start) | collective-permute-done | bytes 1572896 | tf_op jit(solution)/shard_map/ppermute | solution.py:9
  95.6 1.9 collective-permute-start.2
  97.5 118.7 %collective-permute-done.2 = f32[384,1024]{0,1:T(8,128)S(1)} collective-permute-done((f32[384,1024]{0,1:T(8,128)S(1)}, f32[384,1024]{0,1:T(8,128)S(1)}, u32[]{:S(2)}, u32[]{:S(2)}) %collective-permute-start.2) | collective-permute-done | bytes 1572896 | tf_op jit(solution)/shard_map/ppermute | solution.py:9
  216.2 1.9 collective-permute-start.4
  218.2 136.1 %collective-permute-done.4 = f32[384,1024]{0,1:T(8,128)S(1)} collective-permute-done((f32[384,1024]{0,1:T(8,128)S(1)}, f32[384,1024]{0,1:T(8,128)S(1)}, u32[]{:S(2)}, u32[]{:S(2)}) %collective-permute-start.4) | collective-permute-done | bytes 1572896 | tf_op jit(solution)/shard_map/ppermute | solution.py:9
  354.2 2.1 collective-permute-start.6
  356.3 4.2 fusion
  360.5 3.9 fusion.8
  364.4 3.9 fusion.6
  368.3 4.1 fusion.4
  372.4 124.1 %collective-permute-done.6 = f32[384,1024]{0,1:T(8,128)S(1)} collective-permute-done((f32[384,1024]{0,1:T(8,128)S(1)}, f32[384,1024]{0,1:T(8,128)S(1)}, u32[]{:S(2)}, u32[]{:S(2)}) %collective-permute-start.6) | collective-permute-done | bytes 1572896 | tf_op jit(solution)/shard_map/ppermute | solution.py:9
  496.5 3.9 fusion.2
  500.5 1.1 convolution_reduce_fusion
  501.6 304.9 %all-reduce.5 = (f32[384]{0:T(512)S(1)}, f32[]{:T(128)}) all-reduce(f32[384]{0:T(512)S(1)} %convolution_reduce_fusion, f32[]{:T(128)} %get-tuple-element.12), channel_id=1, replica_groups=mesh['frames'=8,'pix'=64] {'pix'}, use_global_device_ids=true, to_apply=%region_3.4 | all-reduce | flops 385 | bytes 3080 | tf_op jit(solution)/shard_map/psum | solution.py:27
  806.5 1.9 collective-permute-start.1
  808.4 13.2 collective-permute-done.1
  821.7 1.9 collective-permute-start.3
  823.6 13.2 collective-permute-done.3
  836.8 1.9 collective-permute-start.5
  838.8 1.3 dynamic-slice
  840.7 11.2 collective-permute-done.5
  851.9 1.9 collective-permute-start.7
  853.9 574.6 %all-reduce.9.cloned.1.call-done = (f32[384,384]{1,0:T(8,128)}, f32[384,384]{1,0:T(8,128)}, f32[384,384]{1,0:T(8,128)}, f32[384,384]{1,0:T(8,128)}, f32[384,384]{1,0:T(8,128)}) async-done(((f32[384,384]{1,0:T(8,128)}, f32[384,384]{1,0:T(8,128)}, f32[384,384]{1,0:T(8,128)}, f32[384,384]{1,0:T(8,128)}, f32[384,384]{1,0:T(8,128)}), (f32[384,384]{1,0:T(8,128)}, f32[384,384]{1,0:T(8,128)}, f32[384,384]{1,0:T(8,128)}, ...) | async-done | bytes 2949136
  1428.4 1.4 fusion.32
  1429.9 1.4 fusion.29
  1431.3 1.4 fusion.26
  1432.8 1.4 fusion.23
  1434.8 2.0 fusion.20
  (15 shorter events, 2.2 us)
Async XLA Ops:
  6.5 0.7 copy-start
  6.5 1421.9 %all-reduce.9.cloned.1.call-start = ((), (), s32[]{:S(2)}) async-start(), calls=%async_computation | async-start | bytes 5898240
  7.2 6.2 copy-start.2
  7.2 6.8 copy-start.1
  21.6 73.9 %collective-permute-start = (f32[384,1024]{0,1:T(8,128)S(1)}, f32[384,1024]{0,1:T(8,128)S(1)}, u32[]{:S(2)}, u32[]{:S(2)}) collective-permute-start(f32[384,1024]{0,1:T(8,128)S(1)} %select_bitcast_fusion), channel_id=1, source_target_pairs={{0,64},{64,128},{128,192},{192,256},{256,320},{320,384},{384,448},... | collective-permute-start | bytes 4718600 | tf_op jit(solution)/shard_map/ppermute | solution.py:9
  95.6 120.7 %collective-permute-start.2 = (f32[384,1024]{0,1:T(8,128)S(1)}, f32[384,1024]{0,1:T(8,128)S(1)}, u32[]{:S(2)}, u32[]{:S(2)}) collective-permute-start(f32[384,1024]{0,1:T(8,128)S(1)} %collective-permute-done), channel_id=1, source_target_pairs={{0,64},{64,128},{128,192},{192,256},{256,320},{320,384},{384,448},... | collective-permute-start | bytes 4718600 | tf_op jit(solution)/shard_map/ppermute | solution.py:9
  216.2 138.0 %collective-permute-start.4 = (f32[384,1024]{0,1:T(8,128)S(1)}, f32[384,1024]{0,1:T(8,128)S(1)}, u32[]{:S(2)}, u32[]{:S(2)}) collective-permute-start(f32[384,1024]{0,1:T(8,128)S(1)} %collective-permute-done.2), channel_id=1, source_target_pairs={{0,64},{64,128},{128,192},{192,256},{256,320},{320,384},{384,448},... | collective-permute-start | bytes 4718600 | tf_op jit(solution)/shard_map/ppermute | solution.py:9
  354.2 142.3 %collective-permute-start.6 = (f32[384,1024]{0,1:T(8,128)S(1)}, f32[384,1024]{0,1:T(8,128)S(1)}, u32[]{:S(2)}, u32[]{:S(2)}) collective-permute-start(f32[384,1024]{0,1:T(8,128)S(1)} %collective-permute-done.4), channel_id=1, source_target_pairs={{0,64},{64,128},{128,192},{192,256},{256,320},{320,384},{384,448},... | collective-permute-start | bytes 4718600 | tf_op jit(solution)/shard_map/ppermute | solution.py:9
  806.5 15.1 %collective-permute-start.1 = (f32[384]{0:T(512)S(1)}, f32[384]{0:T(512)S(1)}, u32[]{:S(2)}, u32[]{:S(2)}) collective-permute-start(f32[384]{0:T(512)S(1)} %get-tuple-element.5), channel_id=1, source_target_pairs={{0,64},{64,128},{128,192},{192,256},{256,320},{320,384},{384,448},... | collective-permute-start | bytes 4616 | tf_op jit(solution)/shard_map/ppermute | solution.py:9
  821.7 15.1 %collective-permute-start.3 = (f32[384]{0:T(512)S(1)}, f32[384]{0:T(512)S(1)}, u32[]{:S(2)}, u32[]{:S(2)}) collective-permute-start(f32[384]{0:T(512)S(1)} %collective-permute-done.1), channel_id=1, source_target_pairs={{0,64},{64,128},{128,192},{192,256},{256,320},{320,384},{384,448},... | collective-permute-start | bytes 4616 | tf_op jit(solution)/shard_map/ppermute | solution.py:9
  836.8 15.1 %collective-permute-start.5 = (f32[384]{0:T(512)S(1)}, f32[384]{0:T(512)S(1)}, u32[]{:S(2)}, u32[]{:S(2)}) collective-permute-start(f32[384]{0:T(512)S(1)} %collective-permute-done.3), channel_id=1, source_target_pairs={{0,64},{64,128},{128,192},{192,256},{256,320},{320,384},{384,448},... | collective-permute-start | bytes 4616 | tf_op jit(solution)/shard_map/ppermute | solution.py:9
  851.9 582.3 %collective-permute-start.7 = (f32[384]{0:T(512)S(1)}, f32[384]{0:T(512)S(1)}, u32[]{:S(2)}, u32[]{:S(2)}) collective-permute-start(f32[384]{0:T(512)S(1)} %collective-permute-done.5), channel_id=1, source_target_pairs={{0,64},{64,128},{128,192},{192,256},{256,320},{320,384},{384,448},... | collective-permute-start | bytes 4616 | tf_op jit(solution)/shard_map/ppermute | solution.py:9
  1434.2 0.6 copy-start.3
Sparse Core Ops, SparseCore 0:
  500.6 927.8 all-reduce.8
where the time goes:
time: 1450 us; the launch traced here: 1440 us
  waiting for transfers between devices  1060 us (73%)
  blocking collectives  305 us (21%)
  matrix products  21.1 us (1%)
  starting transfers between devices  17.6 us (1%)
  local copies, waits for them, and re-layouts  15.5 us (1%)
    unnamed x2, waiting for transfers between devices  575 us
    ppermute x8, waiting for transfers between devices, passed_along(): lax.ppermute(value, axis, [(i, (i + by) % length) for i in range(length)])  486 us
    psum x1, blocking collectives, body(): frame_sums, good_count = lax.psum((partial_sums, jnp.sum(weights)), 'pix')  305 us
  transfers between devices with their start and end apart: 9, of which 8 were waited for; matrix products, arithmetic and copies ran while one was open for 2% of the time, Pallas kernels for 0%

commit v1 on v0

v1 whole, which is shorter than its diff:
```python
import functools

import jax
import jax.numpy as jnp
from jax import lax
from jax.experimental import pallas as pl
from jax.experimental.pallas import tpu as pltpu
from jax.sharding import PartitionSpec as P

NY, NX, NZL = 4, 4, 8
NZ = 2 * NZL
CLASSES = 4
SHIFTS = 5
ROWS = 6
WIDTHS = (256, 256)
VMEM = pl.BlockSpec(memory_space=pltpu.VMEM)
SMEM = pl.BlockSpec(memory_space=pltpu.SMEM)
PARAMS = pltpu.CompilerParams(vmem_limit_bytes=24 * 1024 * 1024)
F32 = jnp.float32


def device_id(x, y, z, core):
    return ((z // NZL) * NY + y) * (NX * NZL * 2) + (x * NZL + z % NZL) * 2 + core


def send(value, target):
    pairs = []
    for x in range(NX):
        for y in range(NY):
            for z in range(NZ):
                for core in range(2):
                    to = target(x, y, z, core)
                    if to is not None:
                        pairs.append((device_id(x, y, z, core), device_id(*to)))
    return lax.ppermute(value, ("frames", "pix"), pairs)


def split2(value):
    high = value.astype(jnp.bfloat16)
    return high, (value - high.astype(F32)).astype(jnp.bfloat16)


def split3(value):
    high = value.astype(jnp.bfloat16)
    return (high, *split2(value - high.astype(F32)))


def dot_nn(left, right):
    return jnp.dot(left, right, preferred_element_type=F32)


def dot_nt(left, right):
    return lax.dot_general(left, right, (((1,), (1,)), ((), ())), preferred_element_type=F32)


def select_kernel(begin, width, place, image, index, mask, first, second, count):
    band = image.shape[1]
    half = index.shape[1] // 2
    start = pl.multiple_of(place[0] * half, half)
    other = pl.multiple_of((1 - place[0]) * half, half)
    wanted = jnp.concatenate(
        [index[:, pl.ds(start + begin, width)], index[:, pl.ds(other + begin, width)]], axis=1
    )
    columns = lax.broadcasted_iota(jnp.int32, (band, 2 * width), 0)
    hot = (columns == wanted).astype(F32).astype(jnp.bfloat16)
    good = mask[...].astype(F32)
    picked = sum(dot_nn(part, hot) for part in reversed(split3(image[...] * good)))
    first[...] = picked[:, :width]
    second[...] = picked[:, width:]
    goods = dot_nn(jnp.broadcast_to(good, (8, band)).astype(jnp.bfloat16), hot)
    count[...] = jnp.broadcast_to(jnp.sum(goods, axis=1, keepdims=True), (8, 128))


def select(begin, width, place, image, index, mask):
    frames, band = image.shape
    block = jax.ShapeDtypeStruct((frames, width), F32)
    return pl.pallas_call(
        functools.partial(select_kernel, begin, width),
        out_shape=(block, block, jax.ShapeDtypeStruct((8, 128), F32)),
        in_specs=[SMEM, VMEM, VMEM, VMEM],
        out_specs=(VMEM, VMEM, VMEM),
        compiler_params=PARAMS,
        cost_estimate=pl.CostEstimate(
            flops=2 * frames * band * 2 * width * 3, bytes_accessed=frames * band * 4, transcendentals=0
        ),
        name="select",
    )(place, image, index, mask)


def gram_kernel(slots, has_previous, place, count, own, back1, back3, back2a, back2b, *refs):
    taken = 2 * len(slots) if has_previous else 0
    previous, outs, ordered = refs[:taken], refs[taken:-1], refs[-1]
    y, x, turn = place[1], place[2], place[3]
    frames, width = own.shape[1], own.shape[2]
    per_x = frames // NX
    per_class = per_x // CLASSES
    part = per_x // NZL
    one = jnp.ones((8, width), jnp.bfloat16)
    ones = jnp.concatenate([one, one, jnp.zeros_like(one)], axis=1)
    line = lax.broadcasted_iota(jnp.int32, (8, frames), 0)

    def from_back2(which):
        return jnp.where(which == 0, back2a[...], back2b[...])

    for at, slot in enumerate(slots):
        row_block = place[4] ^ slot
        for xc in range(NX):
            apart = x ^ xc
            chunk = jnp.where(apart == 3, 1, jnp.where(apart == 0, 0, apart + 1))
            for zl in range(NZL):
                kind = (zl - turn) & (CLASSES - 1)
                upper = zl // CLASSES
                ordered[chunk, kind, upper * part : (upper + 1) * part, :] = own[
                    row_block, xc * per_x + zl * part : xc * per_x + (zl + 1) * part, :
                ]
        high, low = split2(ordered[...].reshape(frames, width))
        rows = jnp.concatenate([jnp.concatenate([high, high, low], axis=1), ones], axis=0)
        flips = [row_block ^ (y < shift).astype(jnp.int32) for shift in range(SHIFTS)]
        others = (
            lambda: own[flips[0]],
            lambda: back1[flips[1]],
            lambda: from_back2(flips[2]),
            lambda: back3[flips[3]],
            lambda: own[1 - row_block],
        )
        sums = jnp.where(line == SHIFTS, 0.5 * count[0:1, 0:1], 0.0)
        outer, inner = outs[2 * at], outs[2 * at + 1]
        spots = []
        for side, (kept, given) in enumerate((((0, 1), (2, 3)), ((0, 2), (1, 3)))):
            for to, before, picks in (
                (inner, previous[2 * at + 1 : 2 * at + 2], kept),
                (outer, previous[2 * at : 2 * at + 1], given),
            ):
                for k, chunk in enumerate(picks):
                    for kind in range(2):
                        spots.append((to, before, (side, k, kind), chunk, side * 2 + kind))

        def store(spot, first, value):
            to, before, lead = spot[:3]
            where = (*lead, slice(first, first + value.shape[0]))
            to[where] = value + before[0][where] if before else value

        for shift, other in enumerate(others):
            high, low = split2(other())
            tile = dot_nt(rows, jnp.concatenate([high, low, high], axis=1))
            sums = jnp.where(line == shift, tile[frames:], sums)
            for spot in spots:
                begin = spot[3] * per_x + spot[4] * per_class
                store(spot, shift * per_class, tile[begin : begin + per_class])
        for spot in spots:
            store(spot, SHIFTS * per_class, sums)


def gram(slots, place, count, own, back1, back3, back2, previous=()):
    _, frames, width = own.shape
    operands = [place, count, own, back1, back3, *back2, *previous]
    lines = SHIFTS * frames // NX // CLASSES + 8
    result = jax.ShapeDtypeStruct((2, 2, 2, lines, frames), F32)
    return pl.pallas_call(
        functools.partial(gram_kernel, slots, bool(previous)),
        out_shape=(result,) * (2 * len(slots)),
        in_specs=[SMEM] + [VMEM] * (len(operands) - 1),
        out_specs=(VMEM,) * (2 * len(slots)),
        scratch_shapes=[pltpu.VMEM((NX, CLASSES, frames // NX // CLASSES, width), F32)],
        compiler_params=PARAMS,
        cost_estimate=pl.CostEstimate(
            flops=len(slots) * 5 * 2 * frames * frames * width * 3,
            bytes_accessed=8 * frames * width * 4 + len(slots) * 5 * frames * frames * 4,
            transcendentals=0,
        ),
        name="gram",
    )(*operands)


def share_kernel(place, near, up, down, far, out1, out2, out3, out4, local, parts):
    l2, core, wrong = place[5], place[6], place[7]
    total = (near[0] + up[...]) + (down[...] + far[...])
    for upper in range(2):
        for e in range(2):
            spot = (upper ^ l2, e ^ core)
            for shift in range(SHIFTS):
                begin = shift * 24 + upper * 12 + e * 6
                parts[(*spot, slice(shift * 6, shift * 6 + 6))] = total[begin : begin + 6]
            parts[(*spot, slice(32, 40))] = total[120:128]
            parts[(*spot, slice(30, 32))] = jnp.zeros((2, total.shape[1]), F32)
    right = wrong == 0
    out1[...] = jnp.where(right, parts[0, 1], parts[0, 0])
    out2[...] = jnp.where(right, parts[1, 1], parts[1, 0])
    out3[...] = jnp.where(right, parts[1, 0], parts[0, 1])
    out4[...] = parts[1, 1]
    local[...] = jnp.where(right, parts[0, 0], 0.0)


def share(place, near, up, down, far):
    frames = up.shape[-1]
    piece = jax.ShapeDtypeStruct((40, frames), F32)
    return pl.pallas_call(
        share_kernel,
        out_shape=(piece,) * 5,
        in_specs=[SMEM] + [VMEM] * 4,
        out_specs=(VMEM,) * 5,
        scratch_shapes=[pltpu.VMEM((2, 2, 40, frames), F32)],
        compiler_params=PARAMS,
        name="share",
    )(place, near, up, down, far)


def finish_kernel(place, local, first, second, third, fourth, out):
    total = (local[...] + first[...]) + (second[...] + third[...]) + fourth[...]
    frames = total.shape[1]
    sums = total[32 : 32 + SHIFTS]
    good = total[32 + SHIFTS : 33 + SHIFTS]
    line = lax.broadcasted_iota(jnp.int32, (ROWS, frames), 0)
    lane = lax.broadcasted_iota(jnp.int32, (ROWS, frames), 1)
    mine = jnp.where(lane == line + place[8], sums[0:1], 0.0)
    own = jnp.sum(mine, axis=1, keepdims=True)
    for shift in range(SHIFTS):
        tile = total[shift * ROWS : (shift + 1) * ROWS]
        out[shift] = tile * good / (own * sums[shift : shift + 1])


def finish(place, *pieces):
    frames = pieces[0].shape[1]
    return pl.pallas_call(
        finish_kernel,
        out_shape=jax.ShapeDtypeStruct((SHIFTS, ROWS, frames), F32),
        in_specs=[SMEM] + [VMEM] * 5,
        out_specs=VMEM,
        compiler_params=PARAMS,
        name="finish",
    )(place, *pieces)


def body(intensity, circle_index, pixel_mask):
    frame_at, pix_at = lax.axis_index("frames"), lax.axis_index("pix")
    zh, y = frame_at >> 2, frame_at & 3
    x, zl, core = pix_at >> 4, (pix_at >> 1) & 7, pix_at & 1
    first_label = ((zl >> 2) ^ zh) ^ 1
    own_row = first_label ^ core
    place = jnp.stack(
        [zh, y, x, zl & 3, own_row, zl >> 2, core, zh ^ core, pix_at * ROWS]
    ).astype(jnp.int32)
    index, mask = circle_index[None, :], pixel_mask[None, :]
    quarter = NZ // 4

    def up(value):
        return send(value, lambda x, y, z, c: (x, (y + 1) % NY, z, c))

    def down(value):
        return send(value, lambda x, y, z, c: (x, (y - 1) % NY, z, c))

    picked, begin = [], 0
    for width in WIDTHS:
        picked.append(select(begin, width, place, intensity, index, mask))
        begin += width
    met = []
    for first, second, _ in picked:
        if met:
            first, before = lax.optimization_barrier((first, met[-1][0]))
            second, also = lax.optimization_barrier((second, met[-1][1]))
            met[-1] = (before, also)
        met.append(
            (
                send(first, lambda x, y, z, c: (x, y, (z + quarter) % NZ, c)),
                send(second, lambda x, y, z, c: (x, y, (z - quarter) % NZ, c)),
            )
        )
    partial = ()
    for (_, _, count), arrived in zip(picked, met):
        own = jnp.stack(arrived)
        back1, back3 = up(own), down(own)
        back2 = (up(back1[0]), down(back3[1]))
        if not partial:
            partial = gram((1, 0), place, count, own, back1, back3, back2)
        else:
            give = gram((1,), place, count, own, back1, back3, back2, partial[:2])
            keep = gram((0,), place, count, own, back1, back3, back2, partial[2:])
            partial = (*give, *keep)

    def across(value):
        return send(value, lambda x, y, z, c: (x, y, z, 1 - c))

    def to_p(value):
        return send(value, lambda x, y, z, c: (x ^ 1, y, z, c))

    def to_q(value):
        return send(value, lambda x, y, z, c: (3 - x, y, z, c))

    give_outer, give_inner, keep_outer, keep_inner = partial
    other_outer = across(give_outer)
    other_inner = across(give_inner)
    outer = keep_outer + other_outer
    got = (to_p(outer[0]), to_q(outer[1]))
    inner = keep_inner + other_inner
    mine = [inner[0] + got[0], inner[1] + got[1]]
    near = mine[0][0] + to_q(mine[0][1])
    away = mine[1][0] + to_p(mine[1][1])
    from_below = send(near[1], lambda x, y, z, c: (x, y, (z + 1) % NZ, c))
    from_above = send(away[1], lambda x, y, z, c: (x, y, (z - 1) % NZ, c))
    from_two = send(away[0], lambda x, y, z, c: (x, y, (z + 2 - 4 * c) % NZ, c))
    pieces = share(place, near, from_below, from_above, from_two)

    def owner(right, wrong):
        def target(x, y, z, c):
            at_home = z // NZL == c
            hop = right if at_home else wrong
            if hop is None:
                return None
            upper, cross = hop
            to = (z ^ (4 * upper)) ^ (0 if at_home else NZL)
            return x, y, to, c ^ cross

        return target

    hops = (((0, 1), (0, 0)), ((1, 1), (1, 0)), ((1, 0), (0, 1)), (None, (1, 1)))
    moved = [send(piece, owner(*hop)) for piece, hop in zip(pieces, hops)]
    return finish(place, pieces[4], *moved)


def solution(mesh):
    return jax.shard_map(
        body,
        mesh=mesh,
        in_specs=(P("frames", "pix"), P("pix"), P("pix")),
        out_specs=P(None, ("frames", "pix"), None),
        check_vma=False,
    )
```

time: 1450 us -> 236 us (0.16)
  waiting for transfers between devices: 1060 us -> 114 us
  blocking collectives: 305 us -> 0 us
  starting transfers between devices: 17.6 us -> 101 us
  matrix products: 21.1 us -> 0 us
  Pallas kernels: 0 us -> 16.4 us
    unnamed x2 -> x0, waiting for transfers between devices: 575 us -> none
    ppermute x8 -> x25, waiting for transfers between devices: 486 us -> 114 us  [send(): return lax.ppermute(value, ('frames', 'pix'), pairs)]
    psum x1 -> x0, blocking collectives: 305 us -> none  [body(): frame_sums, good_count = lax.psum((partial_sums, jnp.sum(weights)), 'pix')]
    ppermute x8 -> x25, starting transfers between devices: 17.6 us -> 101 us  [send(): return lax.ppermute(value, ('frames', 'pix'), pairs)]
    dot_general x6 -> x0, matrix products: 21.1 us -> none  [the longest x5 20 us: cross_rows(): lax.dot_general(left, right, (((1,), (1,)), ((), ())), precision=lax.Prec...]
    pallas_call x0 -> x7, Pallas kernels: none -> 16.4 us  [the longest x3 8.83 us: gram(): pl.pallas_call(functools.partial(gram_kernel, slots, bool(previous)), out...]
  transfers between devices with their start and end apart: 9 -> 25, of which waited for: 8 -> 16; matrix products, arithmetic and copies ran while one was open for 2% -> 0% of each run, Pallas kernels for 0% -> 4%
where the time goes in v1:
time: 236 us; the launch traced here: 235 us
  waiting for transfers between devices  114 us (48%)
  starting transfers between devices  101 us (43%)
  Pallas kernels  16.4 us (7%)
  local copies, waits for them, and re-layouts  3.45 us (1%)
    ppermute x25, waiting for transfers between devices, send(): return lax.ppermute(value, ('frames', 'pix'), pairs)  114 us
    ppermute x25, starting transfers between devices, send(): return lax.ppermute(value, ('frames', 'pix'), pairs)  101 us
    pallas_call x3, Pallas kernels, gram(): pl.pallas_call(functools.partial(gram_kernel, slots, bool(previous)), out...  8.83 us
    pallas_call x2, Pallas kernels, select(): pl.pallas_call(functools.partial(select_kernel, begin, width), out_shape=...  5.69 us
  transfers between devices with their start and end apart: 25, of which 16 were waited for; matrix products, arithmetic and copies ran while one was open for 0% of the time, Pallas kernels for 4%

profile of v1, /device:TPU:1, one launch (start us, length us, event | category | flops | bytes accessed | tf_op | source)
XLA Modules:
  0.0 235.5 jit_solution(3891052289023752566)
XLA Ops:
  3.1 2.8 %select.3 = (f32[384,256]{1,0:T(8,128)S(1)}, f32[384,256]{1,0:T(8,128)S(1)}, f32[8,128]{1,0:T(8,128)S(1)}) custom-call(s32[9]{0:T(128)S(1)} %stack.57.place, f32[384,1536]{1,0:T(8,128)S(1)} %copy-done, s32[1,1024]{1,0:T(1,128)S(1)} %bitcast.52, s32[1,1536]{1,0:T(1,128)S(1)} %broadcast_in_dim.7.mask), custom_call_target="tpu_custom_call" | custom-call | flops 1811939328 | bytes 2359296 | tf_op jit(solution)/shard_map/select/pallas_call | solution.py:77
  6.0 9.6 %collective-permute-start = (f32[384,256]{1,0:T(8,128)S(1)}, f32[384,256]{1,0:T(8,128)S(1)}, u32[]{:S(2)}, u32[]{:S(2)}) collective-permute-start(f32[384,256]{1,0:T(8,128)S(1)} %get-tuple-element.30), channel_id=1, source_target_pairs={{0,8},{1,9},{2,10},{3,11},{4,12},{5,13},{6,14},{7,15},{8,256},{9,2... | collective-permute-start | bytes 1179656 | tf_op jit(solution)/shard_map/ppermute | solution.py:35
  15.6 5.6 %collective-permute-start.2 = (f32[384,256]{1,0:T(8,128)S(1)}, f32[384,256]{1,0:T(8,128)S(1)}, u32[]{:S(2)}, u32[]{:S(2)}) collective-permute-start(f32[384,256]{1,0:T(8,128)S(1)} %get-tuple-element.33), channel_id=1, source_target_pairs={{0,264},{1,265},{2,266},{3,267},{4,268},{5,269},{6,270},{7,271},{8... | collective-permute-start | bytes 1179656 | tf_op jit(solution)/shard_map/ppermute | solution.py:35
  21.2 2.9 %select.2 = (f32[384,256]{1,0:T(8,128)S(1)}, f32[384,256]{1,0:T(8,128)S(1)}, f32[8,128]{1,0:T(8,128)S(1)}) custom-call(s32[9]{0:T(128)S(1)} %stack.57.place, f32[384,1536]{1,0:T(8,128)S(1)} %copy-done, s32[1,1024]{1,0:T(1,128)S(1)} %bitcast.53, s32[1,1536]{1,0:T(1,128)S(1)} %broadcast_in_dim.7.mask), custom_call_target="tpu_custom_call" | custom-call | flops 1811939328 | bytes 2359296 | tf_op jit(solution)/shard_map/select/pallas_call | solution.py:77
  24.1 8.3 %collective-permute-done = f32[384,256]{1,0:T(8,128)S(1)} collective-permute-done((f32[384,256]{1,0:T(8,128)S(1)}, f32[384,256]{1,0:T(8,128)S(1)}, u32[]{:S(2)}, u32[]{:S(2)}) %collective-permute-start) | collective-permute-done | bytes 393248 | tf_op jit(solution)/shard_map/ppermute | solution.py:35
  32.4 26.5 %collective-permute-done.2 = f32[384,256]{1,0:T(8,128)S(1)} collective-permute-done((f32[384,256]{1,0:T(8,128)S(1)}, f32[384,256]{1,0:T(8,128)S(1)}, u32[]{:S(2)}, u32[]{:S(2)}) %collective-permute-start.2) | collective-permute-done | bytes 393248 | tf_op jit(solution)/shard_map/ppermute | solution.py:35
  58.9 6.9 %collective-permute-start.1 = (f32[384,256]{1,0:T(8,128)S(1)}, f32[384,256]{1,0:T(8,128)S(1)}, u32[]{:S(2)}, u32[]{:S(2)}) collective-permute-start(f32[384,256]{1,0:T(8,128)S(1)} %get-tuple-element.31), channel_id=1, source_target_pairs={{0,8},{1,9},{2,10},{3,11},{4,12},{5,13},{6,14},{7,15},{8,256},{9,2... | collective-permute-start | bytes 1179656 | tf_op jit(solution)/shard_map/ppermute | solution.py:35
  68.2 3.2 %collective-permute-start.8 = (f32[2,384,256]{2,1,0:T(8,128)S(1)}, f32[2,384,256]{2,1,0:T(8,128)S(1)}, u32[]{:S(2)}, u32[]{:S(2)}) collective-permute-start(f32[2,384,256]{2,1,0:T(8,128)S(1)} %pad_maximum_fusion.1.own), channel_id=1, source_target_pairs={{0,64},{1,65},{2,66},{3,67},{4,68},{5,69},{6,70},{7,71},{8,72},{9,... | collective-permute-start | bytes 2359304 | tf_op jit(solution)/shard_map/ppermute | solution.py:35
  71.4 3.4 %collective-permute-start.9 = (f32[2,384,256]{2,1,0:T(8,128)S(1)}, f32[2,384,256]{2,1,0:T(8,128)S(1)}, u32[]{:S(2)}, u32[]{:S(2)}) collective-permute-start(f32[2,384,256]{2,1,0:T(8,128)S(1)} %pad_maximum_fusion.1.own), channel_id=1, source_target_pairs={{0,192},{1,193},{2,194},{3,195},{4,196},{5,197},{6,198},{7,199},{8... | collective-permute-start | bytes 2359304 | tf_op jit(solution)/shard_map/ppermute | solution.py:35
  74.8 20.7 %collective-permute-done.1 = f32[384,256]{1,0:T(8,128)S(1)} collective-permute-done((f32[384,256]{1,0:T(8,128)S(1)}, f32[384,256]{1,0:T(8,128)S(1)}, u32[]{:S(2)}, u32[]{:S(2)}) %collective-permute-start.1) | collective-permute-done | bytes 393248 | tf_op jit(solution)/shard_map/ppermute | solution.py:35
  95.5 6.9 %collective-permute-done.3 = f32[384,256]{1,0:T(8,128)S(1)} collective-permute-done((f32[384,256]{1,0:T(8,128)S(1)}, f32[384,256]{1,0:T(8,128)S(1)}, u32[]{:S(2)}, u32[]{:S(2)}) %collective-permute-start.3) | collective-permute-done | bytes 393248 | tf_op jit(solution)/shard_map/ppermute | solution.py:35
  102.5 3.2 %collective-permute-start.4 = (f32[2,384,256]{2,1,0:T(8,128)S(1)}, f32[2,384,256]{2,1,0:T(8,128)S(1)}, u32[]{:S(2)}, u32[]{:S(2)}) collective-permute-start(f32[2,384,256]{2,1,0:T(8,128)S(1)} %pad_maximum_fusion.own), channel_id=1, source_target_pairs={{0,64},{1,65},{2,66},{3,67},{4,68},{5,69},{6,70},{7,71},{8,72},{9,... | collective-permute-start | bytes 2359304 | tf_op jit(solution)/shard_map/ppermute | solution.py:35
  105.7 3.4 %collective-permute-start.5 = (f32[2,384,256]{2,1,0:T(8,128)S(1)}, f32[2,384,256]{2,1,0:T(8,128)S(1)}, u32[]{:S(2)}, u32[]{:S(2)}) collective-permute-start(f32[2,384,256]{2,1,0:T(8,128)S(1)} %pad_maximum_fusion.own), channel_id=1, source_target_pairs={{0,192},{1,193},{2,194},{3,195},{4,196},{5,197},{6,198},{7,199},{8... | collective-permute-start | bytes 2359304 | tf_op jit(solution)/shard_map/ppermute | solution.py:35
  111.1 4.6 %collective-permute-start.11 = (f32[384,256]{1,0:T(8,128)S(1)}, f32[384,256]{1,0:T(8,128)S(1)}, u32[]{:S(2)}, u32[]{:S(2)}) collective-permute-start(f32[384,256]{1,0:T(8,128)S(1)} %slice_bitcast_fusion.8), channel_id=1, source_target_pairs={{0,192},{1,193},{2,194},{3,195},{4,196},{5,197},{6,198},{7,199},{8... | collective-permute-start | bytes 1179656 | tf_op jit(solution)/shard_map/ppermute | solution.py:35
  115.7 8.7 %collective-permute-done.4.back1 = f32[2,384,256]{2,1,0:T(8,128)S(1)} collective-permute-done((f32[2,384,256]{2,1,0:T(8,128)S(1)}, f32[2,384,256]{2,1,0:T(8,128)S(1)}, u32[]{:S(2)}, u32[]{:S(2)}) %collective-permute-start.4) | collective-permute-done | bytes 786464 | tf_op jit(solution)/shard_map/ppermute | solution.py:35
  126.4 4.6 %collective-permute-start.7 = (f32[384,256]{1,0:T(8,128)S(1)}, f32[384,256]{1,0:T(8,128)S(1)}, u32[]{:S(2)}, u32[]{:S(2)}) collective-permute-start(f32[384,256]{1,0:T(8,128)S(1)} %slice_bitcast_fusion.10), channel_id=1, source_target_pairs={{0,192},{1,193},{2,194},{3,195},{4,196},{5,197},{6,198},{7,199},{8... | collective-permute-start | bytes 1179656 | tf_op jit(solution)/shard_map/ppermute | solution.py:35
  134.3 4.0 %gram.3 = (f32[2,2,2,128,384]{4,3,2,1,0:T(8,128)S(1)}, f32[2,2,2,128,384]{4,3,2,1,0:T(8,128)S(1)}, f32[2,2,2,128,384]{4,3,2,1,0:T(8,128)S(1)}, f32[2,2,2,128,384]{4,3,2,1,0:T(8,128)S(1)}) custom-call(s32[9]{0:T(128)S(1)} %stack.57.place, f32[8,128]{1,0:T(8,128)S(1)} %get-tuple-element.35.count, f32[2,384,256]{2,1,0:T(8,128)S(1)} %pad_maximum_fusion.1.own, ...), custom_call_target="tpu_custom_call" | custom-call | flops 2264924160 | bytes 9043968 | tf_op jit(solution)/shard_map/gram/pallas_call | solution.py:159
  138.3 3.0 %collective-permute-done.6.back2a = f32[384,256]{1,0:T(8,128)S(1)} collective-permute-done((f32[384,256]{1,0:T(8,128)S(1)}, f32[384,256]{1,0:T(8,128)S(1)}, u32[]{:S(2)}, u32[]{:S(2)}) %collective-permute-start.6) | collective-permute-done | bytes 393248 | tf_op jit(solution)/shard_map/ppermute | solution.py:35
  142.7 2.4 %gram.5 = (f32[2,2,2,128,384]{4,3,2,1,0:T(8,128)S(1)}, f32[2,2,2,128,384]{4,3,2,1,0:T(8,128)S(1)}) custom-call(s32[9]{0:T(128)S(1)} %stack.57.place, f32[8,128]{1,0:T(8,128)S(1)} %get-tuple-element.28.count, f32[2,384,256]{2,1,0:T(8,128)S(1)} %pad_maximum_fusion.own, f32[2,384,256]{2,1,0:T(8,128)S(1)} %collective-permute-done.4.back1, ...), custom_call_target="tpu_custom_call" | custom-call | flops 1132462080 | bytes 6094848 | tf_op jit(solution)/shard_map/gram/pallas_call | solution.py:159
  145.2 3.6 %collective-permute-start.13 = (f32[2,2,2,128,384]{4,3,2,1,0:T(8,128)S(1)}, f32[2,2,2,128,384]{4,3,2,1,0:T(8,128)S(1)}, u32[]{:S(2)}, u32[]{:S(2)}) collective-permute-start(f32[2,2,2,128,384]{4,3,2,1,0:T(8,128)S(1)} %get-tuple-element.45), channel_id=1, source_target_pairs={{0,1},{1,0},{2,3},{3,2},{4,5},{5,4},{6,7},{7,6},{8,9},{9,8},{10,11... | collective-permute-start | bytes 4718600 | tf_op jit(solution)/shard_map/ppermute | solution.py:35
  150.9 2.4 %gram.4 = (f32[2,2,2,128,384]{4,3,2,1,0:T(8,128)S(1)}, f32[2,2,2,128,384]{4,3,2,1,0:T(8,128)S(1)}) custom-call(s32[9]{0:T(128)S(1)} %stack.57.place, f32[8,128]{1,0:T(8,128)S(1)} %get-tuple-element.28.count, f32[2,384,256]{2,1,0:T(8,128)S(1)} %pad_maximum_fusion.own, f32[2,384,256]{2,1,0:T(8,128)S(1)} %collective-permute-done.4.back1, ...), custom_call_target="tpu_custom_call" | custom-call | flops 1132462080 | bytes 6094848 | tf_op jit(solution)/shard_map/gram/pallas_call | solution.py:159
  153.6 3.1 %collective-permute-start.14 = (f32[2,2,128,384]{3,2,1,0:T(8,128)S(1)}, f32[2,2,128,384]{3,2,1,0:T(8,128)S(1)}, u32[]{:S(2)}, u32[]{:S(2)}) collective-permute-start(f32[2,2,128,384]{3,2,1,0:T(8,128)S(1)} %get-tuple-element.54), channel_id=1, source_target_pairs={{0,16},{1,17},{2,18},{3,19},{4,20},{5,21},{6,22},{7,23},{8,24},{9,... | collective-permute-start | bytes 2359304 | tf_op jit(solution)/shard_map/ppermute | solution.py:35
  156.7 3.8 %collective-permute-start.17 = (f32[2,2,128,384]{3,2,1,0:T(8,128)S(1)}, f32[2,2,128,384]{3,2,1,0:T(8,128)S(1)}, u32[]{:S(2)}, u32[]{:S(2)}) collective-permute-start(f32[2,2,128,384]{3,2,1,0:T(8,128)S(1)} %get-tuple-element.53), channel_id=1, source_target_pairs={{0,48},{1,49},{2,50},{3,51},{4,52},{5,53},{6,54},{7,55},{8,56},{9,... | collective-permute-start | bytes 2359304 | tf_op jit(solution)/shard_map/ppermute | solution.py:35
  160.7 13.5 %collective-permute-done.14 = f32[2,2,128,384]{3,2,1,0:T(8,128)S(1)} collective-permute-done((f32[2,2,128,384]{3,2,1,0:T(8,128)S(1)}, f32[2,2,128,384]{3,2,1,0:T(8,128)S(1)}, u32[]{:S(2)}, u32[]{:S(2)}) %collective-permute-start.14) | collective-permute-done | bytes 786464 | tf_op jit(solution)/shard_map/ppermute | solution.py:35
  174.1 4.0 %collective-permute-done.17 = f32[2,2,128,384]{3,2,1,0:T(8,128)S(1)} collective-permute-done((f32[2,2,128,384]{3,2,1,0:T(8,128)S(1)}, f32[2,2,128,384]{3,2,1,0:T(8,128)S(1)}, u32[]{:S(2)}, u32[]{:S(2)}) %collective-permute-start.17) | collective-permute-done | bytes 786464 | tf_op jit(solution)/shard_map/ppermute | solution.py:35
  180.3 3.8 %collective-permute-start.15 = (f32[2,128,384]{2,1,0:T(8,128)S(1)}, f32[2,128,384]{2,1,0:T(8,128)S(1)}, u32[]{:S(2)}, u32[]{:S(2)}) collective-permute-start(f32[2,128,384]{2,1,0:T(8,128)S(1)} %slice_bitcast_fusion.6), channel_id=1, source_target_pairs={{0,48},{1,49},{2,50},{3,51},{4,52},{5,53},{6,54},{7,55},{8,56},{9,... | collective-permute-start | bytes 1179656 | tf_op jit(solution)/shard_map/ppermute | solution.py:35
  184.1 5.1 %collective-permute-done.18 = f32[2,128,384]{2,1,0:T(8,128)S(1)} collective-permute-done((f32[2,128,384]{2,1,0:T(8,128)S(1)}, f32[2,128,384]{2,1,0:T(8,128)S(1)}, u32[]{:S(2)}, u32[]{:S(2)}) %collective-permute-start.18) | collective-permute-done | bytes 393248 | tf_op jit(solution)/shard_map/ppermute | solution.py:35
  193.2 3.4 %collective-permute-start.16 = (f32[128,384]{1,0:T(8,128)S(1)}, f32[128,384]{1,0:T(8,128)S(1)}, u32[]{:S(2)}, u32[]{:S(2)}) collective-permute-start(f32[128,384]{1,0:T(8,128)S(1)} %slice_bitcast_fusion.14), channel_id=1, source_target_pairs={{0,2},{1,3},{2,4},{3,5},{4,6},{5,7},{6,8},{7,9},{8,10},{9,11},{10,... | collective-permute-start | bytes 589832 | tf_op jit(solution)/shard_map/ppermute | solution.py:35
  196.6 4.2 %collective-permute-done.20.far = f32[128,384]{1,0:T(8,128)S(1)} collective-permute-done((f32[128,384]{1,0:T(8,128)S(1)}, f32[128,384]{1,0:T(8,128)S(1)}, u32[]{:S(2)}, u32[]{:S(2)}) %collective-permute-start.20) | collective-permute-done | bytes 196640 | tf_op jit(solution)/shard_map/ppermute | solution.py:35
  201.9 9.2 %collective-permute-start.21 = (f32[40,384]{1,0:T(8,128)S(1)}, f32[40,384]{1,0:T(8,128)S(1)}, u32[]{:S(2)}, u32[]{:S(2)}) collective-permute-start(f32[40,384]{1,0:T(8,128)S(1)} %get-tuple-element.47), channel_id=1, source_target_pairs={{0,1},{1,257},{2,3},{3,259},{4,5},{5,261},{6,7},{7,263},{8,9},{9,2... | collective-permute-start | bytes 184328 | tf_op jit(solution)/shard_map/ppermute | solution.py:35
  213.1 11.7 %collective-permute-start.23 = (f32[40,384]{1,0:T(8,128)S(1)}, f32[40,384]{1,0:T(8,128)S(1)}, u32[]{:S(2)}, u32[]{:S(2)}) collective-permute-start(f32[40,384]{1,0:T(8,128)S(1)} %get-tuple-element.49), channel_id=1, source_target_pairs={{0,8},{1,256},{2,10},{3,258},{4,12},{5,260},{6,14},{7,262},{8,0},{... | collective-permute-start | bytes 184328 | tf_op jit(solution)/shard_map/ppermute | solution.py:35
  227.7 6.5 %collective-permute-done.24.fourth = f32[40,384]{1,0:T(8,128)S(1)} collective-permute-done((f32[40,384]{1,0:T(8,128)S(1)}, f32[40,384]{1,0:T(8,128)S(1)}, u32[]{:S(2)}, u32[]{:S(2)}) %collective-permute-start.24) | collective-permute-done | bytes 61472 | tf_op jit(solution)/shard_map/ppermute | solution.py:35
  (47 shorter events, 30.2 us)
Async XLA Ops:
  0.8 1.7 copy-start
  2.5 0.7 copy-start.1
  6.0 26.4 %collective-permute-start = (f32[384,256]{1,0:T(8,128)S(1)}, f32[384,256]{1,0:T(8,128)S(1)}, u32[]{:S(2)}, u32[]{:S(2)}) collective-permute-start(f32[384,256]{1,0:T(8,128)S(1)} %get-tuple-element.30), channel_id=1, source_target_pairs={{0,8},{1,9},{2,10},{3,11},{4,12},{5,13},{6,14},{7,15},{8,256},{9,2... | collective-permute-start | bytes 1179656 | tf_op jit(solution)/shard_map/ppermute | solution.py:35
  15.6 43.3 %collective-permute-start.2 = (f32[384,256]{1,0:T(8,128)S(1)}, f32[384,256]{1,0:T(8,128)S(1)}, u32[]{:S(2)}, u32[]{:S(2)}) collective-permute-start(f32[384,256]{1,0:T(8,128)S(1)} %get-tuple-element.33), channel_id=1, source_target_pairs={{0,264},{1,265},{2,266},{3,267},{4,268},{5,269},{6,270},{7,271},{8... | collective-permute-start | bytes 1179656 | tf_op jit(solution)/shard_map/ppermute | solution.py:35
  58.9 36.6 %collective-permute-start.1 = (f32[384,256]{1,0:T(8,128)S(1)}, f32[384,256]{1,0:T(8,128)S(1)}, u32[]{:S(2)}, u32[]{:S(2)}) collective-permute-start(f32[384,256]{1,0:T(8,128)S(1)} %get-tuple-element.31), channel_id=1, source_target_pairs={{0,8},{1,9},{2,10},{3,11},{4,12},{5,13},{6,14},{7,15},{8,256},{9,2... | collective-permute-start | bytes 1179656 | tf_op jit(solution)/shard_map/ppermute | solution.py:35
  65.8 36.6 %collective-permute-start.3 = (f32[384,256]{1,0:T(8,128)S(1)}, f32[384,256]{1,0:T(8,128)S(1)}, u32[]{:S(2)}, u32[]{:S(2)}) collective-permute-start(f32[384,256]{1,0:T(8,128)S(1)} %get-tuple-element.34), channel_id=1, source_target_pairs={{0,264},{1,265},{2,266},{3,267},{4,268},{5,269},{6,270},{7,271},{8... | collective-permute-start | bytes 1179656 | tf_op jit(solution)/shard_map/ppermute | solution.py:35
  68.2 40.9 %collective-permute-start.8 = (f32[2,384,256]{2,1,0:T(8,128)S(1)}, f32[2,384,256]{2,1,0:T(8,128)S(1)}, u32[]{:S(2)}, u32[]{:S(2)}) collective-permute-start(f32[2,384,256]{2,1,0:T(8,128)S(1)} %pad_maximum_fusion.1.own), channel_id=1, source_target_pairs={{0,64},{1,65},{2,66},{3,67},{4,68},{5,69},{6,70},{7,71},{8,72},{9,... | collective-permute-start | bytes 2359304 | tf_op jit(solution)/shard_map/ppermute | solution.py:35
  71.4 39.7 %collective-permute-start.9 = (f32[2,384,256]{2,1,0:T(8,128)S(1)}, f32[2,384,256]{2,1,0:T(8,128)S(1)}, u32[]{:S(2)}, u32[]{:S(2)}) collective-permute-start(f32[2,384,256]{2,1,0:T(8,128)S(1)} %pad_maximum_fusion.1.own), channel_id=1, source_target_pairs={{0,192},{1,193},{2,194},{3,195},{4,196},{5,197},{6,198},{7,199},{8... | collective-permute-start | bytes 2359304 | tf_op jit(solution)/shard_map/ppermute | solution.py:35
  102.5 22.0 %collective-permute-start.4 = (f32[2,384,256]{2,1,0:T(8,128)S(1)}, f32[2,384,256]{2,1,0:T(8,128)S(1)}, u32[]{:S(2)}, u32[]{:S(2)}) collective-permute-start(f32[2,384,256]{2,1,0:T(8,128)S(1)} %pad_maximum_fusion.own), channel_id=1, source_target_pairs={{0,64},{1,65},{2,66},{3,67},{4,68},{5,69},{6,70},{7,71},{8,72},{9,... | collective-permute-start | bytes 2359304 | tf_op jit(solution)/shard_map/ppermute | solution.py:35
  105.7 20.7 %collective-permute-start.5 = (f32[2,384,256]{2,1,0:T(8,128)S(1)}, f32[2,384,256]{2,1,0:T(8,128)S(1)}, u32[]{:S(2)}, u32[]{:S(2)}) collective-permute-start(f32[2,384,256]{2,1,0:T(8,128)S(1)} %pad_maximum_fusion.own), channel_id=1, source_target_pairs={{0,192},{1,193},{2,194},{3,195},{4,196},{5,197},{6,198},{7,199},{8... | collective-permute-start | bytes 2359304 | tf_op jit(solution)/shard_map/ppermute | solution.py:35
  109.1 23.7 %collective-permute-start.10 = (f32[384,256]{1,0:T(8,128)S(1)}, f32[384,256]{1,0:T(8,128)S(1)}, u32[]{:S(2)}, u32[]{:S(2)}) collective-permute-start(f32[384,256]{1,0:T(8,128)S(1)} %slice_bitcast_fusion.9), channel_id=1, source_target_pairs={{0,64},{1,65},{2,66},{3,67},{4,68},{5,69},{6,70},{7,71},{8,72},{9,... | collective-permute-start | bytes 1179656 | tf_op jit(solution)/shard_map/ppermute | solution.py:35
  111.1 23.2 %collective-permute-start.11 = (f32[384,256]{1,0:T(8,128)S(1)}, f32[384,256]{1,0:T(8,128)S(1)}, u32[]{:S(2)}, u32[]{:S(2)}) collective-permute-start(f32[384,256]{1,0:T(8,128)S(1)} %slice_bitcast_fusion.8), channel_id=1, source_target_pairs={{0,192},{1,193},{2,194},{3,195},{4,196},{5,197},{6,198},{7,199},{8... | collective-permute-start | bytes 1179656 | tf_op jit(solution)/shard_map/ppermute | solution.py:35
  124.5 16.8 %collective-permute-start.6 = (f32[384,256]{1,0:T(8,128)S(1)}, f32[384,256]{1,0:T(8,128)S(1)}, u32[]{:S(2)}, u32[]{:S(2)}) collective-permute-start(f32[384,256]{1,0:T(8,128)S(1)} %slice_bitcast_fusion.11), channel_id=1, source_target_pairs={{0,64},{1,65},{2,66},{3,67},{4,68},{5,69},{6,70},{7,71},{8,72},{9,... | collective-permute-start | bytes 1179656 | tf_op jit(solution)/shard_map/ppermute | solution.py:35
  126.4 16.3 %collective-permute-start.7 = (f32[384,256]{1,0:T(8,128)S(1)}, f32[384,256]{1,0:T(8,128)S(1)}, u32[]{:S(2)}, u32[]{:S(2)}) collective-permute-start(f32[384,256]{1,0:T(8,128)S(1)} %slice_bitcast_fusion.10), channel_id=1, source_target_pairs={{0,192},{1,193},{2,194},{3,195},{4,196},{5,197},{6,198},{7,199},{8... | collective-permute-start | bytes 1179656 | tf_op jit(solution)/shard_map/ppermute | solution.py:35
  145.2 8.1 %collective-permute-start.13 = (f32[2,2,2,128,384]{4,3,2,1,0:T(8,128)S(1)}, f32[2,2,2,128,384]{4,3,2,1,0:T(8,128)S(1)}, u32[]{:S(2)}, u32[]{:S(2)}) collective-permute-start(f32[2,2,2,128,384]{4,3,2,1,0:T(8,128)S(1)} %get-tuple-element.45), channel_id=1, source_target_pairs={{0,1},{1,0},{2,3},{3,2},{4,5},{5,4},{6,7},{7,6},{8,9},{9,8},{10,11... | collective-permute-start | bytes 4718600 | tf_op jit(solution)/shard_map/ppermute | solution.py:35
  148.7 11.7 %collective-permute-start.12 = (f32[2,2,2,128,384]{4,3,2,1,0:T(8,128)S(1)}, f32[2,2,2,128,384]{4,3,2,1,0:T(8,128)S(1)}, u32[]{:S(2)}, u32[]{:S(2)}) collective-permute-start(f32[2,2,2,128,384]{4,3,2,1,0:T(8,128)S(1)} %get-tuple-element.43), channel_id=1, source_target_pairs={{0,1},{1,0},{2,3},{3,2},{4,5},{5,4},{6,7},{7,6},{8,9},{9,8},{10,11... | collective-permute-start | bytes 4718600 | tf_op jit(solution)/shard_map/ppermute | solution.py:35
  153.6 20.5 %collective-permute-start.14 = (f32[2,2,128,384]{3,2,1,0:T(8,128)S(1)}, f32[2,2,128,384]{3,2,1,0:T(8,128)S(1)}, u32[]{:S(2)}, u32[]{:S(2)}) collective-permute-start(f32[2,2,128,384]{3,2,1,0:T(8,128)S(1)} %get-tuple-element.54), channel_id=1, source_target_pairs={{0,16},{1,17},{2,18},{3,19},{4,20},{5,21},{6,22},{7,23},{8,24},{9,... | collective-permute-start | bytes 2359304 | tf_op jit(solution)/shard_map/ppermute | solution.py:35
  156.7 21.4 %collective-permute-start.17 = (f32[2,2,128,384]{3,2,1,0:T(8,128)S(1)}, f32[2,2,128,384]{3,2,1,0:T(8,128)S(1)}, u32[]{:S(2)}, u32[]{:S(2)}) collective-permute-start(f32[2,2,128,384]{3,2,1,0:T(8,128)S(1)} %get-tuple-element.53), channel_id=1, source_target_pairs={{0,48},{1,49},{2,50},{3,51},{4,52},{5,53},{6,54},{7,55},{8,56},{9,... | collective-permute-start | bytes 2359304 | tf_op jit(solution)/shard_map/ppermute | solution.py:35
  178.4 10.8 %collective-permute-start.18 = (f32[2,128,384]{2,1,0:T(8,128)S(1)}, f32[2,128,384]{2,1,0:T(8,128)S(1)}, u32[]{:S(2)}, u32[]{:S(2)}) collective-permute-start(f32[2,128,384]{2,1,0:T(8,128)S(1)} %slice_bitcast_fusion.4), channel_id=1, source_target_pairs={{0,16},{1,17},{2,18},{3,19},{4,20},{5,21},{6,22},{7,23},{8,24},{9,... | collective-permute-start | bytes 1179656 | tf_op jit(solution)/shard_map/ppermute | solution.py:35
  180.3 12.8 %collective-permute-start.15 = (f32[2,128,384]{2,1,0:T(8,128)S(1)}, f32[2,128,384]{2,1,0:T(8,128)S(1)}, u32[]{:S(2)}, u32[]{:S(2)}) collective-permute-start(f32[2,128,384]{2,1,0:T(8,128)S(1)} %slice_bitcast_fusion.6), channel_id=1, source_target_pairs={{0,48},{1,49},{2,50},{3,51},{4,52},{5,53},{6,54},{7,55},{8,56},{9,... | collective-permute-start | bytes 1179656 | tf_op jit(solution)/shard_map/ppermute | solution.py:35
  189.3 7.3 %collective-permute-start.19 = (f32[128,384]{1,0:T(8,128)S(1)}, f32[128,384]{1,0:T(8,128)S(1)}, u32[]{:S(2)}, u32[]{:S(2)}) collective-permute-start(f32[128,384]{1,0:T(8,128)S(1)} %get-tuple-element.56), channel_id=1, source_target_pairs={{0,270},{1,271},{2,0},{3,1},{4,2},{5,3},{6,4},{7,5},{8,6},{9,7},{1... | collective-permute-start | bytes 589832 | tf_op jit(solution)/shard_map/ppermute | solution.py:35
  191.2 9.6 %collective-permute-start.20 = (f32[128,384]{1,0:T(8,128)S(1)}, f32[128,384]{1,0:T(8,128)S(1)}, u32[]{:S(2)}, u32[]{:S(2)}) collective-permute-start(f32[128,384]{1,0:T(8,128)S(1)} %get-tuple-element.55), channel_id=1, source_target_pairs={{0,4},{1,269},{2,6},{3,271},{4,8},{5,1},{6,10},{7,3},{8,12},{9,5},... | collective-permute-start | bytes 589832 | tf_op jit(solution)/shard_map/ppermute | solution.py:35
  193.2 8.0 %collective-permute-start.16 = (f32[128,384]{1,0:T(8,128)S(1)}, f32[128,384]{1,0:T(8,128)S(1)}, u32[]{:S(2)}, u32[]{:S(2)}) collective-permute-start(f32[128,384]{1,0:T(8,128)S(1)} %slice_bitcast_fusion.14), channel_id=1, source_target_pairs={{0,2},{1,3},{2,4},{3,5},{4,6},{5,7},{6,8},{7,9},{8,10},{9,11},{10,... | collective-permute-start | bytes 589832 | tf_op jit(solution)/shard_map/ppermute | solution.py:35
  201.9 24.8 %collective-permute-start.21 = (f32[40,384]{1,0:T(8,128)S(1)}, f32[40,384]{1,0:T(8,128)S(1)}, u32[]{:S(2)}, u32[]{:S(2)}) collective-permute-start(f32[40,384]{1,0:T(8,128)S(1)} %get-tuple-element.47), channel_id=1, source_target_pairs={{0,1},{1,257},{2,3},{3,259},{4,5},{5,261},{6,7},{7,263},{8,9},{9,2... | collective-permute-start | bytes 184328 | tf_op jit(solution)/shard_map/ppermute | solution.py:35
  211.1 15.6 %collective-permute-start.22 = (f32[40,384]{1,0:T(8,128)S(1)}, f32[40,384]{1,0:T(8,128)S(1)}, u32[]{:S(2)}, u32[]{:S(2)}) collective-permute-start(f32[40,384]{1,0:T(8,128)S(1)} %get-tuple-element.48), channel_id=1, source_target_pairs={{0,9},{1,265},{2,11},{3,267},{4,13},{5,269},{6,15},{7,271},{8,1},{... | collective-permute-start | bytes 184328 | tf_op jit(solution)/shard_map/ppermute | solution.py:35
  213.1 14.7 %collective-permute-start.23 = (f32[40,384]{1,0:T(8,128)S(1)}, f32[40,384]{1,0:T(8,128)S(1)}, u32[]{:S(2)}, u32[]{:S(2)}) collective-permute-start(f32[40,384]{1,0:T(8,128)S(1)} %get-tuple-element.49), channel_id=1, source_target_pairs={{0,8},{1,256},{2,10},{3,258},{4,12},{5,260},{6,14},{7,262},{8,0},{... | collective-permute-start | bytes 184328 | tf_op jit(solution)/shard_map/ppermute | solution.py:35
  224.8 9.4 %collective-permute-start.24 = (f32[40,384]{1,0:T(8,128)S(1)}, f32[40,384]{1,0:T(8,128)S(1)}, u32[]{:S(2)}, u32[]{:S(2)}) collective-permute-start(f32[40,384]{1,0:T(8,128)S(1)} %get-tuple-element.50), channel_id=1, source_target_pairs={{1,264},{3,266},{5,268},{7,270},{9,256},{11,258},{13,260},{15,262}... | collective-permute-start | bytes 184328 | tf_op jit(solution)/shard_map/ppermute | solution.py:35

commit v2 on v1

--- a/solution.py
+++ b/solution.py
@@ -53,45 +53,42 @@
     return lax.dot_general(left, right, (((1,), (1,)), ((), ())), preferred_element_type=F32)
 
 
-def select_kernel(begin, width, place, image, index, mask, first, second, count):
+def select_kernel(flip, place, image, index, mask, out, count):
     band = image.shape[1]
     half = index.shape[1] // 2
-    start = pl.multiple_of(place[0] * half, half)
-    other = pl.multiple_of((1 - place[0]) * half, half)
-    wanted = jnp.concatenate(
-        [index[:, pl.ds(start + begin, width)], index[:, pl.ds(other + begin, width)]], axis=1
-    )
-    columns = lax.broadcasted_iota(jnp.int32, (band, 2 * width), 0)
-    hot = (columns == wanted).astype(F32).astype(jnp.bfloat16)
+    begin = pl.multiple_of((place[0] ^ flip) * half, half)
+    columns = lax.broadcasted_iota(jnp.int32, (band, half), 0)
+    hot = (columns == index[:, pl.ds(begin, half)]).astype(F32).astype(jnp.bfloat16)
     good = mask[...].astype(F32)
     picked = sum(dot_nn(part, hot) for part in reversed(split3(image[...] * good)))
-    first[...] = picked[:, :width]
-    second[...] = picked[:, width:]
+    out[...] = picked
     goods = dot_nn(jnp.broadcast_to(good, (8, band)).astype(jnp.bfloat16), hot)
     count[...] = jnp.broadcast_to(jnp.sum(goods, axis=1, keepdims=True), (8, 128))
 
 
-def select(begin, width, place, image, index, mask):
+def select(flip, place, image, index, mask):
     frames, band = image.shape
-    block = jax.ShapeDtypeStruct((frames, width), F32)
+    half = index.shape[1] // 2
+    block = jax.ShapeDtypeStruct((frames, half), F32)
     return pl.pallas_call(
-        functools.partial(select_kernel, begin, width),
-        out_shape=(block, block, jax.ShapeDtypeStruct((8, 128), F32)),
+        functools.partial(select_kernel, flip),
+        out_shape=(block, jax.ShapeDtypeStruct((8, 128), F32)),
         in_specs=[SMEM, VMEM, VMEM, VMEM],
-        out_specs=(VMEM, VMEM, VMEM),
+        out_specs=(VMEM, VMEM),
         compiler_params=PARAMS,
         cost_estimate=pl.CostEstimate(
-            flops=2 * frames * band * 2 * width * 3, bytes_accessed=frames * band * 4, transcendentals=0
+            flops=2 * frames * band * half * 3, bytes_accessed=frames * band * 4, transcendentals=0
         ),
         name="select",
     )(place, image, index, mask)
 
 
-def gram_kernel(slots, has_previous, place, count, own, back1, back3, back2a, back2b, *refs):
+def gram_kernel(slots, begin, has_previous, place, count, *refs):
+    stay, move = refs[0:4], refs[4:8]
     taken = 2 * len(slots) if has_previous else 0
-    previous, outs, ordered = refs[:taken], refs[taken:-1], refs[-1]
+    previous, outs, ordered = refs[8 : 8 + taken], refs[8 + taken : -1], refs[-1]
     y, x, turn = place[1], place[2], place[3]
-    frames, width = own.shape[1], own.shape[2]
+    frames, width = move[0].shape
     per_x = frames // NX
     per_class = per_x // CLASSES
     part = per_x // NZL
@@ -99,31 +96,26 @@
     ones = jnp.concatenate([one, one, jnp.zeros_like(one)], axis=1)
     line = lax.broadcasted_iota(jnp.int32, (8, frames), 0)
 
-    def from_back2(which):
-        return jnp.where(which == 0, back2a[...], back2b[...])
+    def block(back, which):
+        return jnp.where(which == 0, stay[back][:, begin : begin + width], move[back][...])
 
     for at, slot in enumerate(slots):
         row_block = place[4] ^ slot
+        left = block(0, row_block)
         for xc in range(NX):
             apart = x ^ xc
             chunk = jnp.where(apart == 3, 1, jnp.where(apart == 0, 0, apart + 1))
             for zl in range(NZL):
                 kind = (zl - turn) & (CLASSES - 1)
                 upper = zl // CLASSES
-                ordered[chunk, kind, upper * part : (upper + 1) * part, :] = own[
-                    row_block, xc * per_x + zl * part : xc * per_x + (zl + 1) * part, :
+                ordered[chunk, kind, upper * part : (upper + 1) * part, :] = left[
+                    xc * per_x + zl * part : xc * per_x + (zl + 1) * part, :
                 ]
         high, low = split2(ordered[...].reshape(frames, width))
         rows = jnp.concatenate([jnp.concatenate([high, high, low], axis=1), ones], axis=0)
-        flips = [row_block ^ (y < shift).astype(jnp.int32) for shift in range(SHIFTS)]
-        others = (
-            lambda: own[flips[0]],
-            lambda: back1[flips[1]],
-            lambda: from_back2(flips[2]),
-            lambda: back3[flips[3]],
-            lambda: own[1 - row_block],
-        )
-        sums = jnp.where(line == SHIFTS, 0.5 * count[0:1, 0:1], 0.0)
+        sums = jnp.where(line == SHIFTS, count[0:1, 0:1], 0.0)
+        if has_previous:
+            sums = jnp.zeros_like(sums)
         outer, inner = outs[2 * at], outs[2 * at + 1]
         spots = []
         for side, (kept, given) in enumerate((((0, 1), (2, 3)), ((0, 2), (1, 3)))):
@@ -140,24 +132,28 @@
             where = (*lead, slice(first, first + value.shape[0]))
             to[where] = value + before[0][where] if before else value
 
-        for shift, other in enumerate(others):
-            high, low = split2(other())
+        for shift in range(SHIFTS):
+            if shift < 4:
+                other = block(shift, row_block ^ (y < shift).astype(jnp.int32))
+            else:
+                other = block(0, 1 - row_block)
+            high, low = split2(other)
             tile = dot_nt(rows, jnp.concatenate([high, low, high], axis=1))
             sums = jnp.where(line == shift, tile[frames:], sums)
             for spot in spots:
-                begin = spot[3] * per_x + spot[4] * per_class
-                store(spot, shift * per_class, tile[begin : begin + per_class])
+                first = spot[3] * per_x + spot[4] * per_class
+                store(spot, shift * per_class, tile[first : first + per_class])
         for spot in spots:
             store(spot, SHIFTS * per_class, sums)
 
 
-def gram(slots, place, count, own, back1, back3, back2, previous=()):
-    _, frames, width = own.shape
-    operands = [place, count, own, back1, back3, *back2, *previous]
+def gram(slots, begin, place, count, stay, move, previous=()):
+    frames, width = move[0].shape
+    operands = [place, count, *stay, *move, *previous]
     lines = SHIFTS * frames // NX // CLASSES + 8
     result = jax.ShapeDtypeStruct((2, 2, 2, lines, frames), F32)
     return pl.pallas_call(
-        functools.partial(gram_kernel, slots, bool(previous)),
+        functools.partial(gram_kernel, slots, begin, bool(previous)),
         out_shape=(result,) * (2 * len(slots)),
         in_specs=[SMEM] + [VMEM] * (len(operands) - 1),
         out_specs=(VMEM,) * (2 * len(slots)),
@@ -235,47 +231,35 @@
     frame_at, pix_at = lax.axis_index("frames"), lax.axis_index("pix")
     zh, y = frame_at >> 2, frame_at & 3
     x, zl, core = pix_at >> 4, (pix_at >> 1) & 7, pix_at & 1
-    first_label = ((zl >> 2) ^ zh) ^ 1
-    own_row = first_label ^ core
     place = jnp.stack(
-        [zh, y, x, zl & 3, own_row, zl >> 2, core, zh ^ core, pix_at * ROWS]
+        [zh, y, x, zl & 3, zh ^ core, zl >> 2, core, zh ^ core, pix_at * ROWS]
     ).astype(jnp.int32)
     index, mask = circle_index[None, :], pixel_mask[None, :]
-    quarter = NZ // 4
-
-    def up(value):
-        return send(value, lambda x, y, z, c: (x, (y + 1) % NY, z, c))
-
-    def down(value):
-        return send(value, lambda x, y, z, c: (x, (y - 1) % NY, z, c))
-
-    picked, begin = [], 0
+
+    def after(value, *others):
+        return lax.optimization_barrier((value, *others))[0]
+
+    def around(value, *before):
+        up = send(value, lambda x, y, z, c: (x, (y + 1) % NY, z, c))
+        down = send(value, lambda x, y, z, c: (x, (y - 1) % NY, z, c))
+        late = after(value, *before) if before else value
+        opposite = send(late, lambda x, y, z, c: (x, (y + 2) % NY, z, c))
+        return value, up, opposite, down
+
+    given, _ = select(0, place, intensity, index, mask)
+    moved = send(given, lambda x, y, z, c: (x, y, (z + NZL) % NZ, c))
+    kept, count = select(1, place, intensity, after(index, given), mask)
+    stay = around(kept)
+    partial, begin = (), 0
     for width in WIDTHS:
-        picked.append(select(begin, width, place, intensity, index, mask))
+        move = around(moved[:, begin : begin + width], *partial)
+        if not partial:
+            partial = gram((1, 0), begin, place, count, stay, move)
+        else:
+            give = gram((1,), begin, place, count, stay, move, partial[:2])
+            keep = gram((0,), begin, place, count, stay, move, partial[2:])
+            partial = (*give, *keep)
         begin += width
-    met = []
-    for first, second, _ in picked:
-        if met:
-            first, before = lax.optimization_barrier((first, met[-1][0]))
-            second, also = lax.optimization_barrier((second, met[-1][1]))
-            met[-1] = (before, also)
-        met.append(
-            (
-                send(first, lambda x, y, z, c: (x, y, (z + quarter) % NZ, c)),
-                send(second, lambda x, y, z, c: (x, y, (z - quarter) % NZ, c)),
-            )
-        )
-    partial = ()
-    for (_, _, count), arrived in zip(picked, met):
-        own = jnp.stack(arrived)
-        back1, back3 = up(own), down(own)
-        back2 = (up(back1[0]), down(back3[1]))
-        if not partial:
-            partial = gram((1, 0), place, count, own, back1, back3, back2)
-        else:
-            give = gram((1,), place, count, own, back1, back3, back2, partial[:2])
-            keep = gram((0,), place, count, own, back1, back3, back2, partial[2:])
-            partial = (*give, *keep)
 
     def across(value):
         return send(value, lambda x, y, z, c: (x, y, z, 1 - c))

time: 236 us -> 231 us (0.979)
  waiting for transfers between devices: 114 us -> 76.8 us
  starting transfers between devices: 101 us -> 131 us
    ppermute x25 -> x23, waiting for transfers between devices: 114 us -> 76.8 us  [send(): return lax.ppermute(value, ('frames', 'pix'), pairs)]
    ppermute x25 -> x23, starting transfers between devices: 101 us -> 131 us  [send(): return lax.ppermute(value, ('frames', 'pix'), pairs)]
  transfers between devices with their start and end apart: 25 -> 23, of which waited for: 16 -> 12; matrix products, arithmetic and copies ran while one was open for 0% -> 0% of each run, Pallas kernels for 4% -> 4%
where the time goes in v2:
time: 231 us; the launch traced here: 230 us
  starting transfers between devices  131 us (57%)
  waiting for transfers between devices  76.8 us (33%)
  Pallas kernels  17.3 us (7%)
  local copies, waits for them, and re-layouts  3.39 us (1%)
    ppermute x23, starting transfers between devices, send(): return lax.ppermute(value, ('frames', 'pix'), pairs)  131 us
    ppermute x23, waiting for transfers between devices, send(): return lax.ppermute(value, ('frames', 'pix'), pairs)  76.8 us
    pallas_call x3, Pallas kernels, gram(): pl.pallas_call(functools.partial(gram_kernel, slots, begin, bool(previous...  9.12 us
    pallas_call x2, Pallas kernels, select(): pl.pallas_call(functools.partial(select_kernel, flip), out_shape=(block,...  6.3 us
  transfers between devices with their start and end apart: 23, of which 12 were waited for; matrix products, arithmetic and copies ran while one was open for 0% of the time, Pallas kernels for 4%

profile of v2, /device:TPU:1, one launch (start us, length us, event | category | flops | bytes accessed | tf_op | source)
XLA Modules:
  0.0 230.0 jit_solution(13098250588081435707)
XLA Ops:
  3.1 3.5 %select.2 = (f32[384,512]{1,0:T(8,128)S(1)}, f32[8,128]{1,0:T(8,128)}) custom-call(s32[9]{0:T(128)S(1)} %stack.36.place, f32[384,1536]{1,0:T(8,128)S(1)} %copy-done, s32[1,1024]{1,0:T(1,128)S(1)} %bitcast.39, s32[1,1536]{1,0:T(1,128)S(1)} %broadcast_in_dim.7.mask), custom_call_target="tpu_custom_call" | custom-call | flops 1811939328 | bytes 2359296 | tf_op jit(solution)/shard_map/select/pallas_call | solution.py:73
  6.6 16.3 %collective-permute-start.3 = (f32[384,512]{1,0:T(8,128)S(1)}, f32[384,512]{1,0:T(8,128)S(1)}, u32[]{:S(2)}, u32[]{:S(2)}) collective-permute-start(f32[384,512]{1,0:T(8,128)S(1)} %get-tuple-element.23), channel_id=1, source_target_pairs={{0,256},{1,257},{2,258},{3,259},{4,260},{5,261},{6,262},{7,263},{8... | collective-permute-start | bytes 2359304 | tf_op jit(solution)/shard_map/ppermute | solution.py:35
  22.9 2.8 %select.3 = (f32[384,512]{1,0:T(8,128)S(1)}, f32[8,128]{1,0:T(8,128)S(1)}) custom-call(s32[9]{0:T(128)S(1)} %stack.36.place, f32[384,1536]{1,0:T(8,128)S(1)} %copy-done, s32[1,1024]{1,0:T(1,128)S(1)} %bitcast.40, s32[1,1536]{1,0:T(1,128)S(1)} %broadcast_in_dim.7.mask), custom_call_target="tpu_custom_call" | custom-call | flops 1811939328 | bytes 2359296 | tf_op jit(solution)/shard_map/select/pallas_call | solution.py:73
  25.7 4.6 %collective-permute-start.2 = (f32[384,512]{1,0:T(8,128)S(1)}, f32[384,512]{1,0:T(8,128)S(1)}, u32[]{:S(2)}, u32[]{:S(2)}) collective-permute-start(f32[384,512]{1,0:T(8,128)S(1)} %get-tuple-element.26.refs_0_), channel_id=1, source_target_pairs={{0,192},{1,193},{2,194},{3,195},{4,196},{5,197},{6,198},{7,199},{8... | collective-permute-start | bytes 2359304 | tf_op jit(solution)/shard_map/ppermute | solution.py:35
  30.4 2.3 collective-permute-start.1
  32.6 2.6 %collective-permute-start = (f32[384,512]{1,0:T(8,128)S(1)}, f32[384,512]{1,0:T(8,128)S(1)}, u32[]{:S(2)}, u32[]{:S(2)}) collective-permute-start(f32[384,512]{1,0:T(8,128)S(1)} %get-tuple-element.26.refs_0_), channel_id=1, source_target_pairs={{0,64},{1,65},{2,66},{3,67},{4,68},{5,69},{6,70},{7,71},{8,72},{9,... | collective-permute-start | bytes 2359304 | tf_op jit(solution)/shard_map/ppermute | solution.py:35
  35.2 12.7 %collective-permute-done.3 = f32[384,512]{1,0:T(8,128)S(1)} collective-permute-done((f32[384,512]{1,0:T(8,128)S(1)}, f32[384,512]{1,0:T(8,128)S(1)}, u32[]{:S(2)}, u32[]{:S(2)}) %collective-permute-start.3) | collective-permute-done | bytes 786464 | tf_op jit(solution)/shard_map/ppermute | solution.py:35
  48.0 5.6 %collective-permute-start.7 = (f32[384,256]{1,0:T(8,128)S(1)}, f32[384,256]{1,0:T(8,128)S(1)}, u32[]{:S(2)}, u32[]{:S(2)}) collective-permute-start(f32[384,256]{1,0:T(8,128)S(1)} %get-tuple-element.45.refs_4_), channel_id=1, source_target_pairs={{0,192},{1,193},{2,194},{3,195},{4,196},{5,197},{6,198},{7,199},{8... | collective-permute-start | bytes 1179656 | tf_op jit(solution)/shard_map/ppermute | solution.py:35
  53.6 2.3 collective-permute-start.6
  55.9 2.6 %collective-permute-start.5 = (f32[384,256]{1,0:T(8,128)S(1)}, f32[384,256]{1,0:T(8,128)S(1)}, u32[]{:S(2)}, u32[]{:S(2)}) collective-permute-start(f32[384,256]{1,0:T(8,128)S(1)} %get-tuple-element.45.refs_4_), channel_id=1, source_target_pairs={{0,64},{1,65},{2,66},{3,67},{4,68},{5,69},{6,70},{7,71},{8,72},{9,... | collective-permute-start | bytes 1179656 | tf_op jit(solution)/shard_map/ppermute | solution.py:35
  58.5 8.4 %collective-permute-start.9 = (f32[384,256]{1,0:T(8,128)S(1)}, f32[384,256]{1,0:T(8,128)S(1)}, u32[]{:S(2)}, u32[]{:S(2)}) collective-permute-start(f32[384,256]{1,0:T(8,128)S(1)} %get-tuple-element.31.refs_4_), channel_id=1, source_target_pairs={{0,192},{1,193},{2,194},{3,195},{4,196},{5,197},{6,198},{7,199},{8... | collective-permute-start | bytes 1179656 | tf_op jit(solution)/shard_map/ppermute | solution.py:35
  66.9 4.8 %collective-permute-done.refs_1_ = f32[384,512]{1,0:T(8,128)S(1)} collective-permute-done((f32[384,512]{1,0:T(8,128)S(1)}, f32[384,512]{1,0:T(8,128)S(1)}, u32[]{:S(2)}, u32[]{:S(2)}) %collective-permute-start) | collective-permute-done | bytes 786464 | tf_op jit(solution)/shard_map/ppermute | solution.py:35
  73.6 3.3 %collective-permute-done.6.refs_6_ = f32[384,256]{1,0:T(8,128)S(1)} collective-permute-done((f32[384,256]{1,0:T(8,128)S(1)}, f32[384,256]{1,0:T(8,128)S(1)}, u32[]{:S(2)}, u32[]{:S(2)}) %collective-permute-start.6) | collective-permute-done | bytes 393248 | tf_op jit(solution)/shard_map/ppermute | solution.py:35
  76.9 9.9 %collective-permute-done.5.refs_5_ = f32[384,256]{1,0:T(8,128)S(1)} collective-permute-done((f32[384,256]{1,0:T(8,128)S(1)}, f32[384,256]{1,0:T(8,128)S(1)}, u32[]{:S(2)}, u32[]{:S(2)}) %collective-permute-start.5) | collective-permute-done | bytes 393248 | tf_op jit(solution)/shard_map/ppermute | solution.py:35
  86.8 4.1 %gram.3 = (f32[2,2,2,128,384]{4,3,2,1,0:T(8,128)S(1)}, f32[2,2,2,128,384]{4,3,2,1,0:T(8,128)S(1)}, f32[2,2,2,128,384]{4,3,2,1,0:T(8,128)S(1)}, f32[2,2,2,128,384]{4,3,2,1,0:T(8,128)S(1)}) custom-call(s32[9]{0:T(128)S(1)} %stack.36.place, f32[8,128]{1,0:T(8,128)S(1)} %get-tuple-element.25.count, f32[384,512]{1,0:T(8,128)S(1)} %get-tuple-element.26.refs_0_, ...), custom_call_target="tpu_custom_call" | custom-call | flops 2264924160 | bytes 9043968 | tf_op jit(solution)/shard_map/gram/pallas_call | solution.py:155
  91.0 2.4 %collective-permute-start.8 = (f32[384,256]{1,0:T(8,128)S(1)}, f32[384,256]{1,0:T(8,128)S(1)}, u32[]{:S(2)}, u32[]{:S(2)}) collective-permute-start(f32[384,256]{1,0:T(8,128)S(1)} %get-tuple-element.31.refs_4_), channel_id=1, source_target_pairs={{0,128},{1,129},{2,130},{3,131},{4,132},{5,133},{6,134},{7,135},{8... | collective-permute-start | bytes 1179656 | tf_op jit(solution)/shard_map/ppermute | solution.py:35
  95.3 9.0 %collective-permute-done.8.refs_6_ = f32[384,256]{1,0:T(8,128)S(1)} collective-permute-done((f32[384,256]{1,0:T(8,128)S(1)}, f32[384,256]{1,0:T(8,128)S(1)}, u32[]{:S(2)}, u32[]{:S(2)}) %collective-permute-start.8) | collective-permute-done | bytes 393248 | tf_op jit(solution)/shard_map/ppermute | solution.py:35
  104.2 2.5 %gram.5 = (f32[2,2,2,128,384]{4,3,2,1,0:T(8,128)S(1)}, f32[2,2,2,128,384]{4,3,2,1,0:T(8,128)S(1)}) custom-call(s32[9]{0:T(128)S(1)} %stack.36.place, f32[8,128]{1,0:T(8,128)S(1)} %get-tuple-element.25.count, f32[384,512]{1,0:T(8,128)S(1)} %get-tuple-element.26.refs_0_, f32[384,512]{1,0:T(8,128)S(1)} %collective-permute-done.refs_1_, ...), custom_call_target="tpu_custom_call" | custom-call | flops 1132462080 | bytes 6094848 | tf_op jit(solution)/shard_map/gram/pallas_call | solution.py:155
  106.7 3.6 %collective-permute-start.11 = (f32[2,2,2,128,384]{4,3,2,1,0:T(8,128)S(1)}, f32[2,2,2,128,384]{4,3,2,1,0:T(8,128)S(1)}, u32[]{:S(2)}, u32[]{:S(2)}) collective-permute-start(f32[2,2,2,128,384]{4,3,2,1,0:T(8,128)S(1)} %get-tuple-element.35), channel_id=1, source_target_pairs={{0,1},{1,0},{2,3},{3,2},{4,5},{5,4},{6,7},{7,6},{8,9},{9,8},{10,11... | collective-permute-start | bytes 4718600 | tf_op jit(solution)/shard_map/ppermute | solution.py:35
  112.4 2.5 %gram.4 = (f32[2,2,2,128,384]{4,3,2,1,0:T(8,128)S(1)}, f32[2,2,2,128,384]{4,3,2,1,0:T(8,128)S(1)}) custom-call(s32[9]{0:T(128)S(1)} %stack.36.place, f32[8,128]{1,0:T(8,128)S(1)} %get-tuple-element.25.count, f32[384,512]{1,0:T(8,128)S(1)} %get-tuple-element.26.refs_0_, f32[384,512]{1,0:T(8,128)S(1)} %collective-permute-done.refs_1_, ...), custom_call_target="tpu_custom_call" | custom-call | flops 1132462080 | bytes 6094848 | tf_op jit(solution)/shard_map/gram/pallas_call | solution.py:155
  115.3 4.4 %collective-permute-start.15 = (f32[2,2,128,384]{3,2,1,0:T(8,128)S(1)}, f32[2,2,128,384]{3,2,1,0:T(8,128)S(1)}, u32[]{:S(2)}, u32[]{:S(2)}) collective-permute-start(f32[2,2,128,384]{3,2,1,0:T(8,128)S(1)} %get-tuple-element.43), channel_id=1, source_target_pairs={{0,48},{1,49},{2,50},{3,51},{4,52},{5,53},{6,54},{7,55},{8,56},{9,... | collective-permute-start | bytes 2359304 | tf_op jit(solution)/shard_map/ppermute | solution.py:35
  121.8 15.2 %collective-permute-done.15 = f32[2,2,128,384]{3,2,1,0:T(8,128)S(1)} collective-permute-done((f32[2,2,128,384]{3,2,1,0:T(8,128)S(1)}, f32[2,2,128,384]{3,2,1,0:T(8,128)S(1)}, u32[]{:S(2)}, u32[]{:S(2)}) %collective-permute-start.15) | collective-permute-done | bytes 786464 | tf_op jit(solution)/shard_map/ppermute | solution.py:35
  137.0 2.9 %collective-permute-done.12 = f32[2,2,128,384]{3,2,1,0:T(8,128)S(1)} collective-permute-done((f32[2,2,128,384]{3,2,1,0:T(8,128)S(1)}, f32[2,2,128,384]{3,2,1,0:T(8,128)S(1)}, u32[]{:S(2)}, u32[]{:S(2)}) %collective-permute-start.12) | collective-permute-done | bytes 786464 | tf_op jit(solution)/shard_map/ppermute | solution.py:35
  144.1 8.0 %collective-permute-done.13 = f32[2,128,384]{2,1,0:T(8,128)S(1)} collective-permute-done((f32[2,128,384]{2,1,0:T(8,128)S(1)}, f32[2,128,384]{2,1,0:T(8,128)S(1)}, u32[]{:S(2)}, u32[]{:S(2)}) %collective-permute-start.13) | collective-permute-done | bytes 393248 | tf_op jit(solution)/shard_map/ppermute | solution.py:35
  152.2 34.4 %collective-permute-start.14 = (f32[128,384]{1,0:T(8,128)S(1)}, f32[128,384]{1,0:T(8,128)S(1)}, u32[]{:S(2)}, u32[]{:S(2)}) collective-permute-start(f32[128,384]{1,0:T(8,128)S(1)} %slice_bitcast_fusion.10), channel_id=1, source_target_pairs={{0,2},{1,3},{2,4},{3,5},{4,6},{5,7},{6,8},{7,9},{8,10},{9,11},{10,... | collective-permute-start | bytes 589832 | tf_op jit(solution)/shard_map/ppermute | solution.py:35
  186.6 6.9 %collective-permute-start.18 = (f32[128,384]{1,0:T(8,128)S(1)}, f32[128,384]{1,0:T(8,128)S(1)}, u32[]{:S(2)}, u32[]{:S(2)}) collective-permute-start(f32[128,384]{1,0:T(8,128)S(1)} %get-tuple-element.47), channel_id=1, source_target_pairs={{0,4},{1,269},{2,6},{3,271},{4,8},{5,1},{6,10},{7,3},{8,12},{9,5},... | collective-permute-start | bytes 589832 | tf_op jit(solution)/shard_map/ppermute | solution.py:35
  193.6 3.4 %collective-permute-start.17 = (f32[128,384]{1,0:T(8,128)S(1)}, f32[128,384]{1,0:T(8,128)S(1)}, u32[]{:S(2)}, u32[]{:S(2)}) collective-permute-start(f32[128,384]{1,0:T(8,128)S(1)} %get-tuple-element.48), channel_id=1, source_target_pairs={{0,270},{1,271},{2,0},{3,1},{4,2},{5,3},{6,4},{7,5},{8,6},{9,7},{1... | collective-permute-start | bytes 589832 | tf_op jit(solution)/shard_map/ppermute | solution.py:35
  197.0 3.9 %collective-permute-done.17.down = f32[128,384]{1,0:T(8,128)S(1)} collective-permute-done((f32[128,384]{1,0:T(8,128)S(1)}, f32[128,384]{1,0:T(8,128)S(1)}, u32[]{:S(2)}, u32[]{:S(2)}) %collective-permute-start.17) | collective-permute-done | bytes 196640 | tf_op jit(solution)/shard_map/ppermute | solution.py:35
  201.5 8.7 %collective-permute-start.19 = (f32[40,384]{1,0:T(8,128)S(1)}, f32[40,384]{1,0:T(8,128)S(1)}, u32[]{:S(2)}, u32[]{:S(2)}) collective-permute-start(f32[40,384]{1,0:T(8,128)S(1)} %get-tuple-element.37), channel_id=1, source_target_pairs={{0,1},{1,257},{2,3},{3,259},{4,5},{5,261},{6,7},{7,263},{8,9},{9,2... | collective-permute-start | bytes 184328 | tf_op jit(solution)/shard_map/ppermute | solution.py:35
  212.2 5.6 %collective-permute-start.21 = (f32[40,384]{1,0:T(8,128)S(1)}, f32[40,384]{1,0:T(8,128)S(1)}, u32[]{:S(2)}, u32[]{:S(2)}) collective-permute-start(f32[40,384]{1,0:T(8,128)S(1)} %get-tuple-element.39), channel_id=1, source_target_pairs={{0,8},{1,256},{2,10},{3,258},{4,12},{5,260},{6,14},{7,262},{8,0},{... | collective-permute-start | bytes 184328 | tf_op jit(solution)/shard_map/ppermute | solution.py:35
  217.8 5.6 %collective-permute-start.22 = (f32[40,384]{1,0:T(8,128)S(1)}, f32[40,384]{1,0:T(8,128)S(1)}, u32[]{:S(2)}, u32[]{:S(2)}) collective-permute-start(f32[40,384]{1,0:T(8,128)S(1)} %get-tuple-element.40), channel_id=1, source_target_pairs={{1,264},{3,266},{5,268},{7,270},{9,256},{11,258},{13,260},{15,262}... | collective-permute-start | bytes 184328 | tf_op jit(solution)/shard_map/ppermute | solution.py:35
  223.5 3.0 %collective-permute-done.21.third = f32[40,384]{1,0:T(8,128)S(1)} collective-permute-done((f32[40,384]{1,0:T(8,128)S(1)}, f32[40,384]{1,0:T(8,128)S(1)}, u32[]{:S(2)}, u32[]{:S(2)}) %collective-permute-start.21) | collective-permute-done | bytes 61472 | tf_op jit(solution)/shard_map/ppermute | solution.py:35
  (38 shorter events, 21.9 us)
Async XLA Ops:
  0.8 1.7 copy-start
  2.5 0.7 copy-start.1
  6.6 41.4 %collective-permute-start.3 = (f32[384,512]{1,0:T(8,128)S(1)}, f32[384,512]{1,0:T(8,128)S(1)}, u32[]{:S(2)}, u32[]{:S(2)}) collective-permute-start(f32[384,512]{1,0:T(8,128)S(1)} %get-tuple-element.23), channel_id=1, source_target_pairs={{0,256},{1,257},{2,258},{3,259},{4,260},{5,261},{6,262},{7,263},{8... | collective-permute-start | bytes 2359304 | tf_op jit(solution)/shard_map/ppermute | solution.py:35
  25.7 30.2 %collective-permute-start.2 = (f32[384,512]{1,0:T(8,128)S(1)}, f32[384,512]{1,0:T(8,128)S(1)}, u32[]{:S(2)}, u32[]{:S(2)}) collective-permute-start(f32[384,512]{1,0:T(8,128)S(1)} %get-tuple-element.26.refs_0_), channel_id=1, source_target_pairs={{0,192},{1,193},{2,194},{3,195},{4,196},{5,197},{6,198},{7,199},{8... | collective-permute-start | bytes 2359304 | tf_op jit(solution)/shard_map/ppermute | solution.py:35
  30.4 28.1 %collective-permute-start.1 = (f32[384,512]{1,0:T(8,128)S(1)}, f32[384,512]{1,0:T(8,128)S(1)}, u32[]{:S(2)}, u32[]{:S(2)}) collective-permute-start(f32[384,512]{1,0:T(8,128)S(1)} %get-tuple-element.26.refs_0_), channel_id=1, source_target_pairs={{0,128},{1,129},{2,130},{3,131},{4,132},{5,133},{6,134},{7,135},{8... | collective-permute-start | bytes 2359304 | tf_op jit(solution)/shard_map/ppermute | solution.py:35
  32.6 39.1 %collective-permute-start = (f32[384,512]{1,0:T(8,128)S(1)}, f32[384,512]{1,0:T(8,128)S(1)}, u32[]{:S(2)}, u32[]{:S(2)}) collective-permute-start(f32[384,512]{1,0:T(8,128)S(1)} %get-tuple-element.26.refs_0_), channel_id=1, source_target_pairs={{0,64},{1,65},{2,66},{3,67},{4,68},{5,69},{6,70},{7,71},{8,72},{9,... | collective-permute-start | bytes 2359304 | tf_op jit(solution)/shard_map/ppermute | solution.py:35
  48.0 25.6 %collective-permute-start.7 = (f32[384,256]{1,0:T(8,128)S(1)}, f32[384,256]{1,0:T(8,128)S(1)}, u32[]{:S(2)}, u32[]{:S(2)}) collective-permute-start(f32[384,256]{1,0:T(8,128)S(1)} %get-tuple-element.45.refs_4_), channel_id=1, source_target_pairs={{0,192},{1,193},{2,194},{3,195},{4,196},{5,197},{6,198},{7,199},{8... | collective-permute-start | bytes 1179656 | tf_op jit(solution)/shard_map/ppermute | solution.py:35
  53.6 23.3 %collective-permute-start.6 = (f32[384,256]{1,0:T(8,128)S(1)}, f32[384,256]{1,0:T(8,128)S(1)}, u32[]{:S(2)}, u32[]{:S(2)}) collective-permute-start(f32[384,256]{1,0:T(8,128)S(1)} %get-tuple-element.45.refs_4_), channel_id=1, source_target_pairs={{0,128},{1,129},{2,130},{3,131},{4,132},{5,133},{6,134},{7,135},{8... | collective-permute-start | bytes 1179656 | tf_op jit(solution)/shard_map/ppermute | solution.py:35
  55.9 30.9 %collective-permute-start.5 = (f32[384,256]{1,0:T(8,128)S(1)}, f32[384,256]{1,0:T(8,128)S(1)}, u32[]{:S(2)}, u32[]{:S(2)}) collective-permute-start(f32[384,256]{1,0:T(8,128)S(1)} %get-tuple-element.45.refs_4_), channel_id=1, source_target_pairs={{0,64},{1,65},{2,66},{3,67},{4,68},{5,69},{6,70},{7,71},{8,72},{9,... | collective-permute-start | bytes 1179656 | tf_op jit(solution)/shard_map/ppermute | solution.py:35
  58.5 34.9 %collective-permute-start.9 = (f32[384,256]{1,0:T(8,128)S(1)}, f32[384,256]{1,0:T(8,128)S(1)}, u32[]{:S(2)}, u32[]{:S(2)}) collective-permute-start(f32[384,256]{1,0:T(8,128)S(1)} %get-tuple-element.31.refs_4_), channel_id=1, source_target_pairs={{0,192},{1,193},{2,194},{3,195},{4,196},{5,197},{6,198},{7,199},{8... | collective-permute-start | bytes 1179656 | tf_op jit(solution)/shard_map/ppermute | solution.py:35
  71.7 23.6 %collective-permute-start.4 = (f32[384,256]{1,0:T(8,128)S(1)}, f32[384,256]{1,0:T(8,128)S(1)}, u32[]{:S(2)}, u32[]{:S(2)}) collective-permute-start(f32[384,256]{1,0:T(8,128)S(1)} %get-tuple-element.31.refs_4_), channel_id=1, source_target_pairs={{0,64},{1,65},{2,66},{3,67},{4,68},{5,69},{6,70},{7,71},{8,72},{9,... | collective-permute-start | bytes 1179656 | tf_op jit(solution)/shard_map/ppermute | solution.py:35
  91.0 13.2 %collective-permute-start.8 = (f32[384,256]{1,0:T(8,128)S(1)}, f32[384,256]{1,0:T(8,128)S(1)}, u32[]{:S(2)}, u32[]{:S(2)}) collective-permute-start(f32[384,256]{1,0:T(8,128)S(1)} %get-tuple-element.31.refs_4_), channel_id=1, source_target_pairs={{0,128},{1,129},{2,130},{3,131},{4,132},{5,133},{6,134},{7,135},{8... | collective-permute-start | bytes 1179656 | tf_op jit(solution)/shard_map/ppermute | solution.py:35
  106.7 8.2 %collective-permute-start.11 = (f32[2,2,2,128,384]{4,3,2,1,0:T(8,128)S(1)}, f32[2,2,2,128,384]{4,3,2,1,0:T(8,128)S(1)}, u32[]{:S(2)}, u32[]{:S(2)}) collective-permute-start(f32[2,2,2,128,384]{4,3,2,1,0:T(8,128)S(1)} %get-tuple-element.35), channel_id=1, source_target_pairs={{0,1},{1,0},{2,3},{3,2},{4,5},{5,4},{6,7},{7,6},{8,9},{9,8},{10,11... | collective-permute-start | bytes 4718600 | tf_op jit(solution)/shard_map/ppermute | solution.py:35
  110.3 11.3 %collective-permute-start.10 = (f32[2,2,2,128,384]{4,3,2,1,0:T(8,128)S(1)}, f32[2,2,2,128,384]{4,3,2,1,0:T(8,128)S(1)}, u32[]{:S(2)}, u32[]{:S(2)}) collective-permute-start(f32[2,2,2,128,384]{4,3,2,1,0:T(8,128)S(1)} %get-tuple-element.33), channel_id=1, source_target_pairs={{0,1},{1,0},{2,3},{3,2},{4,5},{5,4},{6,7},{7,6},{8,9},{9,8},{10,11... | collective-permute-start | bytes 4718600 | tf_op jit(solution)/shard_map/ppermute | solution.py:35
  115.3 21.7 %collective-permute-start.15 = (f32[2,2,128,384]{3,2,1,0:T(8,128)S(1)}, f32[2,2,128,384]{3,2,1,0:T(8,128)S(1)}, u32[]{:S(2)}, u32[]{:S(2)}) collective-permute-start(f32[2,2,128,384]{3,2,1,0:T(8,128)S(1)} %get-tuple-element.43), channel_id=1, source_target_pairs={{0,48},{1,49},{2,50},{3,51},{4,52},{5,53},{6,54},{7,55},{8,56},{9,... | collective-permute-start | bytes 2359304 | tf_op jit(solution)/shard_map/ppermute | solution.py:35
  119.7 20.2 %collective-permute-start.12 = (f32[2,2,128,384]{3,2,1,0:T(8,128)S(1)}, f32[2,2,128,384]{3,2,1,0:T(8,128)S(1)}, u32[]{:S(2)}, u32[]{:S(2)}) collective-permute-start(f32[2,2,128,384]{3,2,1,0:T(8,128)S(1)} %get-tuple-element.44), channel_id=1, source_target_pairs={{0,16},{1,17},{2,18},{3,19},{4,20},{5,21},{6,22},{7,23},{8,24},{9,... | collective-permute-start | bytes 2359304 | tf_op jit(solution)/shard_map/ppermute | solution.py:35
  140.0 12.0 %collective-permute-start.13 = (f32[2,128,384]{2,1,0:T(8,128)S(1)}, f32[2,128,384]{2,1,0:T(8,128)S(1)}, u32[]{:S(2)}, u32[]{:S(2)}) collective-permute-start(f32[2,128,384]{2,1,0:T(8,128)S(1)} %slice_bitcast_fusion.6), channel_id=1, source_target_pairs={{0,48},{1,49},{2,50},{3,51},{4,52},{5,53},{6,54},{7,55},{8,56},{9,... | collective-permute-start | bytes 1179656 | tf_op jit(solution)/shard_map/ppermute | solution.py:35
  142.2 44.3 %collective-permute-start.16 = (f32[2,128,384]{2,1,0:T(8,128)S(1)}, f32[2,128,384]{2,1,0:T(8,128)S(1)}, u32[]{:S(2)}, u32[]{:S(2)}) collective-permute-start(f32[2,128,384]{2,1,0:T(8,128)S(1)} %slice_bitcast_fusion.4), channel_id=1, source_target_pairs={{0,16},{1,17},{2,18},{3,19},{4,20},{5,21},{6,22},{7,23},{8,24},{9,... | collective-permute-start | bytes 1179656 | tf_op jit(solution)/shard_map/ppermute | solution.py:35
  152.2 44.8 %collective-permute-start.14 = (f32[128,384]{1,0:T(8,128)S(1)}, f32[128,384]{1,0:T(8,128)S(1)}, u32[]{:S(2)}, u32[]{:S(2)}) collective-permute-start(f32[128,384]{1,0:T(8,128)S(1)} %slice_bitcast_fusion.10), channel_id=1, source_target_pairs={{0,2},{1,3},{2,4},{3,5},{4,6},{5,7},{6,8},{7,9},{8,10},{9,11},{10,... | collective-permute-start | bytes 589832 | tf_op jit(solution)/shard_map/ppermute | solution.py:35
  186.6 10.3 %collective-permute-start.18 = (f32[128,384]{1,0:T(8,128)S(1)}, f32[128,384]{1,0:T(8,128)S(1)}, u32[]{:S(2)}, u32[]{:S(2)}) collective-permute-start(f32[128,384]{1,0:T(8,128)S(1)} %get-tuple-element.47), channel_id=1, source_target_pairs={{0,4},{1,269},{2,6},{3,271},{4,8},{5,1},{6,10},{7,3},{8,12},{9,5},... | collective-permute-start | bytes 589832 | tf_op jit(solution)/shard_map/ppermute | solution.py:35
  193.6 7.3 %collective-permute-start.17 = (f32[128,384]{1,0:T(8,128)S(1)}, f32[128,384]{1,0:T(8,128)S(1)}, u32[]{:S(2)}, u32[]{:S(2)}) collective-permute-start(f32[128,384]{1,0:T(8,128)S(1)} %get-tuple-element.48), channel_id=1, source_target_pairs={{0,270},{1,271},{2,0},{3,1},{4,2},{5,3},{6,4},{7,5},{8,6},{9,7},{1... | collective-permute-start | bytes 589832 | tf_op jit(solution)/shard_map/ppermute | solution.py:35
  201.5 21.9 %collective-permute-start.19 = (f32[40,384]{1,0:T(8,128)S(1)}, f32[40,384]{1,0:T(8,128)S(1)}, u32[]{:S(2)}, u32[]{:S(2)}) collective-permute-start(f32[40,384]{1,0:T(8,128)S(1)} %get-tuple-element.37), channel_id=1, source_target_pairs={{0,1},{1,257},{2,3},{3,259},{4,5},{5,261},{6,7},{7,263},{8,9},{9,2... | collective-permute-start | bytes 184328 | tf_op jit(solution)/shard_map/ppermute | solution.py:35
  210.3 13.2 %collective-permute-start.20 = (f32[40,384]{1,0:T(8,128)S(1)}, f32[40,384]{1,0:T(8,128)S(1)}, u32[]{:S(2)}, u32[]{:S(2)}) collective-permute-start(f32[40,384]{1,0:T(8,128)S(1)} %get-tuple-element.38), channel_id=1, source_target_pairs={{0,9},{1,265},{2,11},{3,267},{4,13},{5,269},{6,15},{7,271},{8,1},{... | collective-permute-start | bytes 184328 | tf_op jit(solution)/shard_map/ppermute | solution.py:35
  212.2 14.3 %collective-permute-start.21 = (f32[40,384]{1,0:T(8,128)S(1)}, f32[40,384]{1,0:T(8,128)S(1)}, u32[]{:S(2)}, u32[]{:S(2)}) collective-permute-start(f32[40,384]{1,0:T(8,128)S(1)} %get-tuple-element.39), channel_id=1, source_target_pairs={{0,8},{1,256},{2,10},{3,258},{4,12},{5,260},{6,14},{7,262},{8,0},{... | collective-permute-start | bytes 184328 | tf_op jit(solution)/shard_map/ppermute | solution.py:35
  217.8 10.9 %collective-permute-start.22 = (f32[40,384]{1,0:T(8,128)S(1)}, f32[40,384]{1,0:T(8,128)S(1)}, u32[]{:S(2)}, u32[]{:S(2)}) collective-permute-start(f32[40,384]{1,0:T(8,128)S(1)} %get-tuple-element.40), channel_id=1, source_target_pairs={{1,264},{3,266},{5,268},{7,270},{9,256},{11,258},{13,260},{15,262}... | collective-permute-start | bytes 184328 | tf_op jit(solution)/shard_map/ppermute | solution.py:35

commit v3 on v0

v3 whole, which is shorter than its diff:
```python
import functools

import jax
import jax.numpy as jnp
from jax import lax
from jax.experimental import pallas as pl
from jax.experimental.pallas import tpu as pltpu
from jax.sharding import PartitionSpec as P

AXES = {"zh": 2, "y": 4, "x": 4, "l2": 2, "r": 4, "core": 2}
FRAMES, PIX = ("zh", "y"), ("x", "l2", "r", "core")
SHIFTS = 5
ROWS = 6
WIDTHS = (256, 256)
VMEM = pl.BlockSpec(memory_space=pltpu.VMEM)
SMEM = pl.BlockSpec(memory_space=pltpu.SMEM)
PARAMS = pltpu.CompilerParams(vmem_limit_bytes=24 * 1024 * 1024)
F32 = jnp.float32


def pass_on(value, axis, by):
    length = lax.axis_size(axis)
    return lax.ppermute(value, axis, [(i, (i + by) % length) for i in range(length)])


def split2(value):
    high = value.astype(jnp.bfloat16)
    return high, (value - high.astype(F32)).astype(jnp.bfloat16)


def split3(value):
    high = value.astype(jnp.bfloat16)
    return (high, *split2(value - high.astype(F32)))


def dot_nn(left, right):
    return jnp.dot(left, right, preferred_element_type=F32)


def dot_nt(left, right):
    return lax.dot_general(left, right, (((1,), (1,)), ((), ())), preferred_element_type=F32)


def select_kernel(flip, place, image, index, mask, out, count):
    band = image.shape[1]
    half = index.shape[1] // 2
    begin = pl.multiple_of((place[0] ^ flip) * half, half)
    columns = lax.broadcasted_iota(jnp.int32, (band, half), 0)
    hot = (columns == index[:, pl.ds(begin, half)]).astype(F32).astype(jnp.bfloat16)
    good = mask[...].astype(F32)
    picked = sum(dot_nn(part, hot) for part in reversed(split3(image[...] * good)))
    out[...] = picked
    goods = dot_nn(jnp.broadcast_to(good, (8, band)).astype(jnp.bfloat16), hot)
    count[...] = jnp.broadcast_to(jnp.sum(goods, axis=1, keepdims=True), (8, 128))


def select(flip, place, image, index, mask):
    frames, band = image.shape
    half = index.shape[1] // 2
    block = jax.ShapeDtypeStruct((frames, half), F32)
    return pl.pallas_call(
        functools.partial(select_kernel, flip),
        out_shape=(block, jax.ShapeDtypeStruct((8, 128), F32)),
        in_specs=[SMEM, VMEM, VMEM, VMEM],
        out_specs=(VMEM, VMEM),
        compiler_params=PARAMS,
        cost_estimate=pl.CostEstimate(
            flops=2 * frames * band * half * 3, bytes_accessed=frames * band * 4, transcendentals=0
        ),
        name="select",
    )(place, image, index, mask)


def gram_kernel(slots, begin, has_previous, place, count, *refs):
    stay, move = refs[0:4], refs[4:8]
    previous = refs[8 : 8 + len(slots)] if has_previous else ()
    outs, ordered = refs[8 + len(previous) : -1], refs[-1]
    zh, y, core = place[0], place[1], place[2]
    frames, width = move[0].shape
    owners = AXES["x"] * AXES["r"]
    mine = 2 * ROWS
    one = jnp.ones((8, width), jnp.bfloat16)
    ones = jnp.concatenate([one, one, jnp.zeros_like(one)], axis=1)
    line = lax.broadcasted_iota(jnp.int32, (16, frames), 0)

    def block(back, label):
        return jnp.where(label == zh, stay[back][:, begin : begin + width], move[back][...])

    for at, slot in enumerate(slots):
        first = (core ^ slot) == 0
        rows = []
        for label in range(2):
            left = block(0, label)
            for x in range(AXES["x"]):
                for r in range(AXES["r"]):
                    for l2 in range(2):
                        source = x * (frames // AXES["x"]) + (l2 * AXES["r"] + r) * mine
                        to = (x * AXES["r"] + r) * mine + l2 * ROWS
                        ordered[to : to + ROWS, :] = jnp.where(
                            first, left[source : source + ROWS], left[source + ROWS : source + mine]
                        )
            high, low = split2(ordered[...])
            rows.append(jnp.concatenate([high, high, low], axis=1))
        sums = jnp.zeros((16, frames), F32)
        if not has_previous:
            sums = jnp.where((line & 7) == SHIFTS, count[0:1, 0:1], sums)
        size = owners * mine
        for shift in range(SHIFTS):
            tiles = []
            for label in range(2):
                if shift < 4:
                    other = block(shift, label ^ (y < shift).astype(jnp.int32))
                else:
                    other = block(0, 1 - label)
                high, low = split2(other)
                tile = dot_nt(
                    jnp.concatenate([rows[label], ones], axis=0),
                    jnp.concatenate([high, low, high], axis=1),
                )
                sums = jnp.where(line == label * 8 + shift, tile[size : size + 1], sums)
                tiles.append(tile)
            for owner in range(owners):
                where = (owner // AXES["r"], owner % AXES["r"], slice(shift * 24, shift * 24 + 24))
                piece = jnp.concatenate(
                    [tile[owner * mine : (owner + 1) * mine] for tile in tiles], axis=0
                )
                outs[at][where] = piece + previous[at][where] if has_previous else piece
        for owner in range(owners):
            where = (owner // AXES["r"], owner % AXES["r"], slice(120, 136))
            outs[at][where] = sums + previous[at][where] if has_previous else sums


def gram(slots, begin, place, count, stay, move, previous=()):
    frames, width = move[0].shape
    operands = [place, count, *stay, *move, *previous]
    result = jax.ShapeDtypeStruct((AXES["x"], AXES["r"], 136, frames), F32)
    return pl.pallas_call(
        functools.partial(gram_kernel, slots, begin, bool(previous)),
        out_shape=(result,) * len(slots),
        in_specs=[SMEM] + [VMEM] * (len(operands) - 1),
        out_specs=(VMEM,) * len(slots),
        scratch_shapes=[pltpu.VMEM((frames // 2, width), F32)],
        compiler_params=PARAMS,
        cost_estimate=pl.CostEstimate(
            flops=len(slots) * 5 * 2 * frames * frames * width * 3,
            bytes_accessed=8 * frames * width * 4 + len(slots) * 5 * frames * frames * 4,
            transcendentals=0,
        ),
        name="gram",
    )(*operands)


def share_kernel(parts, out):
    total = (parts[0] + parts[1]) + (parts[2] + parts[3])
    for zh in range(2):
        for l2 in range(2):
            to = zh * 2 + l2
            for shift in range(SHIFTS):
                begin = shift * 24 + zh * 12 + l2 * ROWS
                out[to, shift * ROWS : (shift + 1) * ROWS] = total[begin : begin + ROWS]
            out[to, 30:32] = jnp.zeros((2, total.shape[1]), F32)
            out[to, 32:40] = total[120 + zh * 8 : 128 + zh * 8]


def share(parts):
    return pl.pallas_call(
        share_kernel,
        out_shape=jax.ShapeDtypeStruct((4, 40, parts.shape[-1]), F32),
        in_specs=[VMEM],
        out_specs=VMEM,
        compiler_params=PARAMS,
        name="share",
    )(parts)


def finish_kernel(place, parts, out):
    total = (parts[0] + parts[1]) + (parts[2] + parts[3])
    frames = total.shape[1]
    sums = total[32 : 32 + SHIFTS]
    good = total[32 + SHIFTS : 33 + SHIFTS]
    line = lax.broadcasted_iota(jnp.int32, (ROWS, frames), 0)
    lane = lax.broadcasted_iota(jnp.int32, (ROWS, frames), 1)
    mine = jnp.where(lane == line + place[3], sums[0:1], 0.0)
    own = jnp.sum(mine, axis=1, keepdims=True)
    for shift in range(SHIFTS):
        tile = total[shift * ROWS : (shift + 1) * ROWS]
        out[shift] = tile * good / (own * sums[shift : shift + 1])


def finish(place, parts):
    return pl.pallas_call(
        finish_kernel,
        out_shape=jax.ShapeDtypeStruct((SHIFTS, ROWS, parts.shape[-1]), F32),
        in_specs=[SMEM, VMEM],
        out_specs=VMEM,
        compiler_params=PARAMS,
        name="finish",
    )(place, parts)


def body(intensity, circle_index, pixel_mask):
    place = jnp.stack(
        [
            lax.axis_index("zh"),
            lax.axis_index("y"),
            lax.axis_index("core"),
            lax.axis_index(PIX) * ROWS,
        ]
    ).astype(jnp.int32)
    index, mask = circle_index[None, :], pixel_mask[None, :]

    def after(value, *others):
        return lax.optimization_barrier((value, *others))[0]

    def around(value):
        return value, pass_on(value, "y", 1), pass_on(value, "y", 2), pass_on(value, "y", -1)

    given, _ = select(0, place, intensity, index, mask)
    moved = pass_on(given, "zh", 1)
    kept, count = select(1, place, intensity, after(index, given), mask)
    stay = around(kept)
    partial, begin = (), 0
    for width in WIDTHS:
        move = around(moved[:, begin : begin + width])
        if not partial:
            partial = gram((1, 0), begin, place, count, stay, move)
        else:
            give = gram((1,), begin, place, count, stay, move, partial[:1])
            keep = gram((0,), begin, place, count, stay, move, partial[1:])
            partial = (*give, *keep)
        begin += width

    def exchange(parts, axis):
        return lax.all_to_all(parts, axis, 0, 0, tiled=True)

    give, keep = partial
    total = keep + pass_on(give, "core", 1)
    total = jnp.sum(exchange(total, "x"), axis=0)
    pieces = share(exchange(total, "r"))
    return finish(place, exchange(pieces, ("zh", "l2")))


def solution(mesh):
    split = jax.sharding.Mesh(mesh.devices.reshape(tuple(AXES.values())), tuple(AXES))
    return jax.shard_map(
        body,
        mesh=split,
        in_specs=(P(FRAMES, PIX), P(PIX), P(PIX)),
        out_specs=P(None, (*FRAMES, *PIX), None),
        check_vma=False,
    )
```

time: 1450 us -> 245 us (0.17)
  waiting for transfers between devices: 1060 us -> 40.9 us
  blocking collectives: 305 us -> 123 us
  starting transfers between devices: 17.6 us -> 53.4 us
  matrix products: 21.1 us -> 0 us
  Pallas kernels: 0 us -> 18.2 us
    unnamed x2 -> x0, waiting for transfers between devices: 575 us -> none
    ppermute x8 -> x11, waiting for transfers between devices: 486 us -> 40.9 us  [pass_on(): lax.ppermute(value, axis, [(i, (i + by) % length) for i in range(length)])]
    psum x1 -> x0, blocking collectives: 305 us -> none  [body(): frame_sums, good_count = lax.psum((partial_sums, jnp.sum(weights)), 'pix')]
    all_to_all x0 -> x3, blocking collectives: none -> 123 us  [exchange(): return lax.all_to_all(parts, axis, 0, 0, tiled=True)]
    ppermute x8 -> x11, starting transfers between devices: 17.6 us -> 53.4 us  [pass_on(): lax.ppermute(value, axis, [(i, (i + by) % length) for i in range(length)])]
    dot_general x6 -> x0, matrix products: 21.1 us -> none  [the longest x5 20 us: cross_rows(): lax.dot_general(left, right, (((1,), (1,)), ((), ())), precision=lax.Prec...]
    pallas_call x0 -> x7, Pallas kernels: none -> 18.2 us  [the longest x3 10.6 us: gram(): pl.pallas_call(functools.partial(gram_kernel, slots, begin, bool(previous...]
  transfers between devices with their start and end apart: 9 -> 11, of which waited for: 8 -> 6; matrix products, arithmetic and copies ran while one was open for 2% -> 0% of each run, Pallas kernels for 0% -> 4%
where the time goes in v3:
time: 245 us; the launch traced here: 240 us
  blocking collectives  123 us (50%)
  starting transfers between devices  53.4 us (22%)
  waiting for transfers between devices  40.9 us (17%)
  Pallas kernels  18.2 us (7%)
  local copies, waits for them, and re-layouts  3.11 us (1%)
    all_to_all x3, blocking collectives, exchange(): return lax.all_to_all(parts, axis, 0, 0, tiled=True)  123 us
    ppermute x11, starting transfers between devices, pass_on(): lax.ppermute(value, axis, [(i, (i + by) % length) for i in range(length)])  53.4 us
    ppermute x11, waiting for transfers between devices, pass_on(): lax.ppermute(value, axis, [(i, (i + by) % length) for i in range(length)])  40.9 us
    pallas_call x3, Pallas kernels, gram(): pl.pallas_call(functools.partial(gram_kernel, slots, begin, bool(previous...  10.6 us
    pallas_call x2, Pallas kernels, select(): pl.pallas_call(functools.partial(select_kernel, flip), out_shape=(block,...  6.31 us
  transfers between devices with their start and end apart: 11, of which 6 were waited for; matrix products, arithmetic and copies ran while one was open for 0% of the time, Pallas kernels for 4%

profile of v3, /device:TPU:1, one launch (start us, length us, event | category | flops | bytes accessed | tf_op | source)
XLA Modules:
  0.0 240.2 jit_solution(15520891209886651795)
XLA Ops:
  0.0 0.7 broadcast_in_dim.7.mask
  0.7 0.1 pad_add_fusion.place
  0.8 1.7 copy-done
  2.4 0.7 copy-done.1
  3.1 3.5 %select.2 = (f32[384,512]{1,0:T(8,128)S(1)}, f32[8,128]{1,0:T(8,128)}) custom-call(s32[4]{0:T(128)S(1)} %pad_add_fusion.place, f32[384,1536]{1,0:T(8,128)S(1)} %copy-done, s32[1,1024]{1,0:T(1,128)S(1)} %bitcast.5, s32[1,1536]{1,0:T(1,128)S(1)} %broadcast_in_dim.7.mask), custom_call_target="tpu_custom_call" | custom-call | flops 1811939328 | bytes 2359296 | tf_op jit(solution)/shard_map/select/pallas_call | solution.py:61
  6.6 16.3 %collective-permute-start.3 = (f32[384,512]{1,0:T(8,128)S(1)}, f32[384,512]{1,0:T(8,128)S(1)}, u32[]{:S(2)}, u32[]{:S(2)}) collective-permute-start(f32[384,512]{1,0:T(8,128)S(1)} %get-tuple-element.11), channel_id=1, source_target_pairs={{0,256},{256,0},{1,257},{257,1},{2,258},{258,2},{3,259},{259,3},{4... | collective-permute-start | bytes 2359304 | tf_op jit(solution)/shard_map/ppermute | solution.py:23
  22.9 2.8 %select.3 = (f32[384,512]{1,0:T(8,128)S(1)}, f32[8,128]{1,0:T(8,128)S(1)}) custom-call(s32[4]{0:T(128)S(1)} %pad_add_fusion.place, f32[384,1536]{1,0:T(8,128)S(1)} %copy-done, s32[1,1024]{1,0:T(1,128)S(1)} %bitcast.6, s32[1,1536]{1,0:T(1,128)S(1)} %broadcast_in_dim.7.mask), custom_call_target="tpu_custom_call" | custom-call | flops 1811939328 | bytes 2359296 | tf_op jit(solution)/shard_map/select/pallas_call | solution.py:61
  25.7 4.6 %collective-permute-start.2 = (f32[384,512]{1,0:T(8,128)S(1)}, f32[384,512]{1,0:T(8,128)S(1)}, u32[]{:S(2)}, u32[]{:S(2)}) collective-permute-start(f32[384,512]{1,0:T(8,128)S(1)} %get-tuple-element.14.refs_0_), channel_id=1, source_target_pairs={{0,192},{64,0},{128,64},{192,128},{1,193},{65,1},{129,65},{193,129... | collective-permute-start | bytes 2359304 | tf_op jit(solution)/shard_map/ppermute | solution.py:23
  30.4 2.3 collective-permute-start.1
  32.6 2.6 %collective-permute-start = (f32[384,512]{1,0:T(8,128)S(1)}, f32[384,512]{1,0:T(8,128)S(1)}, u32[]{:S(2)}, u32[]{:S(2)}) collective-permute-start(f32[384,512]{1,0:T(8,128)S(1)} %get-tuple-element.14.refs_0_), channel_id=1, source_target_pairs={{0,64},{64,128},{128,192},{192,0},{1,65},{65,129},{129,193},{193,1... | collective-permute-start | bytes 2359304 | tf_op jit(solution)/shard_map/ppermute | solution.py:23
  35.2 12.7 %collective-permute-done.3 = f32[384,512]{1,0:T(8,128)S(1)} collective-permute-done((f32[384,512]{1,0:T(8,128)S(1)}, f32[384,512]{1,0:T(8,128)S(1)}, u32[]{:S(2)}, u32[]{:S(2)}) %collective-permute-start.3) | collective-permute-done | bytes 786464 | tf_op jit(solution)/shard_map/ppermute | solution.py:23
  48.0 5.6 %collective-permute-start.9 = (f32[384,256]{1,0:T(8,128)S(1)}, f32[384,256]{1,0:T(8,128)S(1)}, u32[]{:S(2)}, u32[]{:S(2)}) collective-permute-start(f32[384,256]{1,0:T(8,128)S(1)} %get-tuple-element.17.refs_4_), channel_id=1, source_target_pairs={{0,192},{64,0},{128,64},{192,128},{1,193},{65,1},{129,65},{193,129... | collective-permute-start | bytes 1179656 | tf_op jit(solution)/shard_map/ppermute | solution.py:23
  53.7 2.2 collective-permute-start.8
  55.9 2.6 %collective-permute-start.7 = (f32[384,256]{1,0:T(8,128)S(1)}, f32[384,256]{1,0:T(8,128)S(1)}, u32[]{:S(2)}, u32[]{:S(2)}) collective-permute-start(f32[384,256]{1,0:T(8,128)S(1)} %get-tuple-element.17.refs_4_), channel_id=1, source_target_pairs={{0,64},{64,128},{128,192},{192,0},{1,65},{65,129},{129,193},{193,1... | collective-permute-start | bytes 1179656 | tf_op jit(solution)/shard_map/ppermute | solution.py:23
  58.5 8.3 %collective-permute-start.6 = (f32[384,256]{1,0:T(8,128)S(1)}, f32[384,256]{1,0:T(8,128)S(1)}, u32[]{:S(2)}, u32[]{:S(2)}) collective-permute-start(f32[384,256]{1,0:T(8,128)S(1)} %get-tuple-element.18.refs_4_), channel_id=1, source_target_pairs={{0,192},{64,0},{128,64},{192,128},{1,193},{65,1},{129,65},{193,129... | collective-permute-start | bytes 1179656 | tf_op jit(solution)/shard_map/ppermute | solution.py:23
  66.9 4.8 %collective-permute-done.refs_1_ = f32[384,512]{1,0:T(8,128)S(1)} collective-permute-done((f32[384,512]{1,0:T(8,128)S(1)}, f32[384,512]{1,0:T(8,128)S(1)}, u32[]{:S(2)}, u32[]{:S(2)}) %collective-permute-start) | collective-permute-done | bytes 786464 | tf_op jit(solution)/shard_map/ppermute | solution.py:23
  71.7 2.3 collective-permute-start.5
  74.0 3.9 %collective-permute-start.4 = (f32[384,256]{1,0:T(8,128)S(1)}, f32[384,256]{1,0:T(8,128)S(1)}, u32[]{:S(2)}, u32[]{:S(2)}) collective-permute-start(f32[384,256]{1,0:T(8,128)S(1)} %get-tuple-element.18.refs_4_), channel_id=1, source_target_pairs={{0,64},{64,128},{128,192},{192,0},{1,65},{65,129},{129,193},{193,1... | collective-permute-start | bytes 1179656 | tf_op jit(solution)/shard_map/ppermute | solution.py:23
  77.9 10.4 %collective-permute-done.7.refs_5_ = f32[384,256]{1,0:T(8,128)S(1)} collective-permute-done((f32[384,256]{1,0:T(8,128)S(1)}, f32[384,256]{1,0:T(8,128)S(1)}, u32[]{:S(2)}, u32[]{:S(2)}) %collective-permute-start.7) | collective-permute-done | bytes 393248 | tf_op jit(solution)/shard_map/ppermute | solution.py:23
  88.3 4.9 %gram.3 = (f32[4,4,136,384]{3,2,1,0:T(8,128)S(1)}, f32[4,4,136,384]{3,2,1,0:T(8,128)S(1)}) custom-call(s32[4]{0:T(128)S(1)} %pad_add_fusion.place, f32[8,128]{1,0:T(8,128)S(1)} %get-tuple-element.13.count, f32[384,512]{1,0:T(8,128)S(1)} %get-tuple-element.14.refs_0_, f32[384,512]{1,0:T(8,128)S(1)} %collective-permute-done.refs_1_, ...), custom_call_target="tpu_custom_call" | custom-call | flops 2264924160 | bytes 9043968 | tf_op jit(solution)/shard_map/gram/pallas_call | solution.py:137
  93.2 0.7 collective-permute-done.5.refs_6_
  93.8 9.8 %collective-permute-done.4.refs_5_ = f32[384,256]{1,0:T(8,128)S(1)} collective-permute-done((f32[384,256]{1,0:T(8,128)S(1)}, f32[384,256]{1,0:T(8,128)S(1)}, u32[]{:S(2)}, u32[]{:S(2)}) %collective-permute-start.4) | collective-permute-done | bytes 393248 | tf_op jit(solution)/shard_map/ppermute | solution.py:23
  103.7 2.9 %gram.5 = f32[4,4,136,384]{3,2,1,0:T(8,128)S(1)} custom-call(s32[4]{0:T(128)S(1)} %pad_add_fusion.place, f32[8,128]{1,0:T(8,128)S(1)} %get-tuple-element.13.count, f32[384,512]{1,0:T(8,128)S(1)} %get-tuple-element.14.refs_0_, f32[384,512]{1,0:T(8,128)S(1)} %collective-permute-done.refs_1_, f32[384,512]{1,0:T(8,128)S(1)} %collective-permute-done.1.refs_2_, ...), custom_call_target="tpu_custom_call" | custom-call | flops 1132462080 | bytes 6094848 | tf_op jit(solution)/shard_map/gram/pallas_call | solution.py:137
  106.5 2.7 %collective-permute-start.10 = (f32[4,4,136,384]{3,2,1,0:T(8,128)S(1)}, f32[4,4,136,384]{3,2,1,0:T(8,128)S(1)}, u32[]{:S(2)}, u32[]{:S(2)}) collective-permute-start(f32[4,4,136,384]{3,2,1,0:T(8,128)S(1)} %gram.5), channel_id=1, source_target_pairs={{0,1},{1,0},{2,3},{3,2},{4,5},{5,4},{6,7},{7,6},{8,9},{9,8},{10,11... | collective-permute-start | bytes 10027016 | tf_op jit(solution)/shard_map/ppermute | solution.py:23
  109.2 2.9 %gram.4 = f32[4,4,136,384]{3,2,1,0:T(8,128)S(1)} custom-call(s32[4]{0:T(128)S(1)} %pad_add_fusion.place, f32[8,128]{1,0:T(8,128)S(1)} %get-tuple-element.13.count, f32[384,512]{1,0:T(8,128)S(1)} %get-tuple-element.14.refs_0_, f32[384,512]{1,0:T(8,128)S(1)} %collective-permute-done.refs_1_, f32[384,512]{1,0:T(8,128)S(1)} %collective-permute-done.1.refs_2_, ...), custom_call_target="tpu_custom_call" | custom-call | flops 1132462080 | bytes 6094848 | tf_op jit(solution)/shard_map/gram/pallas_call | solution.py:137
  112.1 2.5 %collective-permute-done.10 = f32[4,4,136,384]{3,2,1,0:T(8,128)S(1)} collective-permute-done((f32[4,4,136,384]{3,2,1,0:T(8,128)S(1)}, f32[4,4,136,384]{3,2,1,0:T(8,128)S(1)}, u32[]{:S(2)}, u32[]{:S(2)}) %collective-permute-start.10) | collective-permute-done | bytes 3342368 | tf_op jit(solution)/shard_map/ppermute | solution.py:23
  114.6 0.3 add.15
  114.9 42.9 %all_to_all.15 = f32[4,4,136,384]{3,2,1,0:T(8,128)S(1)} all-to-all(f32[4,4,136,384]{3,2,1,0:T(8,128)S(1)} %add.15), channel_id=1, replica_groups=mesh['zh'=2,'y'=4,'x'=4,'l2'=2,'r'=4,'core'=2] {'x'}, dimensions={0} | all-to-all | bytes 6684672 | tf_op jit(solution)/shard_map/all_to_all | solution.py:234
  157.9 1.2 reduce_sum.9
  159.0 53.7 %all_to_all.16.parts = f32[4,136,384]{2,1,0:T(8,128)S(1)} all-to-all(f32[4,136,384]{2,1,0:T(8,128)} %reduce_sum.9), channel_id=1, replica_groups=mesh['zh'=2,'y'=4,'x'=4,'l2'=2,'r'=4,'core'=2] {'r'}, dimensions={0} | all-to-all | bytes 1671168 | tf_op jit(solution)/shard_map/all_to_all | solution.py:234
  212.8 26.1 %all_to_all.17.parts = f32[4,40,384]{2,1,0:T(8,128)S(1)} all-to-all(f32[4,40,384]{2,1,0:T(8,128)S(1)} %share.1), channel_id=1, replica_groups=mesh['zh'=2,'y'=4,'x'=4,'l2'=2,'r'=4,'core'=2] {'zh','l2'}, dimensions={0} | all-to-all | bytes 491520 | tf_op jit(solution)/shard_map/all_to_all | solution.py:234
  238.9 1.3 finish.1
  (9 shorter events, 0.1 us)
Async XLA Ops:
  0.8 1.7 copy-start
  2.4 0.7 copy-start.1
  6.6 41.4 %collective-permute-start.3 = (f32[384,512]{1,0:T(8,128)S(1)}, f32[384,512]{1,0:T(8,128)S(1)}, u32[]{:S(2)}, u32[]{:S(2)}) collective-permute-start(f32[384,512]{1,0:T(8,128)S(1)} %get-tuple-element.11), channel_id=1, source_target_pairs={{0,256},{256,0},{1,257},{257,1},{2,258},{258,2},{3,259},{259,3},{4... | collective-permute-start | bytes 2359304 | tf_op jit(solution)/shard_map/ppermute | solution.py:23
  25.7 30.2 %collective-permute-start.2 = (f32[384,512]{1,0:T(8,128)S(1)}, f32[384,512]{1,0:T(8,128)S(1)}, u32[]{:S(2)}, u32[]{:S(2)}) collective-permute-start(f32[384,512]{1,0:T(8,128)S(1)} %get-tuple-element.14.refs_0_), channel_id=1, source_target_pairs={{0,192},{64,0},{128,64},{192,128},{1,193},{65,1},{129,65},{193,129... | collective-permute-start | bytes 2359304 | tf_op jit(solution)/shard_map/ppermute | solution.py:23
  30.4 28.2 %collective-permute-start.1 = (f32[384,512]{1,0:T(8,128)S(1)}, f32[384,512]{1,0:T(8,128)S(1)}, u32[]{:S(2)}, u32[]{:S(2)}) collective-permute-start(f32[384,512]{1,0:T(8,128)S(1)} %get-tuple-element.14.refs_0_), channel_id=1, source_target_pairs={{0,128},{64,192},{128,0},{192,64},{1,129},{65,193},{129,1},{193,65... | collective-permute-start | bytes 2359304 | tf_op jit(solution)/shard_map/ppermute | solution.py:23
  32.6 39.1 %collective-permute-start = (f32[384,512]{1,0:T(8,128)S(1)}, f32[384,512]{1,0:T(8,128)S(1)}, u32[]{:S(2)}, u32[]{:S(2)}) collective-permute-start(f32[384,512]{1,0:T(8,128)S(1)} %get-tuple-element.14.refs_0_), channel_id=1, source_target_pairs={{0,64},{64,128},{128,192},{192,0},{1,65},{65,129},{129,193},{193,1... | collective-permute-start | bytes 2359304 | tf_op jit(solution)/shard_map/ppermute | solution.py:23
  48.0 25.9 %collective-permute-start.9 = (f32[384,256]{1,0:T(8,128)S(1)}, f32[384,256]{1,0:T(8,128)S(1)}, u32[]{:S(2)}, u32[]{:S(2)}) collective-permute-start(f32[384,256]{1,0:T(8,128)S(1)} %get-tuple-element.17.refs_4_), channel_id=1, source_target_pairs={{0,192},{64,0},{128,64},{192,128},{1,193},{65,1},{129,65},{193,129... | collective-permute-start | bytes 1179656 | tf_op jit(solution)/shard_map/ppermute | solution.py:23
  53.7 24.2 %collective-permute-start.8 = (f32[384,256]{1,0:T(8,128)S(1)}, f32[384,256]{1,0:T(8,128)S(1)}, u32[]{:S(2)}, u32[]{:S(2)}) collective-permute-start(f32[384,256]{1,0:T(8,128)S(1)} %get-tuple-element.17.refs_4_), channel_id=1, source_target_pairs={{0,128},{64,192},{128,0},{192,64},{1,129},{65,193},{129,1},{193,65... | collective-permute-start | bytes 1179656 | tf_op jit(solution)/shard_map/ppermute | solution.py:23
  55.9 32.4 %collective-permute-start.7 = (f32[384,256]{1,0:T(8,128)S(1)}, f32[384,256]{1,0:T(8,128)S(1)}, u32[]{:S(2)}, u32[]{:S(2)}) collective-permute-start(f32[384,256]{1,0:T(8,128)S(1)} %get-tuple-element.17.refs_4_), channel_id=1, source_target_pairs={{0,64},{64,128},{128,192},{192,0},{1,65},{65,129},{129,193},{193,1... | collective-permute-start | bytes 1179656 | tf_op jit(solution)/shard_map/ppermute | solution.py:23
  58.5 34.6 %collective-permute-start.6 = (f32[384,256]{1,0:T(8,128)S(1)}, f32[384,256]{1,0:T(8,128)S(1)}, u32[]{:S(2)}, u32[]{:S(2)}) collective-permute-start(f32[384,256]{1,0:T(8,128)S(1)} %get-tuple-element.18.refs_4_), channel_id=1, source_target_pairs={{0,192},{64,0},{128,64},{192,128},{1,193},{65,1},{129,65},{193,129... | collective-permute-start | bytes 1179656 | tf_op jit(solution)/shard_map/ppermute | solution.py:23
  71.7 22.1 %collective-permute-start.5 = (f32[384,256]{1,0:T(8,128)S(1)}, f32[384,256]{1,0:T(8,128)S(1)}, u32[]{:S(2)}, u32[]{:S(2)}) collective-permute-start(f32[384,256]{1,0:T(8,128)S(1)} %get-tuple-element.18.refs_4_), channel_id=1, source_target_pairs={{0,128},{64,192},{128,0},{192,64},{1,129},{65,193},{129,1},{193,65... | collective-permute-start | bytes 1179656 | tf_op jit(solution)/shard_map/ppermute | solution.py:23
  74.0 29.7 %collective-permute-start.4 = (f32[384,256]{1,0:T(8,128)S(1)}, f32[384,256]{1,0:T(8,128)S(1)}, u32[]{:S(2)}, u32[]{:S(2)}) collective-permute-start(f32[384,256]{1,0:T(8,128)S(1)} %get-tuple-element.18.refs_4_), channel_id=1, source_target_pairs={{0,64},{64,128},{128,192},{192,0},{1,65},{65,129},{129,193},{193,1... | collective-permute-start | bytes 1179656 | tf_op jit(solution)/shard_map/ppermute | solution.py:23
  106.5 8.1 %collective-permute-start.10 = (f32[4,4,136,384]{3,2,1,0:T(8,128)S(1)}, f32[4,4,136,384]{3,2,1,0:T(8,128)S(1)}, u32[]{:S(2)}, u32[]{:S(2)}) collective-permute-start(f32[4,4,136,384]{3,2,1,0:T(8,128)S(1)} %gram.5), channel_id=1, source_target_pairs={{0,1},{1,0},{2,3},{3,2},{4,5},{5,4},{6,7},{7,6},{8,9},{9,8},{10,11... | collective-permute-start | bytes 10027016 | tf_op jit(solution)/shard_map/ppermute | solution.py:23

commit v4 on v3

v4 whole, which is shorter than its diff:
```python
import functools
import math

import jax
import jax.numpy as jnp
import numpy as np
from jax import lax
from jax.experimental import pallas as pl
from jax.experimental.pallas import tpu as pltpu
from jax.sharding import PartitionSpec as P

AXES = {"zh": 2, "y": 4, "x": 4, "l2": 2, "r": 4, "core": 2}
FRAMES, PIX = ("zh", "y"), ("x", "l2", "r", "core")
SHIFTS = 5
ROWS = 6
VMEM = pl.BlockSpec(memory_space=pltpu.VMEM)
SMEM = pl.BlockSpec(memory_space=pltpu.SMEM)
PARAMS = pltpu.CompilerParams(vmem_limit_bytes=24 * 1024 * 1024)
F32 = jnp.float32


def send(value, **moves):
    names = tuple(AXES)
    sizes = tuple(AXES.values())
    pairs = []
    for source in range(math.prod(sizes)):
        at = dict(zip(names, (int(i) for i in np.unravel_index(source, sizes))))
        to = [moves[name](at) % AXES[name] if name in moves else at[name] for name in names]
        pairs.append((source, int(np.ravel_multi_index(to, sizes))))
    return lax.ppermute(value, names, pairs)


def along_z(by):
    def target(at):
        z = at["zh"] * 8 + at["l2"] * 4 + at["r"]
        return (z + (by(at["core"]) if callable(by) else by)) % 16

    return {
        "zh": lambda at: target(at) // 8,
        "l2": lambda at: target(at) // 4,
        "r": lambda at: target(at),
    }


def split2(value):
    high = value.astype(jnp.bfloat16)
    return high, (value - high.astype(F32)).astype(jnp.bfloat16)


def split3(value):
    high = value.astype(jnp.bfloat16)
    return (high, *split2(value - high.astype(F32)))


def dot_nn(left, right):
    return jnp.dot(left, right, preferred_element_type=F32)


def dot_nt(left, right):
    return lax.dot_general(left, right, (((1,), (1,)), ((), ())), preferred_element_type=F32)


def select_kernel(flip, place, image, index, mask, out, count):
    band = image.shape[1]
    half = index.shape[1] // 2
    begin = pl.multiple_of((place[0] ^ flip) * half, half)
    columns = lax.broadcasted_iota(jnp.int32, (band, half), 0)
    hot = (columns == index[:, pl.ds(begin, half)]).astype(F32).astype(jnp.bfloat16)
    good = mask[...].astype(F32)
    picked = sum(dot_nn(part, hot) for part in reversed(split3(image[...] * good)))
    out[...] = picked
    goods = dot_nn(jnp.broadcast_to(good, (8, band)).astype(jnp.bfloat16), hot)
    count[...] = jnp.broadcast_to(jnp.sum(goods, axis=1, keepdims=True), (8, 128))


def select(flip, place, image, index, mask):
    frames, band = image.shape
    half = index.shape[1] // 2
    block = jax.ShapeDtypeStruct((frames, half), F32)
    return pl.pallas_call(
        functools.partial(select_kernel, flip),
        out_shape=(block, jax.ShapeDtypeStruct((8, 128), F32)),
        in_specs=[SMEM, VMEM, VMEM, VMEM],
        out_specs=(VMEM, VMEM),
        compiler_params=PARAMS,
        cost_estimate=pl.CostEstimate(
            flops=2 * frames * band * half * 3, bytes_accessed=frames * band * 4, transcendentals=0
        ),
        name="select",
    )(place, image, index, mask)


def gram_kernel(slots, shifts, place, count, stay0, move0, *refs):
    last = shifts == (2,)
    backs, refs = (refs[:3], refs[3:]) if last else (refs[:6], refs[6:])
    previous, outs, ordered = refs[: -1 - len(slots)], refs[-1 - len(slots) : -1], refs[-1]
    zh, y, core, x, r = (place[i] for i in (0, 1, 2, 4, 5))
    frames, width = move0.shape
    owners = AXES["x"] * AXES["r"]
    mine = 2 * ROWS
    one = jnp.ones((8, width), jnp.bfloat16)
    ones = jnp.concatenate([one, one, jnp.zeros_like(one)], axis=1)
    line = lax.broadcasted_iota(jnp.int32, (16, frames), 0)

    def block(back, label):
        if back == 0:
            stay, move = stay0[...], move0[...]
        else:
            at = 3 if back == 3 else 0
            stay, one, two = (ref[...] for ref in backs[at : at + 3])
            move = jnp.concatenate([one, two], axis=1)
        return jnp.where(label == zh, stay, move)

    def place_of(owner):
        apart = x ^ (owner // AXES["r"])
        turn = (owner % AXES["r"] - r) & 3
        side = turn >> 1
        near = jnp.where(side == 0, 2, 1)
        chunk = jnp.where(apart == 3, 3 - near, jnp.where(apart == 1, near, apart + (apart >> 1)))
        return side, chunk, turn & 1

    for at, slot in enumerate(slots):
        first = (core ^ slot) == 0
        out = outs[at]
        rows = []
        for label in range(2):
            left = block(0, label)
            for owner in range(owners):
                for l2 in range(2):
                    begin = owner // 4 * (frames // 4) + (l2 * 4 + owner % 4) * mine
                    to = owner * mine + l2 * ROWS
                    ordered[to : to + ROWS, :] = jnp.where(
                        first, left[begin : begin + ROWS], left[begin + ROWS : begin + mine]
                    )
            high, low = split2(ordered[...])
            rows.append(
                jnp.concatenate([jnp.concatenate([high, high, low], axis=1), ones], axis=0)
            )
        sums = jnp.where((line & 7) == SHIFTS, count[0:1, 0:1], 0.0)
        size = owners * mine
        if last:
            out[...] = previous[at][...]
        for shift in shifts:
            tiles = []
            for label in range(2):
                if shift < 4:
                    other = block(shift, label ^ (y < shift).astype(jnp.int32))
                else:
                    other = block(0, 1 - label)
                high, low = split2(other)
                tile = dot_nt(rows[label], jnp.concatenate([high, low, high], axis=1))
                sums = jnp.where(line == label * 8 + shift, tile[size : size + 1], sums)
                tiles.append(tile)
            for owner in range(owners):
                out[(*place_of(owner), slice(shift * 24, shift * 24 + 24))] = jnp.concatenate(
                    [tile[owner * mine : (owner + 1) * mine] for tile in tiles], axis=0
                )
        for owner in range(owners):
            where = (*place_of(owner), slice(120, 136))
            if last:
                out[where] = jnp.where((line & 7) == 2, sums, out[where])
            else:
                out[where] = sums


def gram(slots, shifts, place, count, stay0, move0, backs, previous=()):
    frames, width = move0.shape
    operands = [place, count, stay0, move0, *backs, *previous]
    result = jax.ShapeDtypeStruct((2, AXES["x"], 2, 136, frames), F32)
    return pl.pallas_call(
        functools.partial(gram_kernel, slots, shifts),
        out_shape=(result,) * len(slots),
        in_specs=[SMEM] + [VMEM] * (len(operands) - 1),
        out_specs=(VMEM,) * len(slots),
        scratch_shapes=[pltpu.VMEM((frames // 2, width), F32)],
        compiler_params=PARAMS,
        cost_estimate=pl.CostEstimate(
            flops=len(slots) * len(shifts) * 2 * frames * frames * width * 3,
            bytes_accessed=6 * frames * width * 4 + len(slots) * 5 * frames * frames * 4,
            transcendentals=0,
        ),
        name="gram",
    )(*operands)


def share_kernel(place, near, below, above, two, *outs):
    total = (near[0] + below[...]) + (above[...] + two[...])
    out = outs[-1]
    for zh in range(2):
        for l2 in range(2):
            to = (zh ^ place[0]) * 2 + (l2 ^ place[6])
            for shift in range(SHIFTS):
                begin = shift * 24 + zh * 12 + l2 * ROWS
                out[to, shift * ROWS : (shift + 1) * ROWS] = total[begin : begin + ROWS]
            out[to, 30:32] = jnp.zeros((2, total.shape[1]), F32)
            out[to, 32:40] = total[120 + zh * 8 : 128 + zh * 8]
    for to in range(4):
        outs[to][...] = out[to]


def share(place, *parts):
    frames = parts[-1].shape[-1]
    return pl.pallas_call(
        share_kernel,
        out_shape=(jax.ShapeDtypeStruct((40, frames), F32),) * 4,
        in_specs=[SMEM] + [VMEM] * 4,
        out_specs=(VMEM,) * 4,
        scratch_shapes=[pltpu.VMEM((4, 40, frames), F32)],
        compiler_params=PARAMS,
        name="share",
    )(place, *parts)


def finish_kernel(place, one, two, three, four, out):
    total = (one[...] + two[...]) + (three[...] + four[...])
    frames = total.shape[1]
    sums = total[32 : 32 + SHIFTS]
    good = total[32 + SHIFTS : 33 + SHIFTS]
    line = lax.broadcasted_iota(jnp.int32, (ROWS, frames), 0)
    lane = lax.broadcasted_iota(jnp.int32, (ROWS, frames), 1)
    mine = jnp.where(lane == line + place[3], sums[0:1], 0.0)
    own = jnp.sum(mine, axis=1, keepdims=True)
    for shift in range(SHIFTS):
        tile = total[shift * ROWS : (shift + 1) * ROWS]
        out[shift] = tile * good / (own * sums[shift : shift + 1])


def finish(place, *parts):
    return pl.pallas_call(
        finish_kernel,
        out_shape=jax.ShapeDtypeStruct((SHIFTS, ROWS, parts[0].shape[-1]), F32),
        in_specs=[SMEM] + [VMEM] * 4,
        out_specs=VMEM,
        compiler_params=PARAMS,
        name="finish",
    )(place, *parts)


def body(intensity, circle_index, pixel_mask):
    place = jnp.stack(
        [
            lax.axis_index("zh"),
            lax.axis_index("y"),
            lax.axis_index("core"),
            lax.axis_index(PIX) * ROWS,
            lax.axis_index("x"),
            lax.axis_index("r"),
            lax.axis_index("l2"),
        ]
    ).astype(jnp.int32)
    index, mask = circle_index[None, :], pixel_mask[None, :]

    def after(value, *others):
        return lax.optimization_barrier((value, *others))[0]

    def up(value):
        return send(value, y=lambda at: at["y"] + 1)

    def down(value):
        return send(value, y=lambda at: at["y"] - 1)

    given, _ = select(0, place, intensity, index, mask)
    moved = send(given, zh=lambda at: at["zh"] + 1)
    kept, count = select(1, place, intensity, after(index, given), mask)
    kept1, kept3 = up(kept), down(kept)
    kept2 = send(kept, y=lambda at: at["y"] + 2)
    half = moved.shape[1] // 2
    one, two, *_ = lax.optimization_barrier(
        (moved[:, :half], moved[:, half:], kept1, kept2, kept3)
    )
    one1, two3 = up(one), down(two)
    two1, one3 = up(two), down(one)
    moved2 = (up(one1), down(two3))
    backs = (kept1, one1, two1, kept3, one3, two3)
    early = gram((1, 0), (0, 1, 3, 4), place, count, kept, moved, backs)
    (give,) = gram((1,), (2,), place, count, kept, moved, (kept2, *moved2), early[:1])
    (keep,) = gram((0,), (2,), place, count, kept, moved, (kept2, *moved2), early[1:])

    def to_p(value):
        return send(value, x=lambda at: at["x"] ^ 1)

    def to_q(value):
        return send(value, x=lambda at: 3 - at["x"])

    total = keep + send(give, core=lambda at: 1 - at["core"])
    near = total[0, :2] + to_p(total[0, 2:])
    away = total[1, :2] + to_q(total[1, 2:])
    near = near[0] + to_q(near[1])
    away = away[0] + to_p(away[1])
    below = send(near[1], **along_z(1))
    above = send(away[1], **along_z(-1))
    middle = send(away[0], **along_z(lambda core: 2 - 4 * core))
    pieces = share(place, near, below, above, middle)
    far = send(pieces[2], zh=lambda at: at["zh"] + 1)
    farther = send(pieces[3], zh=lambda at: at["zh"] + 1, l2=lambda at: at["l2"] + 1)
    next_one = send(pieces[1], l2=lambda at: at["l2"] + 1)
    return finish(place, pieces[0], far, farther, next_one)


def solution(mesh):
    split = jax.sharding.Mesh(mesh.devices.reshape(tuple(AXES.values())), tuple(AXES))
    return jax.shard_map(
        body,
        mesh=split,
        in_specs=(P(FRAMES, PIX), P(PIX), P(PIX)),
        out_specs=P(None, (*FRAMES, *PIX), None),
        check_vma=False,
    )
```

time: 245 us -> 218 us (0.89)
  blocking collectives: 123 us -> 0 us
  starting transfers between devices: 53.4 us -> 117 us
  waiting for transfers between devices: 40.9 us -> 73 us
    all_to_all x3 -> x0, blocking collectives: 123 us -> none  [exchange(): return lax.all_to_all(parts, axis, 0, 0, tiled=True)]
    ppermute x11 -> x21, starting transfers between devices: 53.4 us -> 117 us  [send(): return lax.ppermute(value, names, pairs)]
    ppermute x11 -> x21, waiting for transfers between devices: 40.9 us -> 73 us  [send(): return lax.ppermute(value, names, pairs)]
  transfers between devices with their start and end apart: 11 -> 21, of which waited for: 6 -> 12; matrix products, arithmetic and copies ran while one was open for 0% -> 0% of each run, Pallas kernels for 4% -> 6%
where the time goes in v4:
time: 218 us; the launch traced here: 214 us
  starting transfers between devices  117 us (54%)
  waiting for transfers between devices  73 us (33%)
  Pallas kernels  19.8 us (9%)
  local copies, waits for them, and re-layouts  3.4 us (2%)
    ppermute x21, starting transfers between devices, send(): return lax.ppermute(value, names, pairs)  117 us
    ppermute x21, waiting for transfers between devices, send(): return lax.ppermute(value, names, pairs)  73 us
    pallas_call x3, Pallas kernels, gram(): pl.pallas_call(functools.partial(gram_kernel, slots, shifts), out_shape=(...  11.6 us
    pallas_call x2, Pallas kernels, select(): pl.pallas_call(functools.partial(select_kernel, flip), out_shape=(block,...  6.31 us
  transfers between devices with their start and end apart: 21, of which 12 were waited for; matrix products, arithmetic and copies ran while one was open for 0% of the time, Pallas kernels for 6%

profile of v4, /device:TPU:1, one launch (start us, length us, event | category | flops | bytes accessed | tf_op | source)
XLA Modules:
  0.0 213.9 jit_solution(4164457452501665524)
XLA Ops:
  3.1 3.5 %select.2 = (f32[384,512]{1,0:T(8,128)S(1)}, f32[8,128]{1,0:T(8,128)}) custom-call(s32[7]{0:T(128)S(1)} %stack.31.place, f32[384,1536]{1,0:T(8,128)S(1)} %copy-done, s32[1,1024]{1,0:T(1,128)S(1)} %bitcast.38, s32[1,1536]{1,0:T(1,128)S(1)} %broadcast_in_dim.7.mask), custom_call_target="tpu_custom_call" | custom-call | flops 1811939328 | bytes 2359296 | tf_op jit(solution)/shard_map/select/pallas_call | solution.py:80
  6.6 16.3 %collective-permute-start = (f32[384,512]{1,0:T(8,128)S(1)}, f32[384,512]{1,0:T(8,128)S(1)}, u32[]{:S(2)}, u32[]{:S(2)}) collective-permute-start(f32[384,512]{1,0:T(8,128)S(1)} %get-tuple-element.17), channel_id=1, source_target_pairs={{0,256},{1,257},{2,258},{3,259},{4,260},{5,261},{6,262},{7,263},{8... | collective-permute-start | bytes 2359304 | tf_op jit(solution)/shard_map/ppermute | solution.py:30
  22.9 2.8 %select.3 = (f32[384,512]{1,0:T(8,128)S(1)}, f32[8,128]{1,0:T(8,128)S(1)}) custom-call(s32[7]{0:T(128)S(1)} %stack.31.place, f32[384,1536]{1,0:T(8,128)S(1)} %copy-done, s32[1,1024]{1,0:T(1,128)S(1)} %bitcast.39, s32[1,1536]{1,0:T(1,128)S(1)} %broadcast_in_dim.7.mask), custom_call_target="tpu_custom_call" | custom-call | flops 1811939328 | bytes 2359296 | tf_op jit(solution)/shard_map/select/pallas_call | solution.py:80
  25.7 4.6 %collective-permute-start.3 = (f32[384,512]{1,0:T(8,128)S(1)}, f32[384,512]{1,0:T(8,128)S(1)}, u32[]{:S(2)}, u32[]{:S(2)}) collective-permute-start(f32[384,512]{1,0:T(8,128)S(1)} %get-tuple-element.20.stay0), channel_id=1, source_target_pairs={{0,192},{1,193},{2,194},{3,195},{4,196},{5,197},{6,198},{7,199},{8... | collective-permute-start | bytes 2359304 | tf_op jit(solution)/shard_map/ppermute | solution.py:30
  30.4 1.9 collective-permute-start.2
  32.3 3.5 %collective-permute-start.1 = (f32[384,512]{1,0:T(8,128)S(1)}, f32[384,512]{1,0:T(8,128)S(1)}, u32[]{:S(2)}, u32[]{:S(2)}) collective-permute-start(f32[384,512]{1,0:T(8,128)S(1)} %get-tuple-element.20.stay0), channel_id=1, source_target_pairs={{0,128},{1,129},{2,130},{3,131},{4,132},{5,133},{6,134},{7,135},{8... | collective-permute-start | bytes 2359304 | tf_op jit(solution)/shard_map/ppermute | solution.py:30
  35.8 12.1 %collective-permute-done.move0 = f32[384,512]{1,0:T(8,128)S(1)} collective-permute-done((f32[384,512]{1,0:T(8,128)S(1)}, f32[384,512]{1,0:T(8,128)S(1)}, u32[]{:S(2)}, u32[]{:S(2)}) %collective-permute-start) | collective-permute-done | bytes 786464 | tf_op jit(solution)/shard_map/ppermute | solution.py:30
  48.0 4.3 %collective-permute-done.2.refs_0_ = f32[384,512]{1,0:T(8,128)S(1)} collective-permute-done((f32[384,512]{1,0:T(8,128)S(1)}, f32[384,512]{1,0:T(8,128)S(1)}, u32[]{:S(2)}, u32[]{:S(2)}) %collective-permute-start.2) | collective-permute-done | bytes 786464 | tf_op jit(solution)/shard_map/ppermute | solution.py:30
  52.3 14.8 %collective-permute-done.1.refs_0_ = f32[384,512]{1,0:T(8,128)S(1)} collective-permute-done((f32[384,512]{1,0:T(8,128)S(1)}, f32[384,512]{1,0:T(8,128)S(1)}, u32[]{:S(2)}, u32[]{:S(2)}) %collective-permute-start.1) | collective-permute-done | bytes 786464 | tf_op jit(solution)/shard_map/ppermute | solution.py:30
  69.1 4.6 %collective-permute-start.6 = (f32[384,256]{1,0:T(8,128)S(1)}, f32[384,256]{1,0:T(8,128)S(1)}, u32[]{:S(2)}, u32[]{:S(2)}) collective-permute-start(f32[384,256]{1,0:T(8,128)S(1)} %get-tuple-element.22), channel_id=1, source_target_pairs={{0,192},{1,193},{2,194},{3,195},{4,196},{5,197},{6,198},{7,199},{8... | collective-permute-start | bytes 1179656 | tf_op jit(solution)/shard_map/ppermute | solution.py:30
  73.6 1.9 collective-permute-start.9
  75.6 3.4 %collective-permute-start.8 = (f32[384,256]{1,0:T(8,128)S(1)}, f32[384,256]{1,0:T(8,128)S(1)}, u32[]{:S(2)}, u32[]{:S(2)}) collective-permute-start(f32[384,256]{1,0:T(8,128)S(1)} %get-tuple-element.22), channel_id=1, source_target_pairs={{0,64},{1,65},{2,66},{3,67},{4,68},{5,69},{6,70},{7,71},{8,72},{9,... | collective-permute-start | bytes 1179656 | tf_op jit(solution)/shard_map/ppermute | solution.py:30
  79.0 1.9 collective-permute-start.5
  80.9 4.8 %collective-permute-start.7 = (f32[384,256]{1,0:T(8,128)S(1)}, f32[384,256]{1,0:T(8,128)S(1)}, u32[]{:S(2)}, u32[]{:S(2)}) collective-permute-start(f32[384,256]{1,0:T(8,128)S(1)} %collective-permute-done.6.refs_5_), channel_id=1, source_target_pairs={{0,192},{1,193},{2,194},{3,195},{4,196},{5,197},{6,198},{7,199},{8... | collective-permute-start | bytes 1179656 | tf_op jit(solution)/shard_map/ppermute | solution.py:30
  87.0 7.5 %gram.3 = (f32[2,4,2,136,384]{4,3,2,1,0:T(8,128)S(1)}, f32[2,4,2,136,384]{4,3,2,1,0:T(8,128)S(1)}) custom-call(s32[7]{0:T(128)S(1)} %stack.31.place, f32[8,128]{1,0:T(8,128)S(1)} %get-tuple-element.19.count, f32[384,512]{1,0:T(8,128)S(1)} %get-tuple-element.20.stay0, f32[384,512]{1,0:T(8,128)S(1)} %collective-permute-done.move0, ...), custom_call_target="tpu_custom_call" | custom-call | flops 3623878656 | bytes 10616832 | tf_op jit(solution)/shard_map/gram/pallas_call | solution.py:170
  95.5 2.1 gram.5
  97.5 9.3 %collective-permute-start.10 = (f32[2,4,2,136,384]{4,3,2,1,0:T(8,128)S(1)}, f32[2,4,2,136,384]{4,3,2,1,0:T(8,128)S(1)}, u32[]{:S(2)}, u32[]{:S(2)}) collective-permute-start(f32[2,4,2,136,384]{4,3,2,1,0:T(8,128)S(1)} %gram.5), channel_id=1, source_target_pairs={{0,1},{1,0},{2,3},{3,2},{4,5},{5,4},{6,7},{7,6},{8,9},{9,8},{10,11... | collective-permute-start | bytes 10027016 | tf_op jit(solution)/shard_map/ppermute | solution.py:30
  106.8 2.0 gram.4
  108.9 3.5 %collective-permute-done.10 = f32[2,4,2,136,384]{4,3,2,1,0:T(8,128)S(1)} collective-permute-done((f32[2,4,2,136,384]{4,3,2,1,0:T(8,128)S(1)}, f32[2,4,2,136,384]{4,3,2,1,0:T(8,128)S(1)}, u32[]{:S(2)}, u32[]{:S(2)}) %collective-permute-start.10) | collective-permute-done | bytes 3342368 | tf_op jit(solution)/shard_map/ppermute | solution.py:30
  112.8 4.4 %collective-permute-start.14 = (f32[2,2,136,384]{3,2,1,0:T(8,128)S(1)}, f32[2,2,136,384]{3,2,1,0:T(8,128)S(1)}, u32[]{:S(2)}, u32[]{:S(2)}) collective-permute-start(f32[2,2,136,384]{3,2,1,0:T(8,128)S(1)} %get-tuple-element.31), channel_id=1, source_target_pairs={{0,48},{1,49},{2,50},{3,51},{4,52},{5,53},{6,54},{7,55},{8,56},{9,... | collective-permute-start | bytes 2506760 | tf_op jit(solution)/shard_map/ppermute | solution.py:30
  117.2 1.9 collective-permute-start.11
  119.2 16.6 %collective-permute-done.14 = f32[2,2,136,384]{3,2,1,0:T(8,128)S(1)} collective-permute-done((f32[2,2,136,384]{3,2,1,0:T(8,128)S(1)}, f32[2,2,136,384]{3,2,1,0:T(8,128)S(1)}, u32[]{:S(2)}, u32[]{:S(2)}) %collective-permute-start.14) | collective-permute-done | bytes 835616 | tf_op jit(solution)/shard_map/ppermute | solution.py:30
  135.7 2.9 %collective-permute-done.11 = f32[2,2,136,384]{3,2,1,0:T(8,128)S(1)} collective-permute-done((f32[2,2,136,384]{3,2,1,0:T(8,128)S(1)}, f32[2,2,136,384]{3,2,1,0:T(8,128)S(1)}, u32[]{:S(2)}, u32[]{:S(2)}) %collective-permute-start.11) | collective-permute-done | bytes 835616 | tf_op jit(solution)/shard_map/ppermute | solution.py:30
  138.8 2.1 collective-permute-start.12
  142.9 8.6 %collective-permute-done.12 = f32[2,136,384]{2,1,0:T(8,128)S(1)} collective-permute-done((f32[2,136,384]{2,1,0:T(8,128)S(1)}, f32[2,136,384]{2,1,0:T(8,128)S(1)}, u32[]{:S(2)}, u32[]{:S(2)}) %collective-permute-start.12) | collective-permute-done | bytes 417824 | tf_op jit(solution)/shard_map/ppermute | solution.py:30
  151.6 25.8 %collective-permute-start.13 = (f32[136,384]{1,0:T(8,128)S(1)}, f32[136,384]{1,0:T(8,128)S(1)}, u32[]{:S(2)}, u32[]{:S(2)}) collective-permute-start(f32[136,384]{1,0:T(8,128)S(1)} %slice_bitcast_fusion.10), channel_id=1, source_target_pairs={{0,2},{1,3},{2,4},{3,5},{4,6},{5,7},{6,8},{7,9},{8,10},{9,11},{10,... | collective-permute-start | bytes 626696 | tf_op jit(solution)/shard_map/ppermute | solution.py:30
  177.5 7.1 %collective-permute-start.17 = (f32[136,384]{1,0:T(8,128)S(1)}, f32[136,384]{1,0:T(8,128)S(1)}, u32[]{:S(2)}, u32[]{:S(2)}) collective-permute-start(f32[136,384]{1,0:T(8,128)S(1)} %get-tuple-element.35), channel_id=1, source_target_pairs={{0,4},{1,269},{2,6},{3,271},{4,8},{5,1},{6,10},{7,3},{8,12},{9,5},... | collective-permute-start | bytes 626696 | tf_op jit(solution)/shard_map/ppermute | solution.py:30
  184.6 3.4 %collective-permute-start.16 = (f32[136,384]{1,0:T(8,128)S(1)}, f32[136,384]{1,0:T(8,128)S(1)}, u32[]{:S(2)}, u32[]{:S(2)}) collective-permute-start(f32[136,384]{1,0:T(8,128)S(1)} %get-tuple-element.36), channel_id=1, source_target_pairs={{0,270},{1,271},{2,0},{3,1},{4,2},{5,3},{6,4},{7,5},{8,6},{9,7},{1... | collective-permute-start | bytes 626696 | tf_op jit(solution)/shard_map/ppermute | solution.py:30
  187.9 3.9 %collective-permute-done.16.above = f32[136,384]{1,0:T(8,128)S(1)} collective-permute-done((f32[136,384]{1,0:T(8,128)S(1)}, f32[136,384]{1,0:T(8,128)S(1)}, u32[]{:S(2)}, u32[]{:S(2)}) %collective-permute-start.16) | collective-permute-done | bytes 208928 | tf_op jit(solution)/shard_map/ppermute | solution.py:30
  192.5 9.0 %collective-permute-start.18 = (f32[40,384]{1,0:T(8,128)S(1)}, f32[40,384]{1,0:T(8,128)S(1)}, u32[]{:S(2)}, u32[]{:S(2)}) collective-permute-start(f32[40,384]{1,0:T(8,128)S(1)} %get-tuple-element.26), channel_id=1, source_target_pairs={{0,256},{1,257},{2,258},{3,259},{4,260},{5,261},{6,262},{7,263},{8... | collective-permute-start | bytes 184328 | tf_op jit(solution)/shard_map/ppermute | solution.py:30
  203.5 5.2 %collective-permute-start.20 = (f32[40,384]{1,0:T(8,128)S(1)}, f32[40,384]{1,0:T(8,128)S(1)}, u32[]{:S(2)}, u32[]{:S(2)}) collective-permute-start(f32[40,384]{1,0:T(8,128)S(1)} %get-tuple-element.28), channel_id=1, source_target_pairs={{0,8},{1,9},{2,10},{3,11},{4,12},{5,13},{6,14},{7,15},{8,0},{9,1},... | collective-permute-start | bytes 184328 | tf_op jit(solution)/shard_map/ppermute | solution.py:30
  210.5 2.1 collective-permute-done.20.four
  (33 shorter events, 15.8 us)
Async XLA Ops:
  0.8 1.7 copy-start
  2.5 0.7 copy-start.1
  6.6 41.4 %collective-permute-start = (f32[384,512]{1,0:T(8,128)S(1)}, f32[384,512]{1,0:T(8,128)S(1)}, u32[]{:S(2)}, u32[]{:S(2)}) collective-permute-start(f32[384,512]{1,0:T(8,128)S(1)} %get-tuple-element.17), channel_id=1, source_target_pairs={{0,256},{1,257},{2,258},{3,259},{4,260},{5,261},{6,262},{7,263},{8... | collective-permute-start | bytes 2359304 | tf_op jit(solution)/shard_map/ppermute | solution.py:30
  25.7 22.3 %collective-permute-start.3 = (f32[384,512]{1,0:T(8,128)S(1)}, f32[384,512]{1,0:T(8,128)S(1)}, u32[]{:S(2)}, u32[]{:S(2)}) collective-permute-start(f32[384,512]{1,0:T(8,128)S(1)} %get-tuple-element.20.stay0), channel_id=1, source_target_pairs={{0,192},{1,193},{2,194},{3,195},{4,196},{5,197},{6,198},{7,199},{8... | collective-permute-start | bytes 2359304 | tf_op jit(solution)/shard_map/ppermute | solution.py:30
  30.4 21.9 %collective-permute-start.2 = (f32[384,512]{1,0:T(8,128)S(1)}, f32[384,512]{1,0:T(8,128)S(1)}, u32[]{:S(2)}, u32[]{:S(2)}) collective-permute-start(f32[384,512]{1,0:T(8,128)S(1)} %get-tuple-element.20.stay0), channel_id=1, source_target_pairs={{0,64},{1,65},{2,66},{3,67},{4,68},{5,69},{6,70},{7,71},{8,72},{9,... | collective-permute-start | bytes 2359304 | tf_op jit(solution)/shard_map/ppermute | solution.py:30
  32.3 34.8 %collective-permute-start.1 = (f32[384,512]{1,0:T(8,128)S(1)}, f32[384,512]{1,0:T(8,128)S(1)}, u32[]{:S(2)}, u32[]{:S(2)}) collective-permute-start(f32[384,512]{1,0:T(8,128)S(1)} %get-tuple-element.20.stay0), channel_id=1, source_target_pairs={{0,128},{1,129},{2,130},{3,131},{4,132},{5,133},{6,134},{7,135},{8... | collective-permute-start | bytes 2359304 | tf_op jit(solution)/shard_map/ppermute | solution.py:30
  67.1 11.8 %collective-permute-start.4 = (f32[384,256]{1,0:T(8,128)S(1)}, f32[384,256]{1,0:T(8,128)S(1)}, u32[]{:S(2)}, u32[]{:S(2)}) collective-permute-start(f32[384,256]{1,0:T(8,128)S(1)} %get-tuple-element.21), channel_id=1, source_target_pairs={{0,64},{1,65},{2,66},{3,67},{4,68},{5,69},{6,70},{7,71},{8,72},{9,... | collective-permute-start | bytes 1179656 | tf_op jit(solution)/shard_map/ppermute | solution.py:30
  69.1 11.8 %collective-permute-start.6 = (f32[384,256]{1,0:T(8,128)S(1)}, f32[384,256]{1,0:T(8,128)S(1)}, u32[]{:S(2)}, u32[]{:S(2)}) collective-permute-start(f32[384,256]{1,0:T(8,128)S(1)} %get-tuple-element.22), channel_id=1, source_target_pairs={{0,192},{1,193},{2,194},{3,195},{4,196},{5,197},{6,198},{7,199},{8... | collective-permute-start | bytes 1179656 | tf_op jit(solution)/shard_map/ppermute | solution.py:30
  73.6 13.4 %collective-permute-start.9 = (f32[384,256]{1,0:T(8,128)S(1)}, f32[384,256]{1,0:T(8,128)S(1)}, u32[]{:S(2)}, u32[]{:S(2)}) collective-permute-start(f32[384,256]{1,0:T(8,128)S(1)} %get-tuple-element.21), channel_id=1, source_target_pairs={{0,192},{1,193},{2,194},{3,195},{4,196},{5,197},{6,198},{7,199},{8... | collective-permute-start | bytes 1179656 | tf_op jit(solution)/shard_map/ppermute | solution.py:30
  75.6 11.5 %collective-permute-start.8 = (f32[384,256]{1,0:T(8,128)S(1)}, f32[384,256]{1,0:T(8,128)S(1)}, u32[]{:S(2)}, u32[]{:S(2)}) collective-permute-start(f32[384,256]{1,0:T(8,128)S(1)} %get-tuple-element.22), channel_id=1, source_target_pairs={{0,64},{1,65},{2,66},{3,67},{4,68},{5,69},{6,70},{7,71},{8,72},{9,... | collective-permute-start | bytes 1179656 | tf_op jit(solution)/shard_map/ppermute | solution.py:30
  79.0 15.6 %collective-permute-start.5 = (f32[384,256]{1,0:T(8,128)S(1)}, f32[384,256]{1,0:T(8,128)S(1)}, u32[]{:S(2)}, u32[]{:S(2)}) collective-permute-start(f32[384,256]{1,0:T(8,128)S(1)} %collective-permute-done.4.refs_1_), channel_id=1, source_target_pairs={{0,64},{1,65},{2,66},{3,67},{4,68},{5,69},{6,70},{7,71},{8,72},{9,... | collective-permute-start | bytes 1179656 | tf_op jit(solution)/shard_map/ppermute | solution.py:30
  80.9 14.6 %collective-permute-start.7 = (f32[384,256]{1,0:T(8,128)S(1)}, f32[384,256]{1,0:T(8,128)S(1)}, u32[]{:S(2)}, u32[]{:S(2)}) collective-permute-start(f32[384,256]{1,0:T(8,128)S(1)} %collective-permute-done.6.refs_5_), channel_id=1, source_target_pairs={{0,192},{1,193},{2,194},{3,195},{4,196},{5,197},{6,198},{7,199},{8... | collective-permute-start | bytes 1179656 | tf_op jit(solution)/shard_map/ppermute | solution.py:30
  97.5 14.9 %collective-permute-start.10 = (f32[2,4,2,136,384]{4,3,2,1,0:T(8,128)S(1)}, f32[2,4,2,136,384]{4,3,2,1,0:T(8,128)S(1)}, u32[]{:S(2)}, u32[]{:S(2)}) collective-permute-start(f32[2,4,2,136,384]{4,3,2,1,0:T(8,128)S(1)} %gram.5), channel_id=1, source_target_pairs={{0,1},{1,0},{2,3},{3,2},{4,5},{5,4},{6,7},{7,6},{8,9},{9,8},{10,11... | collective-permute-start | bytes 10027016 | tf_op jit(solution)/shard_map/ppermute | solution.py:30
  112.8 22.9 %collective-permute-start.14 = (f32[2,2,136,384]{3,2,1,0:T(8,128)S(1)}, f32[2,2,136,384]{3,2,1,0:T(8,128)S(1)}, u32[]{:S(2)}, u32[]{:S(2)}) collective-permute-start(f32[2,2,136,384]{3,2,1,0:T(8,128)S(1)} %get-tuple-element.31), channel_id=1, source_target_pairs={{0,48},{1,49},{2,50},{3,51},{4,52},{5,53},{6,54},{7,55},{8,56},{9,... | collective-permute-start | bytes 2506760 | tf_op jit(solution)/shard_map/ppermute | solution.py:30
  117.2 21.4 %collective-permute-start.11 = (f32[2,2,136,384]{3,2,1,0:T(8,128)S(1)}, f32[2,2,136,384]{3,2,1,0:T(8,128)S(1)}, u32[]{:S(2)}, u32[]{:S(2)}) collective-permute-start(f32[2,2,136,384]{3,2,1,0:T(8,128)S(1)} %get-tuple-element.32), channel_id=1, source_target_pairs={{0,16},{1,17},{2,18},{3,19},{4,20},{5,21},{6,22},{7,23},{8,24},{9,... | collective-permute-start | bytes 2506760 | tf_op jit(solution)/shard_map/ppermute | solution.py:30
  138.8 12.7 %collective-permute-start.12 = (f32[2,136,384]{2,1,0:T(8,128)S(1)}, f32[2,136,384]{2,1,0:T(8,128)S(1)}, u32[]{:S(2)}, u32[]{:S(2)}) collective-permute-start(f32[2,136,384]{2,1,0:T(8,128)S(1)} %slice_bitcast_fusion.6), channel_id=1, source_target_pairs={{0,48},{1,49},{2,50},{3,51},{4,52},{5,53},{6,54},{7,55},{8,56},{9,... | collective-permute-start | bytes 1253384 | tf_op jit(solution)/shard_map/ppermute | solution.py:30
  141.0 36.4 %collective-permute-start.15 = (f32[2,136,384]{2,1,0:T(8,128)S(1)}, f32[2,136,384]{2,1,0:T(8,128)S(1)}, u32[]{:S(2)}, u32[]{:S(2)}) collective-permute-start(f32[2,136,384]{2,1,0:T(8,128)S(1)} %slice_bitcast_fusion.4), channel_id=1, source_target_pairs={{0,16},{1,17},{2,18},{3,19},{4,20},{5,21},{6,22},{7,23},{8,24},{9,... | collective-permute-start | bytes 1253384 | tf_op jit(solution)/shard_map/ppermute | solution.py:30
  151.6 36.3 %collective-permute-start.13 = (f32[136,384]{1,0:T(8,128)S(1)}, f32[136,384]{1,0:T(8,128)S(1)}, u32[]{:S(2)}, u32[]{:S(2)}) collective-permute-start(f32[136,384]{1,0:T(8,128)S(1)} %slice_bitcast_fusion.10), channel_id=1, source_target_pairs={{0,2},{1,3},{2,4},{3,5},{4,6},{5,7},{6,8},{7,9},{8,10},{9,11},{10,... | collective-permute-start | bytes 626696 | tf_op jit(solution)/shard_map/ppermute | solution.py:30
  177.5 10.5 %collective-permute-start.17 = (f32[136,384]{1,0:T(8,128)S(1)}, f32[136,384]{1,0:T(8,128)S(1)}, u32[]{:S(2)}, u32[]{:S(2)}) collective-permute-start(f32[136,384]{1,0:T(8,128)S(1)} %get-tuple-element.35), channel_id=1, source_target_pairs={{0,4},{1,269},{2,6},{3,271},{4,8},{5,1},{6,10},{7,3},{8,12},{9,5},... | collective-permute-start | bytes 626696 | tf_op jit(solution)/shard_map/ppermute | solution.py:30
  184.6 7.3 %collective-permute-start.16 = (f32[136,384]{1,0:T(8,128)S(1)}, f32[136,384]{1,0:T(8,128)S(1)}, u32[]{:S(2)}, u32[]{:S(2)}) collective-permute-start(f32[136,384]{1,0:T(8,128)S(1)} %get-tuple-element.36), channel_id=1, source_target_pairs={{0,270},{1,271},{2,0},{3,1},{4,2},{5,3},{6,4},{7,5},{8,6},{9,7},{1... | collective-permute-start | bytes 626696 | tf_op jit(solution)/shard_map/ppermute | solution.py:30
  192.5 16.2 %collective-permute-start.18 = (f32[40,384]{1,0:T(8,128)S(1)}, f32[40,384]{1,0:T(8,128)S(1)}, u32[]{:S(2)}, u32[]{:S(2)}) collective-permute-start(f32[40,384]{1,0:T(8,128)S(1)} %get-tuple-element.26), channel_id=1, source_target_pairs={{0,256},{1,257},{2,258},{3,259},{4,260},{5,261},{6,262},{7,263},{8... | collective-permute-start | bytes 184328 | tf_op jit(solution)/shard_map/ppermute | solution.py:30
  201.6 9.0 %collective-permute-start.19 = (f32[40,384]{1,0:T(8,128)S(1)}, f32[40,384]{1,0:T(8,128)S(1)}, u32[]{:S(2)}, u32[]{:S(2)}) collective-permute-start(f32[40,384]{1,0:T(8,128)S(1)} %get-tuple-element.27), channel_id=1, source_target_pairs={{0,264},{1,265},{2,266},{3,267},{4,268},{5,269},{6,270},{7,271},{8... | collective-permute-start | bytes 184328 | tf_op jit(solution)/shard_map/ppermute | solution.py:30
  203.5 9.2 %collective-permute-start.20 = (f32[40,384]{1,0:T(8,128)S(1)}, f32[40,384]{1,0:T(8,128)S(1)}, u32[]{:S(2)}, u32[]{:S(2)}) collective-permute-start(f32[40,384]{1,0:T(8,128)S(1)} %get-tuple-element.28), channel_id=1, source_target_pairs={{0,8},{1,9},{2,10},{3,11},{4,12},{5,13},{6,14},{7,15},{8,0},{9,1},... | collective-permute-start | bytes 184328 | tf_op jit(solution)/shard_map/ppermute | solution.py:30

commit v5 on v4

v5 whole, which is shorter than its diff:
```python
import functools
import math

import jax
import jax.numpy as jnp
import numpy as np
from jax import lax
from jax.experimental import pallas as pl
from jax.experimental.pallas import tpu as pltpu
from jax.sharding import PartitionSpec as P

AXES = {"zh": 2, "y": 4, "x": 4, "l2": 2, "r": 4, "core": 2}
FRAMES, PIX = ("zh", "y"), ("x", "l2", "r", "core")
SHIFTS = 5
ROWS = 6
ROOM = 384
VMEM = pl.BlockSpec(memory_space=pltpu.VMEM)
SMEM = pl.BlockSpec(memory_space=pltpu.SMEM)
PARAMS = pltpu.CompilerParams(vmem_limit_bytes=24 * 1024 * 1024)
F32 = jnp.float32


def send(value, **moves):
    names = tuple(AXES)
    sizes = tuple(AXES.values())
    pairs = []
    for source in range(math.prod(sizes)):
        at = dict(zip(names, (int(i) for i in np.unravel_index(source, sizes))))
        to = [moves[name](at) % AXES[name] if name in moves else at[name] for name in names]
        pairs.append((source, int(np.ravel_multi_index(to, sizes))))
    return lax.ppermute(value, names, pairs)


def along_z(by):
    def target(at):
        z = at["zh"] * 8 + at["l2"] * 4 + at["r"]
        return (z + (by(at["core"]) if callable(by) else by)) % 16

    return {
        "zh": lambda at: target(at) // 8,
        "l2": lambda at: target(at) // 4,
        "r": lambda at: target(at),
    }


def split2(value):
    high = value.astype(jnp.bfloat16)
    return high, (value - high.astype(F32)).astype(jnp.bfloat16)


def split3(value):
    high = value.astype(jnp.bfloat16)
    return (high, *split2(value - high.astype(F32)))


def as_bf16(value):
    return value.astype(F32).astype(jnp.bfloat16)


def spread(row, lines):
    return jnp.broadcast_to(row, (lines, row.shape[1]))


def dot_nn(left, right):
    return jnp.dot(left, right, preferred_element_type=F32)


def dot_nt(left, right):
    return lax.dot_general(left, right, (((1,), (1,)), ((), ())), preferred_element_type=F32)


def chosen(index, mask, begin, size):
    lanes = 128
    groups = mask.shape[1] // lanes
    padded = -(-groups // 16) * 16
    upper = lax.broadcasted_iota(jnp.int32, (padded, index.shape[1]), 0) == (index >> 7)
    lower = lax.broadcasted_iota(jnp.int32, (lanes, index.shape[1]), 0) == (index & (lanes - 1))
    times = dot_nt(as_bf16(upper), as_bf16(lower))
    rows = [mask[:, i * lanes : (i + 1) * lanes] for i in range(groups)]
    rows.append(jnp.zeros((padded - groups, lanes), jnp.int32))
    times = times * jnp.concatenate(rows, axis=0).astype(F32)
    used = as_bf16(times > 0)
    ahead = lax.broadcasted_iota(jnp.int32, (lanes, lanes), 0) < lax.broadcasted_iota(
        jnp.int32, (lanes, lanes), 1
    )
    above = lax.broadcasted_iota(jnp.int32, (padded, padded), 1) < lax.broadcasted_iota(
        jnp.int32, (padded, padded), 0
    )
    before = jnp.sum(dot_nn(as_bf16(above), used), axis=1, keepdims=True)
    number = dot_nn(used, as_bf16(ahead)) + before
    number = jnp.where(times > 0, number, -1.0).astype(jnp.int32)

    def in_line(value):
        return jnp.concatenate([value[i : i + 1] for i in range(groups)], axis=1)

    wanted = lax.broadcasted_iota(jnp.int32, (size, mask.shape[1]), 0) + begin
    total = jnp.sum(jnp.sum(used.astype(F32), axis=1, keepdims=True), axis=0, keepdims=True)
    return as_bf16(wanted == in_line(number)), in_line(times), total


def select_kernel(compact, flip, place, image, index, mask, out, weights, info):
    band = image.shape[1]
    size = out.shape[1]
    begin = (place[0] ^ flip) * size
    if compact:
        hot, times, total = chosen(index[...], mask[...], begin, size)
        picked = sum(dot_nt(part, hot) for part in reversed(split3(image[...])))
        weight = sum(dot_nt(part, hot) for part in reversed(split2(spread(times, 16))))
        over = jnp.where(total > 2.0 * size, 1.0, 0.0)
    else:
        columns = lax.broadcasted_iota(jnp.int32, (band, size), 0)
        hot = as_bf16(columns == index[:, pl.ds(pl.multiple_of(begin, size), size)])
        picked = sum(dot_nn(part, hot) for part in reversed(split3(image[...])))
        weight = dot_nn(spread(mask[...].astype(F32), 16).astype(jnp.bfloat16), hot)
        over = jnp.zeros((1, 1), F32)
    out[...] = picked
    weights[...] = weight
    count = jnp.sum(weight[0:1], axis=1, keepdims=True)
    line = lax.broadcasted_iota(jnp.int32, (8, 128), 0)
    info[...] = jnp.where(line == 0, count, over)


def select(compact, flip, place, image, index, mask):
    frames, band = image.shape
    size = ROOM if compact else index.shape[1] // 2
    return pl.pallas_call(
        functools.partial(select_kernel, compact, flip),
        out_shape=(
            jax.ShapeDtypeStruct((frames, size), F32),
            jax.ShapeDtypeStruct((16, size), F32),
            jax.ShapeDtypeStruct((8, 128), F32),
        ),
        in_specs=[SMEM, VMEM, VMEM, VMEM],
        out_specs=(VMEM, VMEM, VMEM),
        compiler_params=PARAMS,
        cost_estimate=pl.CostEstimate(
            flops=2 * frames * band * size * 3, bytes_accessed=frames * band * 4, transcendentals=0
        ),
        name="select",
    )(place, image, index, mask)


def gram_kernel(slots, shifts, place, info, weights, stay0, move0, *refs):
    last = shifts == (2,)
    backs, refs = (refs[:3], refs[3:]) if last else (refs[:6], refs[6:])
    previous, refs = refs[: -2 - len(slots)], refs[-2 - len(slots) :]
    outs, ordered, rows = refs[: len(slots)], refs[-2], refs[-1]
    zh, y, core, x, r = (place[i] for i in (0, 1, 2, 4, 5))
    frames, width = move0.shape
    owners = AXES["x"] * AXES["r"]
    mine = 2 * ROWS
    share_of = owners * mine
    size = len(slots) * share_of
    line = lax.broadcasted_iota(jnp.int32, (16, frames), 0)

    def terms(value):
        high, low = split2(value)
        return jnp.concatenate([high, low, high], axis=1)

    def blocks(back):
        if back == 0:
            return terms(stay0[...]), terms(move0[...])
        stay, one, two = backs[3:] if back == 3 else backs[:3]
        return terms(stay[...]), terms(jnp.concatenate([one[...], two[...]], axis=1))

    def place_of(owner):
        apart = x ^ (owner // AXES["r"])
        turn = (owner % AXES["r"] - r) & 3
        side = turn >> 1
        near = jnp.where(side == 0, 2, 1)
        chunk = jnp.where(apart == 3, 3 - near, jnp.where(apart == 1, near, apart + (apart >> 1)))
        return side, chunk, turn & 1

    for kind, left in enumerate((stay0[...], move0[...])):
        for at, slot in enumerate(slots):
            first = (core ^ slot) == 0
            for owner in range(owners):
                for l2 in range(2):
                    begin = owner // 4 * (frames // 4) + (l2 * 4 + owner % 4) * mine
                    to = at * share_of + owner * mine + l2 * ROWS
                    ordered[to : to + ROWS, :] = jnp.where(
                        first, left[begin : begin + ROWS], left[begin + ROWS : begin + mine]
                    )
        for begin, value in ((0, ordered[...] * weights[0:1]), (size, weights[...])):
            high, low = split2(value)
            rows[kind, begin : begin + value.shape[0], :] = jnp.concatenate(
                [high, high, low], axis=1
            )
    sums = jnp.where((line & 7) == SHIFTS, info[0:1, 0:1], 0.0)
    sums = jnp.where((line & 7) == SHIFTS + 1, info[1:2, 0:1], sums)
    if last:
        for out, before in zip(outs, previous):
            out[...] = before[...]
    here = None if last else blocks(0)
    for shift in shifts:
        if shift == 4:
            flip, right = 1, here
        else:
            flip = (y < shift).astype(jnp.int32)
            right = here if shift == 0 else blocks(shift)
        stay, move = (dot_nt(rows[kind ^ flip], right[kind]) for kind in range(2))
        swap = (zh ^ flip) == 1
        tiles = jnp.where(swap, move, stay), jnp.where(swap, stay, move)
        for label in range(2):
            sums = jnp.where(line == label * 8 + shift, tiles[label][size : size + 1], sums)
        for at, out in enumerate(outs):
            for owner in range(owners):
                begin = at * share_of + owner * mine
                out[(*place_of(owner), slice(shift * 24, shift * 24 + 24))] = jnp.concatenate(
                    [tile[begin : begin + mine] for tile in tiles], axis=0
                )
    for out in outs:
        for owner in range(owners):
            where = (*place_of(owner), slice(120, 136))
            out[where] = jnp.where((line & 7) == 2, sums, out[where]) if last else sums


def gram(slots, shifts, place, info, weights, stay0, move0, backs, previous=()):
    frames, width = move0.shape
    operands = [place, info, weights, stay0, move0, *backs, *previous]
    result = jax.ShapeDtypeStruct((2, AXES["x"], 2, 136, frames), F32)
    lines = len(slots) * frames // 2
    return pl.pallas_call(
        functools.partial(gram_kernel, slots, shifts),
        out_shape=(result,) * len(slots),
        in_specs=[SMEM] + [VMEM] * (len(operands) - 1),
        out_specs=(VMEM,) * len(slots),
        scratch_shapes=[
            pltpu.VMEM((lines, width), F32),
            pltpu.VMEM((2, lines + 16, 3 * width), jnp.bfloat16),
        ],
        compiler_params=PARAMS,
        cost_estimate=pl.CostEstimate(
            flops=len(slots) * len(shifts) * 2 * frames * frames * width * 3,
            bytes_accessed=6 * frames * width * 4 + len(slots) * 5 * frames * frames * 4,
            transcendentals=0,
        ),
        name="gram",
    )(*operands)


def share_kernel(place, near, below, above, two, *outs):
    total = (near[0] + below[...]) + (above[...] + two[...])
    out = outs[-1]
    for zh in range(2):
        for l2 in range(2):
            to = (zh ^ place[0]) * 2 + (l2 ^ place[6])
            for shift in range(SHIFTS):
                begin = shift * 24 + zh * 12 + l2 * ROWS
                out[to, shift * ROWS : (shift + 1) * ROWS] = total[begin : begin + ROWS]
            out[to, 30:32] = jnp.zeros((2, total.shape[1]), F32)
            out[to, 32:40] = total[120 + zh * 8 : 128 + zh * 8]
    for to in range(4):
        outs[to][...] = out[to]


def share(place, *parts):
    frames = parts[-1].shape[-1]
    return pl.pallas_call(
        share_kernel,
        out_shape=(jax.ShapeDtypeStruct((40, frames), F32),) * 4,
        in_specs=[SMEM] + [VMEM] * 4,
        out_specs=(VMEM,) * 4,
        scratch_shapes=[pltpu.VMEM((4, 40, frames), F32)],
        compiler_params=PARAMS,
        name="share",
    )(place, *parts)


def finish_kernel(place, one, two, three, four, out, missing):
    total = (one[...] + two[...]) + (three[...] + four[...])
    frames = total.shape[1]
    sums = total[32 : 32 + SHIFTS]
    good = total[32 + SHIFTS : 33 + SHIFTS]
    line = lax.broadcasted_iota(jnp.int32, (ROWS, frames), 0)
    lane = lax.broadcasted_iota(jnp.int32, (ROWS, frames), 1)
    mine = jnp.where(lane == line + place[3], sums[0:1], 0.0)
    own = jnp.sum(mine, axis=1, keepdims=True)
    for shift in range(SHIFTS):
        tile = total[shift * ROWS : (shift + 1) * ROWS]
        out[shift] = tile * good / (own * sums[shift : shift + 1])
    missing[...] = jnp.broadcast_to(total[33 + SHIFTS : 34 + SHIFTS, :128], (8, 128))


def finish(place, *parts):
    return pl.pallas_call(
        finish_kernel,
        out_shape=(
            jax.ShapeDtypeStruct((SHIFTS, ROWS, parts[0].shape[-1]), F32),
            jax.ShapeDtypeStruct((8, 128), F32),
        ),
        in_specs=[SMEM] + [VMEM] * 4,
        out_specs=(VMEM, VMEM),
        compiler_params=PARAMS,
        name="finish",
    )(place, *parts)


def correlate(compact, place, intensity, index, mask):
    def after(value, *others):
        return lax.optimization_barrier((value, *others))[0]

    def up(value):
        return send(value, y=lambda at: at["y"] + 1)

    def down(value):
        return send(value, y=lambda at: at["y"] - 1)

    given, *_ = select(compact, 0, place, intensity, index, mask)
    moved = send(given, zh=lambda at: at["zh"] + 1)
    kept, weights, info = select(compact, 1, place, intensity, after(index, given), mask)
    kept1, kept3 = up(kept), down(kept)
    kept2 = send(kept, y=lambda at: at["y"] + 2)
    half = 256
    one, two, *_ = lax.optimization_barrier(
        (moved[:, :half], moved[:, half:], kept1, kept2, kept3)
    )
    one1, two3 = up(one), down(two)
    two1, one3 = up(two), down(one)
    moved2 = (up(one1), down(two3))
    backs = (kept1, one1, two1, kept3, one3, two3)
    early = gram((1, 0), (0, 1, 3, 4), place, info, weights, kept, moved, backs)
    (give,) = gram((1,), (2,), place, info, weights, kept, moved, (kept2, *moved2), early[:1])
    (keep,) = gram((0,), (2,), place, info, weights, kept, moved, (kept2, *moved2), early[1:])

    def to_p(value):
        return send(value, x=lambda at: at["x"] ^ 1)

    def to_q(value):
        return send(value, x=lambda at: 3 - at["x"])

    total = keep + send(give, core=lambda at: 1 - at["core"])
    near = total[0, :2] + to_p(total[0, 2:])
    away = total[1, :2] + to_q(total[1, 2:])
    near = near[0] + to_q(near[1])
    away = away[0] + to_p(away[1])
    below = send(near[1], **along_z(1))
    above = send(away[1], **along_z(-1))
    middle = send(away[0], **along_z(lambda core: 2 - 4 * core))
    pieces = share(place, near, below, above, middle)
    far = send(pieces[2], zh=lambda at: at["zh"] + 1)
    farther = send(pieces[3], zh=lambda at: at["zh"] + 1, l2=lambda at: at["l2"] + 1)
    next_one = send(pieces[1], l2=lambda at: at["l2"] + 1)
    return finish(place, pieces[0], far, farther, next_one)


def body(intensity, circle_index, pixel_mask):
    place = jnp.stack(
        [
            lax.axis_index("zh"),
            lax.axis_index("y"),
            lax.axis_index("core"),
            lax.axis_index(PIX) * ROWS,
            lax.axis_index("x"),
            lax.axis_index("r"),
            lax.axis_index("l2"),
        ]
    ).astype(jnp.int32)
    operands = (place, intensity, circle_index[None, :], pixel_mask[None, :])
    result, missing = correlate(True, *operands)
    return lax.cond(
        missing[0, 0] > 0.5,
        lambda result, *operands: correlate(False, *operands)[0],
        lambda result, *operands: result,
        result,
        *operands,
    )


def solution(mesh):
    split = jax.sharding.Mesh(mesh.devices.reshape(tuple(AXES.values())), tuple(AXES))
    return jax.shard_map(
        body,
        mesh=split,
        in_specs=(P(FRAMES, PIX), P(PIX), P(PIX)),
        out_specs=P(None, (*FRAMES, *PIX), None),
        check_vma=False,
    )
```

time: 218 us -> 198 us (0.908)
  the two profiles are of different devices: /device:TPU:1 before, /device:TPU:64 now
where the time goes in v5:
time: 198 us; the launch traced here: 197 us
  starting transfers between devices  97.2 us (49%)
  waiting for transfers between devices  76.8 us (39%)
  Pallas kernels  19.4 us (10%)
  local copies, waits for them, and re-layouts  2.33 us (1%)
    ppermute x21, starting transfers between devices, send(): return lax.ppermute(value, names, pairs)  97.2 us
    ppermute x21, waiting for transfers between devices, send(): return lax.ppermute(value, names, pairs)  76.8 us
    pallas_call x2, Pallas kernels, select(): pl.pallas_call(functools.partial(select_kernel, compact, flip), out_shape...  9.19 us
    pallas_call x3, Pallas kernels, gram(): pl.pallas_call(functools.partial(gram_kernel, slots, shifts), out_shape=(...  8.95 us
  transfers between devices with their start and end apart: 21, of which 11 were waited for; matrix products, arithmetic and copies ran while one was open for 0% of the time, Pallas kernels for 6%

profile of v5, /device:TPU:64, one launch (start us, length us, event | category | flops | bytes accessed | tf_op | source)
XLA Modules:
  0.0 197.4 jit_solution(7502716432014472098)
XLA Ops:
  0.9 5.5 %select.6 = (f32[384,384]{1,0:T(8,128)S(1)}, f32[16,384]{1,0:T(8,128)}, f32[8,128]{1,0:T(8,128)}) custom-call(s32[7]{0:T(128)S(1)} %stack.31.place, f32[384,1536]{1,0:T(8,128)} %image.3, s32[1,1024]{1,0:T(1,128)} %bitcast.69, s32[1,1536]{1,0:T(1,128)S(1)} %broadcast_in_dim.7.mask), custom_call_target="tpu_custom_call" | custom-call | flops 1358954496 | bytes 2359296 | tf_op jit(solution)/shard_map/select/pallas_call | solution.py:126
  6.4 13.9 %collective-permute-start.21 = (f32[384,384]{1,0:T(8,128)S(1)}, f32[384,384]{1,0:T(8,128)S(1)}, u32[]{:S(2)}, u32[]{:S(2)}) collective-permute-start(f32[384,384]{1,0:T(8,128)S(1)} %get-tuple-element.50), channel_id=1, source_target_pairs={{0,256},{1,257},{2,258},{3,259},{4,260},{5,261},{6,262},{7,263},{8... | collective-permute-start | bytes 1769480 | tf_op jit(solution)/shard_map/ppermute | solution.py:31
  20.3 3.7 %select.7 = (f32[384,384]{1,0:T(8,128)S(1)}, f32[16,384]{1,0:T(8,128)S(1)}, f32[8,128]{1,0:T(8,128)S(1)}) custom-call(s32[7]{0:T(128)S(1)} %stack.31.place, f32[384,1536]{1,0:T(8,128)S(1)} %copy-done, s32[1,1024]{1,0:T(1,128)S(1)} %bitcast.70, s32[1,1536]{1,0:T(1,128)S(1)} %broadcast_in_dim.7.mask), custom_call_target="tpu_custom_call" | custom-call | flops 1358954496 | bytes 2359296 | tf_op jit(solution)/shard_map/select/pallas_call | solution.py:126
  24.1 4.9 %collective-permute-start.24 = (f32[384,384]{1,0:T(8,128)S(1)}, f32[384,384]{1,0:T(8,128)S(1)}, u32[]{:S(2)}, u32[]{:S(2)}) collective-permute-start(f32[384,384]{1,0:T(8,128)S(1)} %get-tuple-element.54.stay0), channel_id=1, source_target_pairs={{0,192},{1,193},{2,194},{3,195},{4,196},{5,197},{6,198},{7,199},{8... | collective-permute-start | bytes 1769480 | tf_op jit(solution)/shard_map/ppermute | solution.py:31
  29.0 1.9 collective-permute-start.23
  30.9 4.1 %collective-permute-start.22 = (f32[384,384]{1,0:T(8,128)S(1)}, f32[384,384]{1,0:T(8,128)S(1)}, u32[]{:S(2)}, u32[]{:S(2)}) collective-permute-start(f32[384,384]{1,0:T(8,128)S(1)} %get-tuple-element.54.stay0), channel_id=1, source_target_pairs={{0,128},{1,129},{2,130},{3,131},{4,132},{5,133},{6,134},{7,135},{8... | collective-permute-start | bytes 1769480 | tf_op jit(solution)/shard_map/ppermute | solution.py:31
  35.1 21.8 %collective-permute-done.21.move0 = f32[384,384]{1,0:T(8,128)S(1)} collective-permute-done((f32[384,384]{1,0:T(8,128)S(1)}, f32[384,384]{1,0:T(8,128)S(1)}, u32[]{:S(2)}, u32[]{:S(2)}) %collective-permute-start.21) | collective-permute-done | bytes 589856 | tf_op jit(solution)/shard_map/ppermute | solution.py:31
  56.9 2.3 %collective-permute-done.23.refs_0_ = f32[384,384]{1,0:T(8,128)S(1)} collective-permute-done((f32[384,384]{1,0:T(8,128)S(1)}, f32[384,384]{1,0:T(8,128)S(1)}, u32[]{:S(2)}, u32[]{:S(2)}) %collective-permute-start.23) | collective-permute-done | bytes 589856 | tf_op jit(solution)/shard_map/ppermute | solution.py:31
  61.2 5.1 %collective-permute-start.30 = (f32[384,256]{1,0:T(8,128)S(1)}, f32[384,256]{1,0:T(8,128)S(1)}, u32[]{:S(2)}, u32[]{:S(2)}) collective-permute-start(f32[384,256]{1,0:T(8,128)S(1)} %slice.108), channel_id=1, source_target_pairs={{0,192},{1,193},{2,194},{3,195},{4,196},{5,197},{6,198},{7,199},{8... | collective-permute-start | bytes 1179656 | tf_op jit(solution)/shard_map/ppermute | solution.py:31
  66.3 1.9 collective-permute-start.27
  68.3 3.9 %collective-permute-start.29 = (f32[384,128]{1,0:T(8,128)S(1)}, f32[384,128]{1,0:T(8,128)S(1)}, u32[]{:S(2)}, u32[]{:S(2)}) collective-permute-start(f32[384,128]{1,0:T(8,128)S(1)} %slice.109), channel_id=1, source_target_pairs={{0,64},{1,65},{2,66},{3,67},{4,68},{5,69},{6,70},{7,71},{8,72},{9,... | collective-permute-start | bytes 589832 | tf_op jit(solution)/shard_map/ppermute | solution.py:31
  74.1 2.2 %collective-permute-done.27.refs_5_ = f32[384,128]{1,0:T(8,128)S(1)} collective-permute-done((f32[384,128]{1,0:T(8,128)S(1)}, f32[384,128]{1,0:T(8,128)S(1)}, u32[]{:S(2)}, u32[]{:S(2)}) %collective-permute-start.27) | collective-permute-done | bytes 196640 | tf_op jit(solution)/shard_map/ppermute | solution.py:31
  76.3 5.5 %collective-permute-start.28 = (f32[384,128]{1,0:T(8,128)S(1)}, f32[384,128]{1,0:T(8,128)S(1)}, u32[]{:S(2)}, u32[]{:S(2)}) collective-permute-start(f32[384,128]{1,0:T(8,128)S(1)} %collective-permute-done.27.refs_5_), channel_id=1, source_target_pairs={{0,192},{1,193},{2,194},{3,195},{4,196},{5,197},{6,198},{7,199},{8... | collective-permute-start | bytes 589832 | tf_op jit(solution)/shard_map/ppermute | solution.py:31
  81.8 5.5 %gram.9 = (f32[2,4,2,136,384]{4,3,2,1,0:T(8,128)S(1)}, f32[2,4,2,136,384]{4,3,2,1,0:T(8,128)S(1)}) custom-call(s32[7]{0:T(128)S(1)} %stack.31.place, f32[8,128]{1,0:T(8,128)S(1)} %get-tuple-element.52.info, f32[16,384]{1,0:T(8,128)S(1)} %get-tuple-element.53.weights, f32[384,384]{1,0:T(8,128)S(1)} %get-tuple-element.54.stay0, ...), custom_call_target="tpu_custom_call" | custom-call | flops 2717908992 | bytes 9437184 | tf_op jit(solution)/shard_map/gram/pallas_call | solution.py:223
  89.0 2.1 %collective-permute-start.31 = (f32[2,4,2,136,384]{4,3,2,1,0:T(8,128)S(1)}, f32[2,4,2,136,384]{4,3,2,1,0:T(8,128)S(1)}, u32[]{:S(2)}, u32[]{:S(2)}) collective-permute-start(f32[2,4,2,136,384]{4,3,2,1,0:T(8,128)S(1)} %gram.11), channel_id=1, source_target_pairs={{0,1},{1,0},{2,3},{3,2},{4,5},{5,4},{6,7},{7,6},{8,9},{9,8},{10,11... | collective-permute-start | bytes 10027016 | tf_op jit(solution)/shard_map/ppermute | solution.py:31
  92.9 4.0 %collective-permute-done.31 = f32[2,4,2,136,384]{4,3,2,1,0:T(8,128)S(1)} collective-permute-done((f32[2,4,2,136,384]{4,3,2,1,0:T(8,128)S(1)}, f32[2,4,2,136,384]{4,3,2,1,0:T(8,128)S(1)}, u32[]{:S(2)}, u32[]{:S(2)}) %collective-permute-start.31) | collective-permute-done | bytes 3342368 | tf_op jit(solution)/shard_map/ppermute | solution.py:31
  97.3 4.7 %collective-permute-start.35 = (f32[2,2,136,384]{3,2,1,0:T(8,128)S(1)}, f32[2,2,136,384]{3,2,1,0:T(8,128)S(1)}, u32[]{:S(2)}, u32[]{:S(2)}) collective-permute-start(f32[2,2,136,384]{3,2,1,0:T(8,128)S(1)} %get-tuple-element.76), channel_id=1, source_target_pairs={{0,48},{1,49},{2,50},{3,51},{4,52},{5,53},{6,54},{7,55},{8,56},{9,... | collective-permute-start | bytes 2506760 | tf_op jit(solution)/shard_map/ppermute | solution.py:31
  102.0 2.1 %collective-permute-start.32 = (f32[2,2,136,384]{3,2,1,0:T(8,128)S(1)}, f32[2,2,136,384]{3,2,1,0:T(8,128)S(1)}, u32[]{:S(2)}, u32[]{:S(2)}) collective-permute-start(f32[2,2,136,384]{3,2,1,0:T(8,128)S(1)} %get-tuple-element.77), channel_id=1, source_target_pairs={{0,16},{1,17},{2,18},{3,19},{4,20},{5,21},{6,22},{7,23},{8,24},{9,... | collective-permute-start | bytes 2506760 | tf_op jit(solution)/shard_map/ppermute | solution.py:31
  104.2 16.9 %collective-permute-done.35 = f32[2,2,136,384]{3,2,1,0:T(8,128)S(1)} collective-permute-done((f32[2,2,136,384]{3,2,1,0:T(8,128)S(1)}, f32[2,2,136,384]{3,2,1,0:T(8,128)S(1)}, u32[]{:S(2)}, u32[]{:S(2)}) %collective-permute-start.35) | collective-permute-done | bytes 835616 | tf_op jit(solution)/shard_map/ppermute | solution.py:31
  121.1 3.2 %collective-permute-done.32 = f32[2,2,136,384]{3,2,1,0:T(8,128)S(1)} collective-permute-done((f32[2,2,136,384]{3,2,1,0:T(8,128)S(1)}, f32[2,2,136,384]{3,2,1,0:T(8,128)S(1)}, u32[]{:S(2)}, u32[]{:S(2)}) %collective-permute-start.32) | collective-permute-done | bytes 835616 | tf_op jit(solution)/shard_map/ppermute | solution.py:31
  124.5 2.4 %collective-permute-start.33 = (f32[2,136,384]{2,1,0:T(8,128)S(1)}, f32[2,136,384]{2,1,0:T(8,128)S(1)}, u32[]{:S(2)}, u32[]{:S(2)}) collective-permute-start(f32[2,136,384]{2,1,0:T(8,128)S(1)} %slice_bitcast_fusion.17), channel_id=1, source_target_pairs={{0,48},{1,49},{2,50},{3,51},{4,52},{5,53},{6,54},{7,55},{8,56},{9,... | collective-permute-start | bytes 1253384 | tf_op jit(solution)/shard_map/ppermute | solution.py:31
  127.0 2.2 %collective-permute-start.36 = (f32[2,136,384]{2,1,0:T(8,128)S(1)}, f32[2,136,384]{2,1,0:T(8,128)S(1)}, u32[]{:S(2)}, u32[]{:S(2)}) collective-permute-start(f32[2,136,384]{2,1,0:T(8,128)S(1)} %slice_bitcast_fusion.15), channel_id=1, source_target_pairs={{0,16},{1,17},{2,18},{3,19},{4,20},{5,21},{6,22},{7,23},{8,24},{9,... | collective-permute-start | bytes 1253384 | tf_op jit(solution)/shard_map/ppermute | solution.py:31
  129.2 9.0 %collective-permute-done.33 = f32[2,136,384]{2,1,0:T(8,128)S(1)} collective-permute-done((f32[2,136,384]{2,1,0:T(8,128)S(1)}, f32[2,136,384]{2,1,0:T(8,128)S(1)}, u32[]{:S(2)}, u32[]{:S(2)}) %collective-permute-start.33) | collective-permute-done | bytes 417824 | tf_op jit(solution)/shard_map/ppermute | solution.py:31
  138.3 9.5 %collective-permute-start.34 = (f32[136,384]{1,0:T(8,128)S(1)}, f32[136,384]{1,0:T(8,128)S(1)}, u32[]{:S(2)}, u32[]{:S(2)}) collective-permute-start(f32[136,384]{1,0:T(8,128)S(1)} %slice_bitcast_fusion.21), channel_id=1, source_target_pairs={{0,2},{1,3},{2,4},{3,5},{4,6},{5,7},{6,8},{7,9},{8,10},{9,11},{10,... | collective-permute-start | bytes 626696 | tf_op jit(solution)/shard_map/ppermute | solution.py:31
  147.9 5.5 %collective-permute-start.38 = (f32[136,384]{1,0:T(8,128)S(1)}, f32[136,384]{1,0:T(8,128)S(1)}, u32[]{:S(2)}, u32[]{:S(2)}) collective-permute-start(f32[136,384]{1,0:T(8,128)S(1)} %get-tuple-element.78), channel_id=1, source_target_pairs={{0,4},{1,269},{2,6},{3,271},{4,8},{5,1},{6,10},{7,3},{8,12},{9,5},... | collective-permute-start | bytes 626696 | tf_op jit(solution)/shard_map/ppermute | solution.py:31
  153.3 6.3 %collective-permute-start.37 = (f32[136,384]{1,0:T(8,128)S(1)}, f32[136,384]{1,0:T(8,128)S(1)}, u32[]{:S(2)}, u32[]{:S(2)}) collective-permute-start(f32[136,384]{1,0:T(8,128)S(1)} %get-tuple-element.79), channel_id=1, source_target_pairs={{0,270},{1,271},{2,0},{3,1},{4,2},{5,3},{6,4},{7,5},{8,6},{9,7},{1... | collective-permute-start | bytes 626696 | tf_op jit(solution)/shard_map/ppermute | solution.py:31
  159.6 5.8 %collective-permute-done.38.two = f32[136,384]{1,0:T(8,128)S(1)} collective-permute-done((f32[136,384]{1,0:T(8,128)S(1)}, f32[136,384]{1,0:T(8,128)S(1)}, u32[]{:S(2)}, u32[]{:S(2)}) %collective-permute-start.38) | collective-permute-done | bytes 208928 | tf_op jit(solution)/shard_map/ppermute | solution.py:31
  165.4 3.5 %collective-permute-done.37.above = f32[136,384]{1,0:T(8,128)S(1)} collective-permute-done((f32[136,384]{1,0:T(8,128)S(1)}, f32[136,384]{1,0:T(8,128)S(1)}, u32[]{:S(2)}, u32[]{:S(2)}) %collective-permute-start.37) | collective-permute-done | bytes 208928 | tf_op jit(solution)/shard_map/ppermute | solution.py:31
  169.5 9.0 %collective-permute-start.39 = (f32[40,384]{1,0:T(8,128)S(1)}, f32[40,384]{1,0:T(8,128)S(1)}, u32[]{:S(2)}, u32[]{:S(2)}) collective-permute-start(f32[40,384]{1,0:T(8,128)S(1)} %get-tuple-element.60), channel_id=1, source_target_pairs={{0,256},{1,257},{2,258},{3,259},{4,260},{5,261},{6,262},{7,263},{8... | collective-permute-start | bytes 184328 | tf_op jit(solution)/shard_map/ppermute | solution.py:31
  178.6 6.4 %collective-permute-start.40 = (f32[40,384]{1,0:T(8,128)S(1)}, f32[40,384]{1,0:T(8,128)S(1)}, u32[]{:S(2)}, u32[]{:S(2)}) collective-permute-start(f32[40,384]{1,0:T(8,128)S(1)} %get-tuple-element.61), channel_id=1, source_target_pairs={{0,264},{1,265},{2,266},{3,267},{4,268},{5,269},{6,270},{7,271},{8... | collective-permute-start | bytes 184328 | tf_op jit(solution)/shard_map/ppermute | solution.py:31
  186.9 2.9 %collective-permute-done.40.three = f32[40,384]{1,0:T(8,128)S(1)} collective-permute-done((f32[40,384]{1,0:T(8,128)S(1)}, f32[40,384]{1,0:T(8,128)S(1)}, u32[]{:S(2)}, u32[]{:S(2)}) %collective-permute-start.40) | collective-permute-done | bytes 61472 | tf_op jit(solution)/shard_map/ppermute | solution.py:31
  189.8 5.2 %collective-permute-done.41.four = f32[40,384]{1,0:T(8,128)S(1)} collective-permute-done((f32[40,384]{1,0:T(8,128)S(1)}, f32[40,384]{1,0:T(8,128)S(1)}, u32[]{:S(2)}, u32[]{:S(2)}) %collective-permute-start.41) | collective-permute-done | bytes 61472 | tf_op jit(solution)/shard_map/ppermute | solution.py:31
  (38 shorter events, 13.5 us)
Async XLA Ops:
  0.0 20.3 %copy-start = (f32[384,1536]{1,0:T(8,128)S(1)}, f32[384,1536]{1,0:T(8,128)}, u32[]{:S(2)}) copy-start(f32[384,1536]{1,0:T(8,128)} %image.3) | copy-start | bytes 7077892
  0.0 20.3 %copy-start.2 = (s32[1024]{0:T(1024)S(1)}, s32[1024]{0:T(1024)}, u32[]{:S(2)}) copy-start(s32[1024]{0:T(1024)} %param.6) | copy-start | bytes 12292
  6.4 50.5 %collective-permute-start.21 = (f32[384,384]{1,0:T(8,128)S(1)}, f32[384,384]{1,0:T(8,128)S(1)}, u32[]{:S(2)}, u32[]{:S(2)}) collective-permute-start(f32[384,384]{1,0:T(8,128)S(1)} %get-tuple-element.50), channel_id=1, source_target_pairs={{0,256},{1,257},{2,258},{3,259},{4,260},{5,261},{6,262},{7,263},{8... | collective-permute-start | bytes 1769480 | tf_op jit(solution)/shard_map/ppermute | solution.py:31
  24.1 32.9 %collective-permute-start.24 = (f32[384,384]{1,0:T(8,128)S(1)}, f32[384,384]{1,0:T(8,128)S(1)}, u32[]{:S(2)}, u32[]{:S(2)}) collective-permute-start(f32[384,384]{1,0:T(8,128)S(1)} %get-tuple-element.54.stay0), channel_id=1, source_target_pairs={{0,192},{1,193},{2,194},{3,195},{4,196},{5,197},{6,198},{7,199},{8... | collective-permute-start | bytes 1769480 | tf_op jit(solution)/shard_map/ppermute | solution.py:31
  29.0 30.3 %collective-permute-start.23 = (f32[384,384]{1,0:T(8,128)S(1)}, f32[384,384]{1,0:T(8,128)S(1)}, u32[]{:S(2)}, u32[]{:S(2)}) collective-permute-start(f32[384,384]{1,0:T(8,128)S(1)} %get-tuple-element.54.stay0), channel_id=1, source_target_pairs={{0,64},{1,65},{2,66},{3,67},{4,68},{5,69},{6,70},{7,71},{8,72},{9,... | collective-permute-start | bytes 1769480 | tf_op jit(solution)/shard_map/ppermute | solution.py:31
  30.9 28.3 %collective-permute-start.22 = (f32[384,384]{1,0:T(8,128)S(1)}, f32[384,384]{1,0:T(8,128)S(1)}, u32[]{:S(2)}, u32[]{:S(2)}) collective-permute-start(f32[384,384]{1,0:T(8,128)S(1)} %get-tuple-element.54.stay0), channel_id=1, source_target_pairs={{0,128},{1,129},{2,130},{3,131},{4,132},{5,133},{6,134},{7,135},{8... | collective-permute-start | bytes 1769480 | tf_op jit(solution)/shard_map/ppermute | solution.py:31
  59.3 12.9 %collective-permute-start.25 = (f32[384,256]{1,0:T(8,128)S(1)}, f32[384,256]{1,0:T(8,128)S(1)}, u32[]{:S(2)}, u32[]{:S(2)}) collective-permute-start(f32[384,256]{1,0:T(8,128)S(1)} %slice.108), channel_id=1, source_target_pairs={{0,64},{1,65},{2,66},{3,67},{4,68},{5,69},{6,70},{7,71},{8,72},{9,... | collective-permute-start | bytes 1179656 | tf_op jit(solution)/shard_map/ppermute | solution.py:31
  61.2 20.6 %collective-permute-start.30 = (f32[384,256]{1,0:T(8,128)S(1)}, f32[384,256]{1,0:T(8,128)S(1)}, u32[]{:S(2)}, u32[]{:S(2)}) collective-permute-start(f32[384,256]{1,0:T(8,128)S(1)} %slice.108), channel_id=1, source_target_pairs={{0,192},{1,193},{2,194},{3,195},{4,196},{5,197},{6,198},{7,199},{8... | collective-permute-start | bytes 1179656 | tf_op jit(solution)/shard_map/ppermute | solution.py:31
  66.3 10.0 %collective-permute-start.27 = (f32[384,128]{1,0:T(8,128)S(1)}, f32[384,128]{1,0:T(8,128)S(1)}, u32[]{:S(2)}, u32[]{:S(2)}) collective-permute-start(f32[384,128]{1,0:T(8,128)S(1)} %slice.109), channel_id=1, source_target_pairs={{0,192},{1,193},{2,194},{3,195},{4,196},{5,197},{6,198},{7,199},{8... | collective-permute-start | bytes 589832 | tf_op jit(solution)/shard_map/ppermute | solution.py:31
  68.3 13.5 %collective-permute-start.29 = (f32[384,128]{1,0:T(8,128)S(1)}, f32[384,128]{1,0:T(8,128)S(1)}, u32[]{:S(2)}, u32[]{:S(2)}) collective-permute-start(f32[384,128]{1,0:T(8,128)S(1)} %slice.109), channel_id=1, source_target_pairs={{0,64},{1,65},{2,66},{3,67},{4,68},{5,69},{6,70},{7,71},{8,72},{9,... | collective-permute-start | bytes 589832 | tf_op jit(solution)/shard_map/ppermute | solution.py:31
  72.2 15.1 %collective-permute-start.26 = (f32[384,256]{1,0:T(8,128)S(1)}, f32[384,256]{1,0:T(8,128)S(1)}, u32[]{:S(2)}, u32[]{:S(2)}) collective-permute-start(f32[384,256]{1,0:T(8,128)S(1)} %collective-permute-done.25.refs_1_), channel_id=1, source_target_pairs={{0,64},{1,65},{2,66},{3,67},{4,68},{5,69},{6,70},{7,71},{8,72},{9,... | collective-permute-start | bytes 1179656 | tf_op jit(solution)/shard_map/ppermute | solution.py:31
  76.3 11.0 %collective-permute-start.28 = (f32[384,128]{1,0:T(8,128)S(1)}, f32[384,128]{1,0:T(8,128)S(1)}, u32[]{:S(2)}, u32[]{:S(2)}) collective-permute-start(f32[384,128]{1,0:T(8,128)S(1)} %collective-permute-done.27.refs_5_), channel_id=1, source_target_pairs={{0,192},{1,193},{2,194},{3,195},{4,196},{5,197},{6,198},{7,199},{8... | collective-permute-start | bytes 589832 | tf_op jit(solution)/shard_map/ppermute | solution.py:31
  89.0 7.8 %collective-permute-start.31 = (f32[2,4,2,136,384]{4,3,2,1,0:T(8,128)S(1)}, f32[2,4,2,136,384]{4,3,2,1,0:T(8,128)S(1)}, u32[]{:S(2)}, u32[]{:S(2)}) collective-permute-start(f32[2,4,2,136,384]{4,3,2,1,0:T(8,128)S(1)} %gram.11), channel_id=1, source_target_pairs={{0,1},{1,0},{2,3},{3,2},{4,5},{5,4},{6,7},{7,6},{8,9},{9,8},{10,11... | collective-permute-start | bytes 10027016 | tf_op jit(solution)/shard_map/ppermute | solution.py:31
  97.3 23.7 %collective-permute-start.35 = (f32[2,2,136,384]{3,2,1,0:T(8,128)S(1)}, f32[2,2,136,384]{3,2,1,0:T(8,128)S(1)}, u32[]{:S(2)}, u32[]{:S(2)}) collective-permute-start(f32[2,2,136,384]{3,2,1,0:T(8,128)S(1)} %get-tuple-element.76), channel_id=1, source_target_pairs={{0,48},{1,49},{2,50},{3,51},{4,52},{5,53},{6,54},{7,55},{8,56},{9,... | collective-permute-start | bytes 2506760 | tf_op jit(solution)/shard_map/ppermute | solution.py:31
  102.0 22.2 %collective-permute-start.32 = (f32[2,2,136,384]{3,2,1,0:T(8,128)S(1)}, f32[2,2,136,384]{3,2,1,0:T(8,128)S(1)}, u32[]{:S(2)}, u32[]{:S(2)}) collective-permute-start(f32[2,2,136,384]{3,2,1,0:T(8,128)S(1)} %get-tuple-element.77), channel_id=1, source_target_pairs={{0,16},{1,17},{2,18},{3,19},{4,20},{5,21},{6,22},{7,23},{8,24},{9,... | collective-permute-start | bytes 2506760 | tf_op jit(solution)/shard_map/ppermute | solution.py:31
  124.5 13.6 %collective-permute-start.33 = (f32[2,136,384]{2,1,0:T(8,128)S(1)}, f32[2,136,384]{2,1,0:T(8,128)S(1)}, u32[]{:S(2)}, u32[]{:S(2)}) collective-permute-start(f32[2,136,384]{2,1,0:T(8,128)S(1)} %slice_bitcast_fusion.17), channel_id=1, source_target_pairs={{0,48},{1,49},{2,50},{3,51},{4,52},{5,53},{6,54},{7,55},{8,56},{9,... | collective-permute-start | bytes 1253384 | tf_op jit(solution)/shard_map/ppermute | solution.py:31
  127.0 20.8 %collective-permute-start.36 = (f32[2,136,384]{2,1,0:T(8,128)S(1)}, f32[2,136,384]{2,1,0:T(8,128)S(1)}, u32[]{:S(2)}, u32[]{:S(2)}) collective-permute-start(f32[2,136,384]{2,1,0:T(8,128)S(1)} %slice_bitcast_fusion.15), channel_id=1, source_target_pairs={{0,16},{1,17},{2,18},{3,19},{4,20},{5,21},{6,22},{7,23},{8,24},{9,... | collective-permute-start | bytes 1253384 | tf_op jit(solution)/shard_map/ppermute | solution.py:31
  138.3 21.4 %collective-permute-start.34 = (f32[136,384]{1,0:T(8,128)S(1)}, f32[136,384]{1,0:T(8,128)S(1)}, u32[]{:S(2)}, u32[]{:S(2)}) collective-permute-start(f32[136,384]{1,0:T(8,128)S(1)} %slice_bitcast_fusion.21), channel_id=1, source_target_pairs={{0,2},{1,3},{2,4},{3,5},{4,6},{5,7},{6,8},{7,9},{8,10},{9,11},{10,... | collective-permute-start | bytes 626696 | tf_op jit(solution)/shard_map/ppermute | solution.py:31
  147.9 17.5 %collective-permute-start.38 = (f32[136,384]{1,0:T(8,128)S(1)}, f32[136,384]{1,0:T(8,128)S(1)}, u32[]{:S(2)}, u32[]{:S(2)}) collective-permute-start(f32[136,384]{1,0:T(8,128)S(1)} %get-tuple-element.78), channel_id=1, source_target_pairs={{0,4},{1,269},{2,6},{3,271},{4,8},{5,1},{6,10},{7,3},{8,12},{9,5},... | collective-permute-start | bytes 626696 | tf_op jit(solution)/shard_map/ppermute | solution.py:31
  153.3 15.5 %collective-permute-start.37 = (f32[136,384]{1,0:T(8,128)S(1)}, f32[136,384]{1,0:T(8,128)S(1)}, u32[]{:S(2)}, u32[]{:S(2)}) collective-permute-start(f32[136,384]{1,0:T(8,128)S(1)} %get-tuple-element.79), channel_id=1, source_target_pairs={{0,270},{1,271},{2,0},{3,1},{4,2},{5,3},{6,4},{7,5},{8,6},{9,7},{1... | collective-permute-start | bytes 626696 | tf_op jit(solution)/shard_map/ppermute | solution.py:31
  169.5 17.4 %collective-permute-start.39 = (f32[40,384]{1,0:T(8,128)S(1)}, f32[40,384]{1,0:T(8,128)S(1)}, u32[]{:S(2)}, u32[]{:S(2)}) collective-permute-start(f32[40,384]{1,0:T(8,128)S(1)} %get-tuple-element.60), channel_id=1, source_target_pairs={{0,256},{1,257},{2,258},{3,259},{4,260},{5,261},{6,262},{7,263},{8... | collective-permute-start | bytes 184328 | tf_op jit(solution)/shard_map/ppermute | solution.py:31
  178.6 11.2 %collective-permute-start.40 = (f32[40,384]{1,0:T(8,128)S(1)}, f32[40,384]{1,0:T(8,128)S(1)}, u32[]{:S(2)}, u32[]{:S(2)}) collective-permute-start(f32[40,384]{1,0:T(8,128)S(1)} %get-tuple-element.61), channel_id=1, source_target_pairs={{0,264},{1,265},{2,266},{3,267},{4,268},{5,269},{6,270},{7,271},{8... | collective-permute-start | bytes 184328 | tf_op jit(solution)/shard_map/ppermute | solution.py:31
  184.9 10.0 %collective-permute-start.41 = (f32[40,384]{1,0:T(8,128)S(1)}, f32[40,384]{1,0:T(8,128)S(1)}, u32[]{:S(2)}, u32[]{:S(2)}) collective-permute-start(f32[40,384]{1,0:T(8,128)S(1)} %get-tuple-element.62), channel_id=1, source_target_pairs={{0,8},{1,9},{2,10},{3,11},{4,12},{5,13},{6,14},{7,15},{8,0},{9,1},... | collective-permute-start | bytes 184328 | tf_op jit(solution)/shard_map/ppermute | solution.py:31
  196.8 0.6 copy-start.1

commit v6 on v5

--- a/solution.py
+++ b/solution.py
@@ -140,9 +140,8 @@
     )(place, image, index, mask)
 
 
-def gram_kernel(slots, shifts, place, info, weights, stay0, move0, *refs):
-    last = shifts == (2,)
-    backs, refs = (refs[:3], refs[3:]) if last else (refs[:6], refs[6:])
+def gram_kernel(slots, last, place, info, weights, stay0, move0, *refs):
+    backs, refs = (refs[:2], refs[2:]) if last else (refs[:4], refs[4:])
     previous, refs = refs[: -2 - len(slots)], refs[-2 - len(slots) :]
     outs, ordered, rows = refs[: len(slots)], refs[-2], refs[-1]
     zh, y, core, x, r = (place[i] for i in (0, 1, 2, 4, 5))
@@ -157,19 +156,14 @@
         high, low = split2(value)
         return jnp.concatenate([high, low, high], axis=1)
 
-    def blocks(back):
-        if back == 0:
-            return terms(stay0[...]), terms(move0[...])
-        stay, one, two = backs[3:] if back == 3 else backs[:3]
-        return terms(stay[...]), terms(jnp.concatenate([one[...], two[...]], axis=1))
-
-    def place_of(owner):
+    def blocks(pair):
+        return [terms(block[...]) for block in pair]
+
+    def place_of(owner, slot):
         apart = x ^ (owner // AXES["r"])
-        turn = (owner % AXES["r"] - r) & 3
-        side = turn >> 1
-        near = jnp.where(side == 0, 2, 1)
+        near = 2 - (core ^ slot)
         chunk = jnp.where(apart == 3, 3 - near, jnp.where(apart == 1, near, apart + (apart >> 1)))
-        return side, chunk, turn & 1
+        return chunk, (owner % AXES["r"] - r) & 3
 
     for kind, left in enumerate((stay0[...], move0[...])):
         for at, slot in enumerate(slots):
@@ -191,13 +185,19 @@
     if last:
         for out, before in zip(outs, previous):
             out[...] = before[...]
-    here = None if last else blocks(0)
-    for shift in shifts:
-        if shift == 4:
-            flip, right = 1, here
+    if last:
+        others = [(2, blocks(backs))]
+    else:
+        here = blocks((stay0, move0))
+        others = [(0, here), (4, here)]
+        others += [(1 + 2 * core, backs[:2]), (3 - 2 * core, backs[2:])]
+    for shift, right in others:
+        if isinstance(shift, int):
+            flip = 1 if shift == 4 else (y < shift).astype(jnp.int32)
+            begin_row = shift * 24
         else:
-            flip = (y < shift).astype(jnp.int32)
-            right = here if shift == 0 else blocks(shift)
+            flip, right = (y < shift).astype(jnp.int32), blocks(right)
+            begin_row = pl.multiple_of(shift * 24, 8)
         stay, move = (dot_nt(rows[kind ^ flip], right[kind]) for kind in range(2))
         swap = (zh ^ flip) == 1
         tiles = jnp.where(swap, move, stay), jnp.where(swap, stay, move)
@@ -206,22 +206,22 @@
         for at, out in enumerate(outs):
             for owner in range(owners):
                 begin = at * share_of + owner * mine
-                out[(*place_of(owner), slice(shift * 24, shift * 24 + 24))] = jnp.concatenate(
+                out[(*place_of(owner, slots[at]), pl.ds(begin_row, 24))] = jnp.concatenate(
                     [tile[begin : begin + mine] for tile in tiles], axis=0
                 )
-    for out in outs:
+    for slot, out in zip(slots, outs):
         for owner in range(owners):
-            where = (*place_of(owner), slice(120, 136))
+            where = (*place_of(owner, slot), slice(120, 136))
             out[where] = jnp.where((line & 7) == 2, sums, out[where]) if last else sums
 
 
-def gram(slots, shifts, place, info, weights, stay0, move0, backs, previous=()):
+def gram(slots, last, place, info, weights, stay0, move0, backs, previous=()):
     frames, width = move0.shape
     operands = [place, info, weights, stay0, move0, *backs, *previous]
-    result = jax.ShapeDtypeStruct((2, AXES["x"], 2, 136, frames), F32)
+    result = jax.ShapeDtypeStruct((AXES["x"], AXES["r"], 136, frames), F32)
     lines = len(slots) * frames // 2
     return pl.pallas_call(
-        functools.partial(gram_kernel, slots, shifts),
+        functools.partial(gram_kernel, slots, last),
         out_shape=(result,) * len(slots),
         in_specs=[SMEM] + [VMEM] * (len(operands) - 1),
         out_specs=(VMEM,) * len(slots),
@@ -231,7 +231,7 @@
         ],
         compiler_params=PARAMS,
         cost_estimate=pl.CostEstimate(
-            flops=len(slots) * len(shifts) * 2 * frames * frames * width * 3,
+            flops=len(slots) * (1 if last else 4) * 2 * frames * frames * width * 3,
             bytes_accessed=6 * frames * width * 4 + len(slots) * 5 * frames * frames * 4,
             transcendentals=0,
         ),
@@ -300,43 +300,34 @@
     def after(value, *others):
         return lax.optimization_barrier((value, *others))[0]
 
-    def up(value):
-        return send(value, y=lambda at: at["y"] + 1)
-
-    def down(value):
-        return send(value, y=lambda at: at["y"] - 1)
+    def first(value):
+        return send(value, y=lambda at: at["y"] + 1 - 2 * at["core"])
+
+    def second(value):
+        return send(value, y=lambda at: at["y"] - 1 + 2 * at["core"])
 
     given, *_ = select(compact, 0, place, intensity, index, mask)
     moved = send(given, zh=lambda at: at["zh"] + 1)
     kept, weights, info = select(compact, 1, place, intensity, after(index, given), mask)
-    kept1, kept3 = up(kept), down(kept)
-    kept2 = send(kept, y=lambda at: at["y"] + 2)
-    half = 256
-    one, two, *_ = lax.optimization_barrier(
-        (moved[:, :half], moved[:, half:], kept1, kept2, kept3)
-    )
-    one1, two3 = up(one), down(two)
-    two1, one3 = up(two), down(one)
-    moved2 = (up(one1), down(two3))
-    backs = (kept1, one1, two1, kept3, one3, two3)
-    early = gram((1, 0), (0, 1, 3, 4), place, info, weights, kept, moved, backs)
-    (give,) = gram((1,), (2,), place, info, weights, kept, moved, (kept2, *moved2), early[:1])
-    (keep,) = gram((0,), (2,), place, info, weights, kept, moved, (kept2, *moved2), early[1:])
-
-    def to_p(value):
-        return send(value, x=lambda at: at["x"] ^ 1)
-
-    def to_q(value):
-        return send(value, x=lambda at: 3 - at["x"])
+    kept_backs = first(kept), second(kept), send(kept, y=lambda at: at["y"] + 2)
+    moved = after(jnp.where(weights[0:1] > 0, moved, 0.0), *kept_backs)
+    moved_first, moved_second = first(moved), second(moved)
+    moved_opposite = first(moved_first)
+    blocks = (place, info, weights, kept, moved)
+    backs = (kept_backs[0], moved_first, kept_backs[1], moved_second)
+    early = gram((1, 0), False, *blocks, backs)
+    backs = (kept_backs[2], moved_opposite)
+    (give,) = gram((1,), True, *blocks, backs, early[:1])
+    (keep,) = gram((0,), True, *blocks, backs, early[1:])
 
     total = keep + send(give, core=lambda at: 1 - at["core"])
-    near = total[0, :2] + to_p(total[0, 2:])
-    away = total[1, :2] + to_q(total[1, 2:])
-    near = near[0] + to_q(near[1])
-    away = away[0] + to_p(away[1])
+    near = total[:2] + send(
+        total[2:], x=lambda at: 3 - at["x"] if at["core"] else at["x"] ^ 1
+    )
+    near = near[0] + send(near[1], x=lambda at: at["x"] ^ 1 if at["core"] else 3 - at["x"])
     below = send(near[1], **along_z(1))
-    above = send(away[1], **along_z(-1))
-    middle = send(away[0], **along_z(lambda core: 2 - 4 * core))
+    above = send(near[3], **along_z(-1))
+    middle = send(near[2], **along_z(lambda core: 2 - 4 * core))
     pieces = share(place, near, below, above, middle)
     far = send(pieces[2], zh=lambda at: at["zh"] + 1)
     farther = send(pieces[3], zh=lambda at: at["zh"] + 1, l2=lambda at: at["l2"] + 1)

time: 198 us -> 198 us (level)
  the two profiles are of different devices: /device:TPU:64 before, /device:TPU:1 now
where the time goes in v6:
time: 198 us; the launch traced here: 194 us
  starting transfers between devices  99.2 us (50%)
  waiting for transfers between devices  71.5 us (36%)
  Pallas kernels  19.6 us (10%)
  local copies, waits for them, and re-layouts  2.13 us (1%)
    ppermute x16, starting transfers between devices, send(): return lax.ppermute(value, names, pairs)  99.2 us
    ppermute x16, waiting for transfers between devices, send(): return lax.ppermute(value, names, pairs)  71.5 us
    pallas_call x2, Pallas kernels, select(): pl.pallas_call(functools.partial(select_kernel, compact, flip), out_shape...  9.34 us
    pallas_call x3, Pallas kernels, gram(): pl.pallas_call(functools.partial(gram_kernel, slots, last), out_shape=(re...  8.98 us
  transfers between devices with their start and end apart: 16, of which 11 were waited for; matrix products, arithmetic and copies ran while one was open for 0% of the time, Pallas kernels for 6%

profile of v6, /device:TPU:1, one launch (start us, length us, event | category | flops | bytes accessed | tf_op | source)
XLA Modules:
  0.0 194.1 jit_solution(18100163278225699527)
XLA Ops:
  0.8 5.6 %select.6 = (f32[384,384]{1,0:T(8,128)S(1)}, f32[16,384]{1,0:T(8,128)}, f32[8,128]{1,0:T(8,128)}) custom-call(s32[7]{0:T(128)S(1)} %stack.31.place, f32[384,1536]{1,0:T(8,128)} %image.3, s32[1,1024]{1,0:T(1,128)} %bitcast.33, s32[1,1536]{1,0:T(1,128)S(1)} %broadcast_in_dim.35.mask), custom_call_target="tpu_custom_call" | custom-call | flops 1358954496 | bytes 2359296 | tf_op jit(solution)/shard_map/select/pallas_call | solution.py:126
  6.4 16.3 %collective-permute-start.16 = (f32[384,384]{1,0:T(8,128)S(1)}, f32[384,384]{1,0:T(8,128)S(1)}, u32[]{:S(2)}, u32[]{:S(2)}) collective-permute-start(f32[384,384]{1,0:T(8,128)S(1)} %get-tuple-element.48), channel_id=1, source_target_pairs={{0,256},{1,257},{2,258},{3,259},{4,260},{5,261},{6,262},{7,263},{8... | collective-permute-start | bytes 1769480 | tf_op jit(solution)/shard_map/ppermute | solution.py:31
  22.7 3.7 %select.7 = (f32[384,384]{1,0:T(8,128)S(1)}, f32[16,384]{1,0:T(8,128)S(1)}, f32[8,128]{1,0:T(8,128)S(1)}) custom-call(s32[7]{0:T(128)S(1)} %stack.31.place, f32[384,1536]{1,0:T(8,128)S(1)} %copy-done, s32[1,1024]{1,0:T(1,128)S(1)} %bitcast.34, s32[1,1536]{1,0:T(1,128)S(1)} %broadcast_in_dim.35.mask), custom_call_target="tpu_custom_call" | custom-call | flops 1358954496 | bytes 2359296 | tf_op jit(solution)/shard_map/select/pallas_call | solution.py:126
  26.4 4.8 %collective-permute-start.19 = (f32[384,384]{1,0:T(8,128)S(1)}, f32[384,384]{1,0:T(8,128)S(1)}, u32[]{:S(2)}, u32[]{:S(2)}) collective-permute-start(f32[384,384]{1,0:T(8,128)S(1)} %get-tuple-element.52.stay0), channel_id=1, source_target_pairs={{0,128},{1,129},{2,130},{3,131},{4,132},{5,133},{6,134},{7,135},{8... | collective-permute-start | bytes 1769480 | tf_op jit(solution)/shard_map/ppermute | solution.py:31
  31.3 2.3 %collective-permute-start.18 = (f32[384,384]{1,0:T(8,128)S(1)}, f32[384,384]{1,0:T(8,128)S(1)}, u32[]{:S(2)}, u32[]{:S(2)}) collective-permute-start(f32[384,384]{1,0:T(8,128)S(1)} %get-tuple-element.52.stay0), channel_id=1, source_target_pairs={{0,192},{1,65},{2,194},{3,67},{4,196},{5,69},{6,198},{7,71},{8,200... | collective-permute-start | bytes 1769480 | tf_op jit(solution)/shard_map/ppermute | solution.py:31
  33.6 4.2 %collective-permute-start.17 = (f32[384,384]{1,0:T(8,128)S(1)}, f32[384,384]{1,0:T(8,128)S(1)}, u32[]{:S(2)}, u32[]{:S(2)}) collective-permute-start(f32[384,384]{1,0:T(8,128)S(1)} %get-tuple-element.52.stay0), channel_id=1, source_target_pairs={{0,64},{1,193},{2,66},{3,195},{4,68},{5,197},{6,70},{7,199},{8,72}... | collective-permute-start | bytes 1769480 | tf_op jit(solution)/shard_map/ppermute | solution.py:31
  37.8 1.2 collective-permute-done.16
  39.1 4.7 %collective-permute-done.19.refs_0_ = f32[384,384]{1,0:T(8,128)S(1)} collective-permute-done((f32[384,384]{1,0:T(8,128)S(1)}, f32[384,384]{1,0:T(8,128)S(1)}, u32[]{:S(2)}, u32[]{:S(2)}) %collective-permute-start.19) | collective-permute-done | bytes 589856 | tf_op jit(solution)/shard_map/ppermute | solution.py:31
  43.8 14.0 %collective-permute-done.18.refs_2_ = f32[384,384]{1,0:T(8,128)S(1)} collective-permute-done((f32[384,384]{1,0:T(8,128)S(1)}, f32[384,384]{1,0:T(8,128)S(1)}, u32[]{:S(2)}, u32[]{:S(2)}) %collective-permute-start.18) | collective-permute-done | bytes 589856 | tf_op jit(solution)/shard_map/ppermute | solution.py:31
  57.7 4.6 %collective-permute-start.20 = (f32[384,384]{1,0:T(8,128)S(1)}, f32[384,384]{1,0:T(8,128)S(1)}, u32[]{:S(2)}, u32[]{:S(2)}) collective-permute-start(f32[384,384]{1,0:T(8,128)S(1)} %broadcast_select_fusion.1.move0), channel_id=1, source_target_pairs={{0,64},{1,193},{2,66},{3,195},{4,68},{5,197},{6,70},{7,199},{8,72}... | collective-permute-start | bytes 1769480 | tf_op jit(solution)/shard_map/ppermute | solution.py:31
  62.4 1.9 collective-permute-start.22
  64.3 7.6 %collective-permute-done.20.refs_1_ = f32[384,384]{1,0:T(8,128)S(1)} collective-permute-done((f32[384,384]{1,0:T(8,128)S(1)}, f32[384,384]{1,0:T(8,128)S(1)}, u32[]{:S(2)}, u32[]{:S(2)}) %collective-permute-start.20) | collective-permute-done | bytes 589856 | tf_op jit(solution)/shard_map/ppermute | solution.py:31
  71.9 5.3 %collective-permute-start.21 = (f32[384,384]{1,0:T(8,128)S(1)}, f32[384,384]{1,0:T(8,128)S(1)}, u32[]{:S(2)}, u32[]{:S(2)}) collective-permute-start(f32[384,384]{1,0:T(8,128)S(1)} %collective-permute-done.20.refs_1_), channel_id=1, source_target_pairs={{0,64},{1,193},{2,66},{3,195},{4,68},{5,197},{6,70},{7,199},{8,72}... | collective-permute-start | bytes 1769480 | tf_op jit(solution)/shard_map/ppermute | solution.py:31
  77.3 5.5 %gram.9 = (f32[4,4,136,384]{3,2,1,0:T(8,128)S(1)}, f32[4,4,136,384]{3,2,1,0:T(8,128)S(1)}) custom-call(s32[7]{0:T(128)S(1)} %stack.31.place, f32[8,128]{1,0:T(8,128)S(1)} %get-tuple-element.50.info, f32[16,384]{1,0:T(8,128)S(1)} %get-tuple-element.51.weights, f32[384,384]{1,0:T(8,128)S(1)} %get-tuple-element.52.stay0, ...), custom_call_target="tpu_custom_call" | custom-call | flops 2717908992 | bytes 9437184 | tf_op jit(solution)/shard_map/gram/pallas_call | solution.py:223
  82.8 1.2 collective-permute-done.21.refs_1_
  84.1 1.7 gram.11
  85.8 5.5 %collective-permute-start.23 = (f32[4,4,136,384]{3,2,1,0:T(8,128)S(1)}, f32[4,4,136,384]{3,2,1,0:T(8,128)S(1)}, u32[]{:S(2)}, u32[]{:S(2)}) collective-permute-start(f32[4,4,136,384]{3,2,1,0:T(8,128)S(1)} %gram.11), channel_id=1, source_target_pairs={{0,1},{1,0},{2,3},{3,2},{4,5},{5,4},{6,7},{7,6},{8,9},{9,8},{10,11... | collective-permute-start | bytes 10027016 | tf_op jit(solution)/shard_map/ppermute | solution.py:31
  91.3 1.7 gram.10
  93.1 3.6 %collective-permute-done.23 = f32[4,4,136,384]{3,2,1,0:T(8,128)S(1)} collective-permute-done((f32[4,4,136,384]{3,2,1,0:T(8,128)S(1)}, f32[4,4,136,384]{3,2,1,0:T(8,128)S(1)}, u32[]{:S(2)}, u32[]{:S(2)}) %collective-permute-start.23) | collective-permute-done | bytes 3342368 | tf_op jit(solution)/shard_map/ppermute | solution.py:31
  97.1 4.4 %collective-permute-start.24 = (f32[2,4,136,384]{3,2,1,0:T(8,128)S(1)}, f32[2,4,136,384]{3,2,1,0:T(8,128)S(1)}, u32[]{:S(2)}, u32[]{:S(2)}) collective-permute-start(f32[2,4,136,384]{3,2,1,0:T(8,128)S(1)} %slice.68), channel_id=1, source_target_pairs={{0,16},{1,49},{2,18},{3,51},{4,20},{5,53},{6,22},{7,55},{8,24},{9,... | collective-permute-start | bytes 5013512 | tf_op jit(solution)/shard_map/ppermute | solution.py:31
  101.5 19.0 %collective-permute-done.24 = f32[2,4,136,384]{3,2,1,0:T(8,128)S(1)} collective-permute-done((f32[2,4,136,384]{3,2,1,0:T(8,128)S(1)}, f32[2,4,136,384]{3,2,1,0:T(8,128)S(1)}, u32[]{:S(2)}, u32[]{:S(2)}) %collective-permute-start.24) | collective-permute-done | bytes 1671200 | tf_op jit(solution)/shard_map/ppermute | solution.py:31
  120.9 2.2 %collective-permute-start.25 = (f32[4,136,384]{2,1,0:T(8,128)S(1)}, f32[4,136,384]{2,1,0:T(8,128)S(1)}, u32[]{:S(2)}, u32[]{:S(2)}) collective-permute-start(f32[4,136,384]{2,1,0:T(8,128)S(1)} %slice_bitcast_fusion.5), channel_id=1, source_target_pairs={{0,48},{1,17},{2,50},{3,19},{4,52},{5,21},{6,54},{7,23},{8,56},{9,... | collective-permute-start | bytes 2506760 | tf_op jit(solution)/shard_map/ppermute | solution.py:31
  123.1 11.3 %collective-permute-done.25 = f32[4,136,384]{2,1,0:T(8,128)S(1)} collective-permute-done((f32[4,136,384]{2,1,0:T(8,128)S(1)}, f32[4,136,384]{2,1,0:T(8,128)S(1)}, u32[]{:S(2)}, u32[]{:S(2)}) %collective-permute-start.25) | collective-permute-done | bytes 835616 | tf_op jit(solution)/shard_map/ppermute | solution.py:31
  134.6 26.1 %collective-permute-start.28 = (f32[136,384]{1,0:T(8,128)S(1)}, f32[136,384]{1,0:T(8,128)S(1)}, u32[]{:S(2)}, u32[]{:S(2)}) collective-permute-start(f32[136,384]{1,0:T(8,128)S(1)} %get-tuple-element.66), channel_id=1, source_target_pairs={{0,4},{1,269},{2,6},{3,271},{4,8},{5,1},{6,10},{7,3},{8,12},{9,5},... | collective-permute-start | bytes 626696 | tf_op jit(solution)/shard_map/ppermute | solution.py:31
  160.7 1.9 collective-permute-start.27
  162.6 3.4 %collective-permute-start.26 = (f32[136,384]{1,0:T(8,128)S(1)}, f32[136,384]{1,0:T(8,128)S(1)}, u32[]{:S(2)}, u32[]{:S(2)}) collective-permute-start(f32[136,384]{1,0:T(8,128)S(1)} %get-tuple-element.68), channel_id=1, source_target_pairs={{0,2},{1,3},{2,4},{3,5},{4,6},{5,7},{6,8},{7,9},{8,10},{9,11},{10,... | collective-permute-start | bytes 626696 | tf_op jit(solution)/shard_map/ppermute | solution.py:31
  166.0 1.9 collective-permute-done.27.above
  167.9 4.6 %collective-permute-done.26.below = f32[136,384]{1,0:T(8,128)S(1)} collective-permute-done((f32[136,384]{1,0:T(8,128)S(1)}, f32[136,384]{1,0:T(8,128)S(1)}, u32[]{:S(2)}, u32[]{:S(2)}) %collective-permute-start.26) | collective-permute-done | bytes 208928 | tf_op jit(solution)/shard_map/ppermute | solution.py:31
  173.2 3.5 %collective-permute-start.29 = (f32[40,384]{1,0:T(8,128)S(1)}, f32[40,384]{1,0:T(8,128)S(1)}, u32[]{:S(2)}, u32[]{:S(2)}) collective-permute-start(f32[40,384]{1,0:T(8,128)S(1)} %get-tuple-element.57), channel_id=1, source_target_pairs={{0,256},{1,257},{2,258},{3,259},{4,260},{5,261},{6,262},{7,263},{8... | collective-permute-start | bytes 184328 | tf_op jit(solution)/shard_map/ppermute | solution.py:31
  176.7 3.4 %collective-permute-start.30 = (f32[40,384]{1,0:T(8,128)S(1)}, f32[40,384]{1,0:T(8,128)S(1)}, u32[]{:S(2)}, u32[]{:S(2)}) collective-permute-start(f32[40,384]{1,0:T(8,128)S(1)} %get-tuple-element.58), channel_id=1, source_target_pairs={{0,264},{1,265},{2,266},{3,267},{4,268},{5,269},{6,270},{7,271},{8... | collective-permute-start | bytes 184328 | tf_op jit(solution)/shard_map/ppermute | solution.py:31
  180.1 9.3 %collective-permute-start.31 = (f32[40,384]{1,0:T(8,128)S(1)}, f32[40,384]{1,0:T(8,128)S(1)}, u32[]{:S(2)}, u32[]{:S(2)}) collective-permute-start(f32[40,384]{1,0:T(8,128)S(1)} %get-tuple-element.59), channel_id=1, source_target_pairs={{0,8},{1,9},{2,10},{3,11},{4,12},{5,13},{6,14},{7,15},{8,0},{9,1},... | collective-permute-start | bytes 184328 | tf_op jit(solution)/shard_map/ppermute | solution.py:31
  189.4 2.2 %collective-permute-done.31.four = f32[40,384]{1,0:T(8,128)S(1)} collective-permute-done((f32[40,384]{1,0:T(8,128)S(1)}, f32[40,384]{1,0:T(8,128)S(1)}, u32[]{:S(2)}, u32[]{:S(2)}) %collective-permute-start.31) | collective-permute-done | bytes 61472 | tf_op jit(solution)/shard_map/ppermute | solution.py:31
  (25 shorter events, 4.1 us)
Async XLA Ops:
  0.8 21.9 %copy-start = (f32[384,1536]{1,0:T(8,128)S(1)}, f32[384,1536]{1,0:T(8,128)}, u32[]{:S(2)}) copy-start(f32[384,1536]{1,0:T(8,128)} %image.3) | copy-start | bytes 7077892
  0.8 21.9 %copy-start.2 = (s32[1024]{0:T(1024)S(1)}, s32[1024]{0:T(1024)}, u32[]{:S(2)}) copy-start(s32[1024]{0:T(1024)} %param.6) | copy-start | bytes 12292
  6.4 32.6 %collective-permute-start.16 = (f32[384,384]{1,0:T(8,128)S(1)}, f32[384,384]{1,0:T(8,128)S(1)}, u32[]{:S(2)}, u32[]{:S(2)}) collective-permute-start(f32[384,384]{1,0:T(8,128)S(1)} %get-tuple-element.48), channel_id=1, source_target_pairs={{0,256},{1,257},{2,258},{3,259},{4,260},{5,261},{6,262},{7,263},{8... | collective-permute-start | bytes 1769480 | tf_op jit(solution)/shard_map/ppermute | solution.py:31
  26.4 17.3 %collective-permute-start.19 = (f32[384,384]{1,0:T(8,128)S(1)}, f32[384,384]{1,0:T(8,128)S(1)}, u32[]{:S(2)}, u32[]{:S(2)}) collective-permute-start(f32[384,384]{1,0:T(8,128)S(1)} %get-tuple-element.52.stay0), channel_id=1, source_target_pairs={{0,128},{1,129},{2,130},{3,131},{4,132},{5,133},{6,134},{7,135},{8... | collective-permute-start | bytes 1769480 | tf_op jit(solution)/shard_map/ppermute | solution.py:31
  31.3 26.5 %collective-permute-start.18 = (f32[384,384]{1,0:T(8,128)S(1)}, f32[384,384]{1,0:T(8,128)S(1)}, u32[]{:S(2)}, u32[]{:S(2)}) collective-permute-start(f32[384,384]{1,0:T(8,128)S(1)} %get-tuple-element.52.stay0), channel_id=1, source_target_pairs={{0,192},{1,65},{2,194},{3,67},{4,196},{5,69},{6,198},{7,71},{8,200... | collective-permute-start | bytes 1769480 | tf_op jit(solution)/shard_map/ppermute | solution.py:31
  33.6 24.1 %collective-permute-start.17 = (f32[384,384]{1,0:T(8,128)S(1)}, f32[384,384]{1,0:T(8,128)S(1)}, u32[]{:S(2)}, u32[]{:S(2)}) collective-permute-start(f32[384,384]{1,0:T(8,128)S(1)} %get-tuple-element.52.stay0), channel_id=1, source_target_pairs={{0,64},{1,193},{2,66},{3,195},{4,68},{5,197},{6,70},{7,199},{8,72}... | collective-permute-start | bytes 1769480 | tf_op jit(solution)/shard_map/ppermute | solution.py:31
  57.7 14.2 %collective-permute-start.20 = (f32[384,384]{1,0:T(8,128)S(1)}, f32[384,384]{1,0:T(8,128)S(1)}, u32[]{:S(2)}, u32[]{:S(2)}) collective-permute-start(f32[384,384]{1,0:T(8,128)S(1)} %broadcast_select_fusion.1.move0), channel_id=1, source_target_pairs={{0,64},{1,193},{2,66},{3,195},{4,68},{5,197},{6,70},{7,199},{8,72}... | collective-permute-start | bytes 1769480 | tf_op jit(solution)/shard_map/ppermute | solution.py:31
  62.4 14.9 %collective-permute-start.22 = (f32[384,384]{1,0:T(8,128)S(1)}, f32[384,384]{1,0:T(8,128)S(1)}, u32[]{:S(2)}, u32[]{:S(2)}) collective-permute-start(f32[384,384]{1,0:T(8,128)S(1)} %broadcast_select_fusion.1.move0), channel_id=1, source_target_pairs={{0,192},{1,65},{2,194},{3,67},{4,196},{5,69},{6,198},{7,71},{8,200... | collective-permute-start | bytes 1769480 | tf_op jit(solution)/shard_map/ppermute | solution.py:31
  71.9 12.1 %collective-permute-start.21 = (f32[384,384]{1,0:T(8,128)S(1)}, f32[384,384]{1,0:T(8,128)S(1)}, u32[]{:S(2)}, u32[]{:S(2)}) collective-permute-start(f32[384,384]{1,0:T(8,128)S(1)} %collective-permute-done.20.refs_1_), channel_id=1, source_target_pairs={{0,64},{1,193},{2,66},{3,195},{4,68},{5,197},{6,70},{7,199},{8,72}... | collective-permute-start | bytes 1769480 | tf_op jit(solution)/shard_map/ppermute | solution.py:31
  85.8 10.9 %collective-permute-start.23 = (f32[4,4,136,384]{3,2,1,0:T(8,128)S(1)}, f32[4,4,136,384]{3,2,1,0:T(8,128)S(1)}, u32[]{:S(2)}, u32[]{:S(2)}) collective-permute-start(f32[4,4,136,384]{3,2,1,0:T(8,128)S(1)} %gram.11), channel_id=1, source_target_pairs={{0,1},{1,0},{2,3},{3,2},{4,5},{5,4},{6,7},{7,6},{8,9},{9,8},{10,11... | collective-permute-start | bytes 10027016 | tf_op jit(solution)/shard_map/ppermute | solution.py:31
  97.1 23.4 %collective-permute-start.24 = (f32[2,4,136,384]{3,2,1,0:T(8,128)S(1)}, f32[2,4,136,384]{3,2,1,0:T(8,128)S(1)}, u32[]{:S(2)}, u32[]{:S(2)}) collective-permute-start(f32[2,4,136,384]{3,2,1,0:T(8,128)S(1)} %slice.68), channel_id=1, source_target_pairs={{0,16},{1,49},{2,18},{3,51},{4,20},{5,53},{6,22},{7,55},{8,24},{9,... | collective-permute-start | bytes 5013512 | tf_op jit(solution)/shard_map/ppermute | solution.py:31
  120.9 13.6 %collective-permute-start.25 = (f32[4,136,384]{2,1,0:T(8,128)S(1)}, f32[4,136,384]{2,1,0:T(8,128)S(1)}, u32[]{:S(2)}, u32[]{:S(2)}) collective-permute-start(f32[4,136,384]{2,1,0:T(8,128)S(1)} %slice_bitcast_fusion.5), channel_id=1, source_target_pairs={{0,48},{1,17},{2,50},{3,19},{4,52},{5,21},{6,54},{7,23},{8,56},{9,... | collective-permute-start | bytes 2506760 | tf_op jit(solution)/shard_map/ppermute | solution.py:31
  134.6 31.4 %collective-permute-start.28 = (f32[136,384]{1,0:T(8,128)S(1)}, f32[136,384]{1,0:T(8,128)S(1)}, u32[]{:S(2)}, u32[]{:S(2)}) collective-permute-start(f32[136,384]{1,0:T(8,128)S(1)} %get-tuple-element.66), channel_id=1, source_target_pairs={{0,4},{1,269},{2,6},{3,271},{4,8},{5,1},{6,10},{7,3},{8,12},{9,5},... | collective-permute-start | bytes 626696 | tf_op jit(solution)/shard_map/ppermute | solution.py:31
  160.7 7.2 %collective-permute-start.27 = (f32[136,384]{1,0:T(8,128)S(1)}, f32[136,384]{1,0:T(8,128)S(1)}, u32[]{:S(2)}, u32[]{:S(2)}) collective-permute-start(f32[136,384]{1,0:T(8,128)S(1)} %get-tuple-element.67), channel_id=1, source_target_pairs={{0,270},{1,271},{2,0},{3,1},{4,2},{5,3},{6,4},{7,5},{8,6},{9,7},{1... | collective-permute-start | bytes 626696 | tf_op jit(solution)/shard_map/ppermute | solution.py:31
  162.6 9.9 %collective-permute-start.26 = (f32[136,384]{1,0:T(8,128)S(1)}, f32[136,384]{1,0:T(8,128)S(1)}, u32[]{:S(2)}, u32[]{:S(2)}) collective-permute-start(f32[136,384]{1,0:T(8,128)S(1)} %get-tuple-element.68), channel_id=1, source_target_pairs={{0,2},{1,3},{2,4},{3,5},{4,6},{5,7},{6,8},{7,9},{8,10},{9,11},{10,... | collective-permute-start | bytes 626696 | tf_op jit(solution)/shard_map/ppermute | solution.py:31
  173.2 16.2 %collective-permute-start.29 = (f32[40,384]{1,0:T(8,128)S(1)}, f32[40,384]{1,0:T(8,128)S(1)}, u32[]{:S(2)}, u32[]{:S(2)}) collective-permute-start(f32[40,384]{1,0:T(8,128)S(1)} %get-tuple-element.57), channel_id=1, source_target_pairs={{0,256},{1,257},{2,258},{3,259},{4,260},{5,261},{6,262},{7,263},{8... | collective-permute-start | bytes 184328 | tf_op jit(solution)/shard_map/ppermute | solution.py:31
  176.7 12.7 %collective-permute-start.30 = (f32[40,384]{1,0:T(8,128)S(1)}, f32[40,384]{1,0:T(8,128)S(1)}, u32[]{:S(2)}, u32[]{:S(2)}) collective-permute-start(f32[40,384]{1,0:T(8,128)S(1)} %get-tuple-element.58), channel_id=1, source_target_pairs={{0,264},{1,265},{2,266},{3,267},{4,268},{5,269},{6,270},{7,271},{8... | collective-permute-start | bytes 184328 | tf_op jit(solution)/shard_map/ppermute | solution.py:31
  180.1 11.5 %collective-permute-start.31 = (f32[40,384]{1,0:T(8,128)S(1)}, f32[40,384]{1,0:T(8,128)S(1)}, u32[]{:S(2)}, u32[]{:S(2)}) collective-permute-start(f32[40,384]{1,0:T(8,128)S(1)} %get-tuple-element.59), channel_id=1, source_target_pairs={{0,8},{1,9},{2,10},{3,11},{4,12},{5,13},{6,14},{7,15},{8,0},{9,1},... | collective-permute-start | bytes 184328 | tf_op jit(solution)/shard_map/ppermute | solution.py:31
  193.4 0.6 copy-start.1

commit v7 on v6

--- a/solution.py
+++ b/solution.py
@@ -320,10 +320,9 @@
     (give,) = gram((1,), True, *blocks, backs, early[:1])
     (keep,) = gram((0,), True, *blocks, backs, early[1:])
 
-    total = keep + send(give, core=lambda at: 1 - at["core"])
-    near = total[:2] + send(
-        total[2:], x=lambda at: 3 - at["x"] if at["core"] else at["x"] ^ 1
-    )
+    away = keep[2:] + send(give[2:], core=lambda at: 1 - at["core"])
+    near = keep[:2] + send(give[:2], core=lambda at: 1 - at["core"])
+    near = near + send(away, x=lambda at: 3 - at["x"] if at["core"] else at["x"] ^ 1)
     near = near[0] + send(near[1], x=lambda at: at["x"] ^ 1 if at["core"] else 3 - at["x"])
     below = send(near[1], **along_z(1))
     above = send(near[3], **along_z(-1))

time: 198 us -> 196 us (0.990)
  waiting for transfers between devices: 71.5 us -> 68.1 us
    ppermute x16 -> x17, waiting for transfers between devices: 71.5 us -> 68.1 us  [send(): return lax.ppermute(value, names, pairs)]
    ppermute x16 -> x17, starting transfers between devices: 99.2 us -> 101 us  [send(): return lax.ppermute(value, names, pairs)]
  transfers between devices with their start and end apart: 16 -> 17, of which waited for: 11 -> 10; matrix products, arithmetic and copies ran while one was open for 0% -> 0% of each run, Pallas kernels for 6% -> 6%
where the time goes in v7:
time: 196 us; the launch traced here: 193 us
  starting transfers between devices  101 us (52%)
  waiting for transfers between devices  68.1 us (35%)
  Pallas kernels  19.6 us (10%)
  local copies, waits for them, and re-layouts  2.24 us (1%)
    ppermute x17, starting transfers between devices, send(): return lax.ppermute(value, names, pairs)  101 us
    ppermute x17, waiting for transfers between devices, send(): return lax.ppermute(value, names, pairs)  68.1 us
    pallas_call x2, Pallas kernels, select(): pl.pallas_call(functools.partial(select_kernel, compact, flip), out_shape...  9.34 us
    pallas_call x3, Pallas kernels, gram(): pl.pallas_call(functools.partial(gram_kernel, slots, last), out_shape=(re...  8.98 us
  transfers between devices with their start and end apart: 17, of which 10 were waited for; matrix products, arithmetic and copies ran while one was open for 0% of the time, Pallas kernels for 6%

profile of v7, /device:TPU:1, one launch (start us, length us, event | category | flops | bytes accessed | tf_op | source)
XLA Modules:
  0.0 192.5 jit_solution(6907730512687548410)
XLA Ops:
  0.8 5.6 %select.6 = (f32[384,384]{1,0:T(8,128)S(1)}, f32[16,384]{1,0:T(8,128)}, f32[8,128]{1,0:T(8,128)}) custom-call(s32[7]{0:T(128)S(1)} %stack.31.place, f32[384,1536]{1,0:T(8,128)} %image.3, s32[1,1024]{1,0:T(1,128)} %bitcast.33, s32[1,1536]{1,0:T(1,128)S(1)} %broadcast_in_dim.35.mask), custom_call_target="tpu_custom_call" | custom-call | flops 1358954496 | bytes 2359296 | tf_op jit(solution)/shard_map/select/pallas_call | solution.py:126
  6.4 16.3 %collective-permute-start.17 = (f32[384,384]{1,0:T(8,128)S(1)}, f32[384,384]{1,0:T(8,128)S(1)}, u32[]{:S(2)}, u32[]{:S(2)}) collective-permute-start(f32[384,384]{1,0:T(8,128)S(1)} %get-tuple-element.48), channel_id=1, source_target_pairs={{0,256},{1,257},{2,258},{3,259},{4,260},{5,261},{6,262},{7,263},{8... | collective-permute-start | bytes 1769480 | tf_op jit(solution)/shard_map/ppermute | solution.py:31
  22.7 3.7 %select.7 = (f32[384,384]{1,0:T(8,128)S(1)}, f32[16,384]{1,0:T(8,128)S(1)}, f32[8,128]{1,0:T(8,128)S(1)}) custom-call(s32[7]{0:T(128)S(1)} %stack.31.place, f32[384,1536]{1,0:T(8,128)S(1)} %copy-done, s32[1,1024]{1,0:T(1,128)S(1)} %bitcast.34, s32[1,1536]{1,0:T(1,128)S(1)} %broadcast_in_dim.35.mask), custom_call_target="tpu_custom_call" | custom-call | flops 1358954496 | bytes 2359296 | tf_op jit(solution)/shard_map/select/pallas_call | solution.py:126
  26.4 4.8 %collective-permute-start.20 = (f32[384,384]{1,0:T(8,128)S(1)}, f32[384,384]{1,0:T(8,128)S(1)}, u32[]{:S(2)}, u32[]{:S(2)}) collective-permute-start(f32[384,384]{1,0:T(8,128)S(1)} %get-tuple-element.52.stay0), channel_id=1, source_target_pairs={{0,128},{1,129},{2,130},{3,131},{4,132},{5,133},{6,134},{7,135},{8... | collective-permute-start | bytes 1769480 | tf_op jit(solution)/shard_map/ppermute | solution.py:31
  31.3 2.3 %collective-permute-start.19 = (f32[384,384]{1,0:T(8,128)S(1)}, f32[384,384]{1,0:T(8,128)S(1)}, u32[]{:S(2)}, u32[]{:S(2)}) collective-permute-start(f32[384,384]{1,0:T(8,128)S(1)} %get-tuple-element.52.stay0), channel_id=1, source_target_pairs={{0,192},{1,65},{2,194},{3,67},{4,196},{5,69},{6,198},{7,71},{8,200... | collective-permute-start | bytes 1769480 | tf_op jit(solution)/shard_map/ppermute | solution.py:31
  33.6 4.2 %collective-permute-start.18 = (f32[384,384]{1,0:T(8,128)S(1)}, f32[384,384]{1,0:T(8,128)S(1)}, u32[]{:S(2)}, u32[]{:S(2)}) collective-permute-start(f32[384,384]{1,0:T(8,128)S(1)} %get-tuple-element.52.stay0), channel_id=1, source_target_pairs={{0,64},{1,193},{2,66},{3,195},{4,68},{5,197},{6,70},{7,199},{8,72}... | collective-permute-start | bytes 1769480 | tf_op jit(solution)/shard_map/ppermute | solution.py:31
  37.8 1.2 collective-permute-done.17
  39.1 4.7 %collective-permute-done.20.refs_0_ = f32[384,384]{1,0:T(8,128)S(1)} collective-permute-done((f32[384,384]{1,0:T(8,128)S(1)}, f32[384,384]{1,0:T(8,128)S(1)}, u32[]{:S(2)}, u32[]{:S(2)}) %collective-permute-start.20) | collective-permute-done | bytes 589856 | tf_op jit(solution)/shard_map/ppermute | solution.py:31
  43.8 14.0 %collective-permute-done.19.refs_2_ = f32[384,384]{1,0:T(8,128)S(1)} collective-permute-done((f32[384,384]{1,0:T(8,128)S(1)}, f32[384,384]{1,0:T(8,128)S(1)}, u32[]{:S(2)}, u32[]{:S(2)}) %collective-permute-start.19) | collective-permute-done | bytes 589856 | tf_op jit(solution)/shard_map/ppermute | solution.py:31
  57.7 4.6 %collective-permute-start.21 = (f32[384,384]{1,0:T(8,128)S(1)}, f32[384,384]{1,0:T(8,128)S(1)}, u32[]{:S(2)}, u32[]{:S(2)}) collective-permute-start(f32[384,384]{1,0:T(8,128)S(1)} %broadcast_select_fusion.1.move0), channel_id=1, source_target_pairs={{0,64},{1,193},{2,66},{3,195},{4,68},{5,197},{6,70},{7,199},{8,72}... | collective-permute-start | bytes 1769480 | tf_op jit(solution)/shard_map/ppermute | solution.py:31
  62.4 1.9 collective-permute-start.23
  64.3 7.6 %collective-permute-done.21.refs_1_ = f32[384,384]{1,0:T(8,128)S(1)} collective-permute-done((f32[384,384]{1,0:T(8,128)S(1)}, f32[384,384]{1,0:T(8,128)S(1)}, u32[]{:S(2)}, u32[]{:S(2)}) %collective-permute-start.21) | collective-permute-done | bytes 589856 | tf_op jit(solution)/shard_map/ppermute | solution.py:31
  71.9 5.3 %collective-permute-start.22 = (f32[384,384]{1,0:T(8,128)S(1)}, f32[384,384]{1,0:T(8,128)S(1)}, u32[]{:S(2)}, u32[]{:S(2)}) collective-permute-start(f32[384,384]{1,0:T(8,128)S(1)} %collective-permute-done.21.refs_1_), channel_id=1, source_target_pairs={{0,64},{1,193},{2,66},{3,195},{4,68},{5,197},{6,70},{7,199},{8,72}... | collective-permute-start | bytes 1769480 | tf_op jit(solution)/shard_map/ppermute | solution.py:31
  77.3 5.5 %gram.9 = (f32[4,4,136,384]{3,2,1,0:T(8,128)S(1)}, f32[4,4,136,384]{3,2,1,0:T(8,128)S(1)}) custom-call(s32[7]{0:T(128)S(1)} %stack.31.place, f32[8,128]{1,0:T(8,128)S(1)} %get-tuple-element.50.info, f32[16,384]{1,0:T(8,128)S(1)} %get-tuple-element.51.weights, f32[384,384]{1,0:T(8,128)S(1)} %get-tuple-element.52.stay0, ...), custom_call_target="tpu_custom_call" | custom-call | flops 2717908992 | bytes 9437184 | tf_op jit(solution)/shard_map/gram/pallas_call | solution.py:223
  82.8 1.2 collective-permute-done.22.refs_1_
  84.1 1.7 gram.11
  86.0 5.4 %collective-permute-start.25 = (f32[2,4,136,384]{3,2,1,0:T(8,128)S(1)}, f32[2,4,136,384]{3,2,1,0:T(8,128)S(1)}, u32[]{:S(2)}, u32[]{:S(2)}) collective-permute-start(f32[2,4,136,384]{3,2,1,0:T(8,128)S(1)} %get-tuple-element.69), channel_id=1, source_target_pairs={{0,1},{1,0},{2,3},{3,2},{4,5},{5,4},{6,7},{7,6},{8,9},{9,8},{10,11... | collective-permute-start | bytes 5013512 | tf_op jit(solution)/shard_map/ppermute | solution.py:31
  91.4 2.1 %collective-permute-start.24 = (f32[2,4,136,384]{3,2,1,0:T(8,128)S(1)}, f32[2,4,136,384]{3,2,1,0:T(8,128)S(1)}, u32[]{:S(2)}, u32[]{:S(2)}) collective-permute-start(f32[2,4,136,384]{3,2,1,0:T(8,128)S(1)} %get-tuple-element.68), channel_id=1, source_target_pairs={{0,1},{1,0},{2,3},{3,2},{4,5},{5,4},{6,7},{7,6},{8,9},{9,8},{10,11... | collective-permute-start | bytes 5013512 | tf_op jit(solution)/shard_map/ppermute | solution.py:31
  93.5 1.7 gram.10
  95.4 4.4 %collective-permute-start.26 = (f32[2,4,136,384]{3,2,1,0:T(8,128)S(1)}, f32[2,4,136,384]{3,2,1,0:T(8,128)S(1)}, u32[]{:S(2)}, u32[]{:S(2)}) collective-permute-start(f32[2,4,136,384]{3,2,1,0:T(8,128)S(1)} %slice_add_fusion.2), channel_id=1, source_target_pairs={{0,16},{1,49},{2,18},{3,51},{4,20},{5,53},{6,22},{7,55},{8,24},{9,... | collective-permute-start | bytes 5013512 | tf_op jit(solution)/shard_map/ppermute | solution.py:31
  99.8 19.0 %collective-permute-done.26 = f32[2,4,136,384]{3,2,1,0:T(8,128)S(1)} collective-permute-done((f32[2,4,136,384]{3,2,1,0:T(8,128)S(1)}, f32[2,4,136,384]{3,2,1,0:T(8,128)S(1)}, u32[]{:S(2)}, u32[]{:S(2)}) %collective-permute-start.26) | collective-permute-done | bytes 1671200 | tf_op jit(solution)/shard_map/ppermute | solution.py:31
  119.1 2.2 %collective-permute-start.27 = (f32[4,136,384]{2,1,0:T(8,128)S(1)}, f32[4,136,384]{2,1,0:T(8,128)S(1)}, u32[]{:S(2)}, u32[]{:S(2)}) collective-permute-start(f32[4,136,384]{2,1,0:T(8,128)S(1)} %slice_bitcast_fusion.5), channel_id=1, source_target_pairs={{0,48},{1,17},{2,50},{3,19},{4,52},{5,21},{6,54},{7,23},{8,56},{9,... | collective-permute-start | bytes 2506760 | tf_op jit(solution)/shard_map/ppermute | solution.py:31
  121.3 11.3 %collective-permute-done.27 = f32[4,136,384]{2,1,0:T(8,128)S(1)} collective-permute-done((f32[4,136,384]{2,1,0:T(8,128)S(1)}, f32[4,136,384]{2,1,0:T(8,128)S(1)}, u32[]{:S(2)}, u32[]{:S(2)}) %collective-permute-start.27) | collective-permute-done | bytes 835616 | tf_op jit(solution)/shard_map/ppermute | solution.py:31
  132.8 26.1 %collective-permute-start.30 = (f32[136,384]{1,0:T(8,128)S(1)}, f32[136,384]{1,0:T(8,128)S(1)}, u32[]{:S(2)}, u32[]{:S(2)}) collective-permute-start(f32[136,384]{1,0:T(8,128)S(1)} %get-tuple-element.70), channel_id=1, source_target_pairs={{0,4},{1,269},{2,6},{3,271},{4,8},{5,1},{6,10},{7,3},{8,12},{9,5},... | collective-permute-start | bytes 626696 | tf_op jit(solution)/shard_map/ppermute | solution.py:31
  158.9 1.9 collective-permute-start.29
  160.9 3.4 %collective-permute-start.28 = (f32[136,384]{1,0:T(8,128)S(1)}, f32[136,384]{1,0:T(8,128)S(1)}, u32[]{:S(2)}, u32[]{:S(2)}) collective-permute-start(f32[136,384]{1,0:T(8,128)S(1)} %get-tuple-element.72), channel_id=1, source_target_pairs={{0,2},{1,3},{2,4},{3,5},{4,6},{5,7},{6,8},{7,9},{8,10},{9,11},{10,... | collective-permute-start | bytes 626696 | tf_op jit(solution)/shard_map/ppermute | solution.py:31
  164.2 2.0 %collective-permute-done.29.above = f32[136,384]{1,0:T(8,128)S(1)} collective-permute-done((f32[136,384]{1,0:T(8,128)S(1)}, f32[136,384]{1,0:T(8,128)S(1)}, u32[]{:S(2)}, u32[]{:S(2)}) %collective-permute-start.29) | collective-permute-done | bytes 208928 | tf_op jit(solution)/shard_map/ppermute | solution.py:31
  166.2 4.4 %collective-permute-done.28.below = f32[136,384]{1,0:T(8,128)S(1)} collective-permute-done((f32[136,384]{1,0:T(8,128)S(1)}, f32[136,384]{1,0:T(8,128)S(1)}, u32[]{:S(2)}, u32[]{:S(2)}) %collective-permute-start.28) | collective-permute-done | bytes 208928 | tf_op jit(solution)/shard_map/ppermute | solution.py:31
  171.3 3.6 %collective-permute-start.31 = (f32[40,384]{1,0:T(8,128)S(1)}, f32[40,384]{1,0:T(8,128)S(1)}, u32[]{:S(2)}, u32[]{:S(2)}) collective-permute-start(f32[40,384]{1,0:T(8,128)S(1)} %get-tuple-element.57), channel_id=1, source_target_pairs={{0,256},{1,257},{2,258},{3,259},{4,260},{5,261},{6,262},{7,263},{8... | collective-permute-start | bytes 184328 | tf_op jit(solution)/shard_map/ppermute | solution.py:31
  174.9 3.3 %collective-permute-start.32 = (f32[40,384]{1,0:T(8,128)S(1)}, f32[40,384]{1,0:T(8,128)S(1)}, u32[]{:S(2)}, u32[]{:S(2)}) collective-permute-start(f32[40,384]{1,0:T(8,128)S(1)} %get-tuple-element.58), channel_id=1, source_target_pairs={{0,264},{1,265},{2,266},{3,267},{4,268},{5,269},{6,270},{7,271},{8... | collective-permute-start | bytes 184328 | tf_op jit(solution)/shard_map/ppermute | solution.py:31
  178.2 9.3 %collective-permute-start.33 = (f32[40,384]{1,0:T(8,128)S(1)}, f32[40,384]{1,0:T(8,128)S(1)}, u32[]{:S(2)}, u32[]{:S(2)}) collective-permute-start(f32[40,384]{1,0:T(8,128)S(1)} %get-tuple-element.59), channel_id=1, source_target_pairs={{0,8},{1,9},{2,10},{3,11},{4,12},{5,13},{6,14},{7,15},{8,0},{9,1},... | collective-permute-start | bytes 184328 | tf_op jit(solution)/shard_map/ppermute | solution.py:31
  187.5 2.6 %collective-permute-done.33.four = f32[40,384]{1,0:T(8,128)S(1)} collective-permute-done((f32[40,384]{1,0:T(8,128)S(1)}, f32[40,384]{1,0:T(8,128)S(1)}, u32[]{:S(2)}, u32[]{:S(2)}) %collective-permute-start.33) | collective-permute-done | bytes 61472 | tf_op jit(solution)/shard_map/ppermute | solution.py:31
  (27 shorter events, 4.1 us)
Async XLA Ops:
  0.8 21.9 %copy-start = (f32[384,1536]{1,0:T(8,128)S(1)}, f32[384,1536]{1,0:T(8,128)}, u32[]{:S(2)}) copy-start(f32[384,1536]{1,0:T(8,128)} %image.3) | copy-start | bytes 7077892
  0.8 21.9 %copy-start.2 = (s32[1024]{0:T(1024)S(1)}, s32[1024]{0:T(1024)}, u32[]{:S(2)}) copy-start(s32[1024]{0:T(1024)} %param.6) | copy-start | bytes 12292
  6.4 32.6 %collective-permute-start.17 = (f32[384,384]{1,0:T(8,128)S(1)}, f32[384,384]{1,0:T(8,128)S(1)}, u32[]{:S(2)}, u32[]{:S(2)}) collective-permute-start(f32[384,384]{1,0:T(8,128)S(1)} %get-tuple-element.48), channel_id=1, source_target_pairs={{0,256},{1,257},{2,258},{3,259},{4,260},{5,261},{6,262},{7,263},{8... | collective-permute-start | bytes 1769480 | tf_op jit(solution)/shard_map/ppermute | solution.py:31
  26.4 17.3 %collective-permute-start.20 = (f32[384,384]{1,0:T(8,128)S(1)}, f32[384,384]{1,0:T(8,128)S(1)}, u32[]{:S(2)}, u32[]{:S(2)}) collective-permute-start(f32[384,384]{1,0:T(8,128)S(1)} %get-tuple-element.52.stay0), channel_id=1, source_target_pairs={{0,128},{1,129},{2,130},{3,131},{4,132},{5,133},{6,134},{7,135},{8... | collective-permute-start | bytes 1769480 | tf_op jit(solution)/shard_map/ppermute | solution.py:31
  31.3 26.5 %collective-permute-start.19 = (f32[384,384]{1,0:T(8,128)S(1)}, f32[384,384]{1,0:T(8,128)S(1)}, u32[]{:S(2)}, u32[]{:S(2)}) collective-permute-start(f32[384,384]{1,0:T(8,128)S(1)} %get-tuple-element.52.stay0), channel_id=1, source_target_pairs={{0,192},{1,65},{2,194},{3,67},{4,196},{5,69},{6,198},{7,71},{8,200... | collective-permute-start | bytes 1769480 | tf_op jit(solution)/shard_map/ppermute | solution.py:31
  33.6 24.2 %collective-permute-start.18 = (f32[384,384]{1,0:T(8,128)S(1)}, f32[384,384]{1,0:T(8,128)S(1)}, u32[]{:S(2)}, u32[]{:S(2)}) collective-permute-start(f32[384,384]{1,0:T(8,128)S(1)} %get-tuple-element.52.stay0), channel_id=1, source_target_pairs={{0,64},{1,193},{2,66},{3,195},{4,68},{5,197},{6,70},{7,199},{8,72}... | collective-permute-start | bytes 1769480 | tf_op jit(solution)/shard_map/ppermute | solution.py:31
  57.7 14.2 %collective-permute-start.21 = (f32[384,384]{1,0:T(8,128)S(1)}, f32[384,384]{1,0:T(8,128)S(1)}, u32[]{:S(2)}, u32[]{:S(2)}) collective-permute-start(f32[384,384]{1,0:T(8,128)S(1)} %broadcast_select_fusion.1.move0), channel_id=1, source_target_pairs={{0,64},{1,193},{2,66},{3,195},{4,68},{5,197},{6,70},{7,199},{8,72}... | collective-permute-start | bytes 1769480 | tf_op jit(solution)/shard_map/ppermute | solution.py:31
  62.4 14.9 %collective-permute-start.23 = (f32[384,384]{1,0:T(8,128)S(1)}, f32[384,384]{1,0:T(8,128)S(1)}, u32[]{:S(2)}, u32[]{:S(2)}) collective-permute-start(f32[384,384]{1,0:T(8,128)S(1)} %broadcast_select_fusion.1.move0), channel_id=1, source_target_pairs={{0,192},{1,65},{2,194},{3,67},{4,196},{5,69},{6,198},{7,71},{8,200... | collective-permute-start | bytes 1769480 | tf_op jit(solution)/shard_map/ppermute | solution.py:31
  71.9 12.1 %collective-permute-start.22 = (f32[384,384]{1,0:T(8,128)S(1)}, f32[384,384]{1,0:T(8,128)S(1)}, u32[]{:S(2)}, u32[]{:S(2)}) collective-permute-start(f32[384,384]{1,0:T(8,128)S(1)} %collective-permute-done.21.refs_1_), channel_id=1, source_target_pairs={{0,64},{1,193},{2,66},{3,195},{4,68},{5,197},{6,70},{7,199},{8,72}... | collective-permute-start | bytes 1769480 | tf_op jit(solution)/shard_map/ppermute | solution.py:31
  86.0 9.2 %collective-permute-start.25 = (f32[2,4,136,384]{3,2,1,0:T(8,128)S(1)}, f32[2,4,136,384]{3,2,1,0:T(8,128)S(1)}, u32[]{:S(2)}, u32[]{:S(2)}) collective-permute-start(f32[2,4,136,384]{3,2,1,0:T(8,128)S(1)} %get-tuple-element.69), channel_id=1, source_target_pairs={{0,1},{1,0},{2,3},{3,2},{4,5},{5,4},{6,7},{7,6},{8,9},{9,8},{10,11... | collective-permute-start | bytes 5013512 | tf_op jit(solution)/shard_map/ppermute | solution.py:31
  91.4 8.4 %collective-permute-start.24 = (f32[2,4,136,384]{3,2,1,0:T(8,128)S(1)}, f32[2,4,136,384]{3,2,1,0:T(8,128)S(1)}, u32[]{:S(2)}, u32[]{:S(2)}) collective-permute-start(f32[2,4,136,384]{3,2,1,0:T(8,128)S(1)} %get-tuple-element.68), channel_id=1, source_target_pairs={{0,1},{1,0},{2,3},{3,2},{4,5},{5,4},{6,7},{7,6},{8,9},{9,8},{10,11... | collective-permute-start | bytes 5013512 | tf_op jit(solution)/shard_map/ppermute | solution.py:31
  95.4 23.4 %collective-permute-start.26 = (f32[2,4,136,384]{3,2,1,0:T(8,128)S(1)}, f32[2,4,136,384]{3,2,1,0:T(8,128)S(1)}, u32[]{:S(2)}, u32[]{:S(2)}) collective-permute-start(f32[2,4,136,384]{3,2,1,0:T(8,128)S(1)} %slice_add_fusion.2), channel_id=1, source_target_pairs={{0,16},{1,49},{2,18},{3,51},{4,20},{5,53},{6,22},{7,55},{8,24},{9,... | collective-permute-start | bytes 5013512 | tf_op jit(solution)/shard_map/ppermute | solution.py:31
  119.1 13.6 %collective-permute-start.27 = (f32[4,136,384]{2,1,0:T(8,128)S(1)}, f32[4,136,384]{2,1,0:T(8,128)S(1)}, u32[]{:S(2)}, u32[]{:S(2)}) collective-permute-start(f32[4,136,384]{2,1,0:T(8,128)S(1)} %slice_bitcast_fusion.5), channel_id=1, source_target_pairs={{0,48},{1,17},{2,50},{3,19},{4,52},{5,21},{6,54},{7,23},{8,56},{9,... | collective-permute-start | bytes 2506760 | tf_op jit(solution)/shard_map/ppermute | solution.py:31
  132.8 31.4 %collective-permute-start.30 = (f32[136,384]{1,0:T(8,128)S(1)}, f32[136,384]{1,0:T(8,128)S(1)}, u32[]{:S(2)}, u32[]{:S(2)}) collective-permute-start(f32[136,384]{1,0:T(8,128)S(1)} %get-tuple-element.70), channel_id=1, source_target_pairs={{0,4},{1,269},{2,6},{3,271},{4,8},{5,1},{6,10},{7,3},{8,12},{9,5},... | collective-permute-start | bytes 626696 | tf_op jit(solution)/shard_map/ppermute | solution.py:31
  158.9 7.3 %collective-permute-start.29 = (f32[136,384]{1,0:T(8,128)S(1)}, f32[136,384]{1,0:T(8,128)S(1)}, u32[]{:S(2)}, u32[]{:S(2)}) collective-permute-start(f32[136,384]{1,0:T(8,128)S(1)} %get-tuple-element.71), channel_id=1, source_target_pairs={{0,270},{1,271},{2,0},{3,1},{4,2},{5,3},{6,4},{7,5},{8,6},{9,7},{1... | collective-permute-start | bytes 626696 | tf_op jit(solution)/shard_map/ppermute | solution.py:31
  160.9 9.8 %collective-permute-start.28 = (f32[136,384]{1,0:T(8,128)S(1)}, f32[136,384]{1,0:T(8,128)S(1)}, u32[]{:S(2)}, u32[]{:S(2)}) collective-permute-start(f32[136,384]{1,0:T(8,128)S(1)} %get-tuple-element.72), channel_id=1, source_target_pairs={{0,2},{1,3},{2,4},{3,5},{4,6},{5,7},{6,8},{7,9},{8,10},{9,11},{10,... | collective-permute-start | bytes 626696 | tf_op jit(solution)/shard_map/ppermute | solution.py:31
  171.3 16.2 %collective-permute-start.31 = (f32[40,384]{1,0:T(8,128)S(1)}, f32[40,384]{1,0:T(8,128)S(1)}, u32[]{:S(2)}, u32[]{:S(2)}) collective-permute-start(f32[40,384]{1,0:T(8,128)S(1)} %get-tuple-element.57), channel_id=1, source_target_pairs={{0,256},{1,257},{2,258},{3,259},{4,260},{5,261},{6,262},{7,263},{8... | collective-permute-start | bytes 184328 | tf_op jit(solution)/shard_map/ppermute | solution.py:31
  174.9 12.6 %collective-permute-start.32 = (f32[40,384]{1,0:T(8,128)S(1)}, f32[40,384]{1,0:T(8,128)S(1)}, u32[]{:S(2)}, u32[]{:S(2)}) collective-permute-start(f32[40,384]{1,0:T(8,128)S(1)} %get-tuple-element.58), channel_id=1, source_target_pairs={{0,264},{1,265},{2,266},{3,267},{4,268},{5,269},{6,270},{7,271},{8... | collective-permute-start | bytes 184328 | tf_op jit(solution)/shard_map/ppermute | solution.py:31
  178.2 11.9 %collective-permute-start.33 = (f32[40,384]{1,0:T(8,128)S(1)}, f32[40,384]{1,0:T(8,128)S(1)}, u32[]{:S(2)}, u32[]{:S(2)}) collective-permute-start(f32[40,384]{1,0:T(8,128)S(1)} %get-tuple-element.59), channel_id=1, source_target_pairs={{0,8},{1,9},{2,10},{3,11},{4,12},{5,13},{6,14},{7,15},{8,0},{9,1},... | collective-permute-start | bytes 184328 | tf_op jit(solution)/shard_map/ppermute | solution.py:31
  191.9 0.6 copy-start.1

commit v8 on v7

--- a/solution.py
+++ b/solution.py
@@ -104,13 +104,13 @@
     begin = (place[0] ^ flip) * size
     if compact:
         hot, times, total = chosen(index[...], mask[...], begin, size)
-        picked = sum(dot_nt(part, hot) for part in reversed(split3(image[...])))
+        picked = sum(dot_nt(part, hot) for part in reversed(split2(image[...])))
         weight = sum(dot_nt(part, hot) for part in reversed(split2(spread(times, 16))))
         over = jnp.where(total > 2.0 * size, 1.0, 0.0)
     else:
         columns = lax.broadcasted_iota(jnp.int32, (band, size), 0)
         hot = as_bf16(columns == index[:, pl.ds(pl.multiple_of(begin, size), size)])
-        picked = sum(dot_nn(part, hot) for part in reversed(split3(image[...])))
+        picked = sum(dot_nn(part, hot) for part in reversed(split2(image[...])))
         weight = dot_nn(spread(mask[...].astype(F32), 16).astype(jnp.bfloat16), hot)
         over = jnp.zeros((1, 1), F32)
     out[...] = picked

time: 196 us -> 195 us (level)
  transfers between devices with their start and end apart: 17 -> 17, of which waited for: 10 -> 10; matrix products, arithmetic and copies ran while one was open for 0% -> 0% of each run, Pallas kernels for 6% -> 5%
where the time goes in v8:
time: 195 us; the launch traced here: 192 us
  starting transfers between devices  102 us (52%)
  waiting for transfers between devices  67.9 us (35%)
  Pallas kernels  18.4 us (9%)
  local copies, waits for them, and re-layouts  2.24 us (1%)
    ppermute x17, starting transfers between devices, send(): return lax.ppermute(value, names, pairs)  102 us
    ppermute x17, waiting for transfers between devices, send(): return lax.ppermute(value, names, pairs)  67.9 us
    pallas_call x3, Pallas kernels, gram(): pl.pallas_call(functools.partial(gram_kernel, slots, last), out_shape=(re...  8.98 us
    pallas_call x2, Pallas kernels, select(): pl.pallas_call(functools.partial(select_kernel, compact, flip), out_shape...  8.11 us
  transfers between devices with their start and end apart: 17, of which 10 were waited for; matrix products, arithmetic and copies ran while one was open for 0% of the time, Pallas kernels for 5%

profile of v8, /device:TPU:1, one launch (start us, length us, event | category | flops | bytes accessed | tf_op | source)
XLA Modules:
  0.0 191.7 jit_solution(2747327231018655745)
XLA Ops:
  0.8 5.0 %select.6 = (f32[384,384]{1,0:T(8,128)S(1)}, f32[16,384]{1,0:T(8,128)}, f32[8,128]{1,0:T(8,128)}) custom-call(s32[7]{0:T(128)S(1)} %stack.31.place, f32[384,1536]{1,0:T(8,128)} %image.3, s32[1,1024]{1,0:T(1,128)} %bitcast.33, s32[1,1536]{1,0:T(1,128)S(1)} %broadcast_in_dim.35.mask), custom_call_target="tpu_custom_call" | custom-call | flops 1358954496 | bytes 2359296 | tf_op jit(solution)/shard_map/select/pallas_call | solution.py:126
  5.8 16.3 %collective-permute-start.17 = (f32[384,384]{1,0:T(8,128)S(1)}, f32[384,384]{1,0:T(8,128)S(1)}, u32[]{:S(2)}, u32[]{:S(2)}) collective-permute-start(f32[384,384]{1,0:T(8,128)S(1)} %get-tuple-element.48), channel_id=1, source_target_pairs={{0,256},{1,257},{2,258},{3,259},{4,260},{5,261},{6,262},{7,263},{8... | collective-permute-start | bytes 1769480 | tf_op jit(solution)/shard_map/ppermute | solution.py:31
  22.1 3.1 %select.7 = (f32[384,384]{1,0:T(8,128)S(1)}, f32[16,384]{1,0:T(8,128)S(1)}, f32[8,128]{1,0:T(8,128)S(1)}) custom-call(s32[7]{0:T(128)S(1)} %stack.31.place, f32[384,1536]{1,0:T(8,128)S(1)} %copy-done, s32[1,1024]{1,0:T(1,128)S(1)} %bitcast.34, s32[1,1536]{1,0:T(1,128)S(1)} %broadcast_in_dim.35.mask), custom_call_target="tpu_custom_call" | custom-call | flops 1358954496 | bytes 2359296 | tf_op jit(solution)/shard_map/select/pallas_call | solution.py:126
  25.2 4.8 %collective-permute-start.20 = (f32[384,384]{1,0:T(8,128)S(1)}, f32[384,384]{1,0:T(8,128)S(1)}, u32[]{:S(2)}, u32[]{:S(2)}) collective-permute-start(f32[384,384]{1,0:T(8,128)S(1)} %get-tuple-element.52.stay0), channel_id=1, source_target_pairs={{0,128},{1,129},{2,130},{3,131},{4,132},{5,133},{6,134},{7,135},{8... | collective-permute-start | bytes 1769480 | tf_op jit(solution)/shard_map/ppermute | solution.py:31
  30.0 2.3 %collective-permute-start.19 = (f32[384,384]{1,0:T(8,128)S(1)}, f32[384,384]{1,0:T(8,128)S(1)}, u32[]{:S(2)}, u32[]{:S(2)}) collective-permute-start(f32[384,384]{1,0:T(8,128)S(1)} %get-tuple-element.52.stay0), channel_id=1, source_target_pairs={{0,192},{1,65},{2,194},{3,67},{4,196},{5,69},{6,198},{7,71},{8,200... | collective-permute-start | bytes 1769480 | tf_op jit(solution)/shard_map/ppermute | solution.py:31
  32.3 4.2 %collective-permute-start.18 = (f32[384,384]{1,0:T(8,128)S(1)}, f32[384,384]{1,0:T(8,128)S(1)}, u32[]{:S(2)}, u32[]{:S(2)}) collective-permute-start(f32[384,384]{1,0:T(8,128)S(1)} %get-tuple-element.52.stay0), channel_id=1, source_target_pairs={{0,64},{1,193},{2,66},{3,195},{4,68},{5,197},{6,70},{7,199},{8,72}... | collective-permute-start | bytes 1769480 | tf_op jit(solution)/shard_map/ppermute | solution.py:31
  36.6 1.8 collective-permute-done.17
  38.4 4.1 %collective-permute-done.20.refs_0_ = f32[384,384]{1,0:T(8,128)S(1)} collective-permute-done((f32[384,384]{1,0:T(8,128)S(1)}, f32[384,384]{1,0:T(8,128)S(1)}, u32[]{:S(2)}, u32[]{:S(2)}) %collective-permute-start.20) | collective-permute-done | bytes 589856 | tf_op jit(solution)/shard_map/ppermute | solution.py:31
  42.5 14.0 %collective-permute-done.19.refs_2_ = f32[384,384]{1,0:T(8,128)S(1)} collective-permute-done((f32[384,384]{1,0:T(8,128)S(1)}, f32[384,384]{1,0:T(8,128)S(1)}, u32[]{:S(2)}, u32[]{:S(2)}) %collective-permute-start.19) | collective-permute-done | bytes 589856 | tf_op jit(solution)/shard_map/ppermute | solution.py:31
  56.5 4.6 %collective-permute-start.21 = (f32[384,384]{1,0:T(8,128)S(1)}, f32[384,384]{1,0:T(8,128)S(1)}, u32[]{:S(2)}, u32[]{:S(2)}) collective-permute-start(f32[384,384]{1,0:T(8,128)S(1)} %broadcast_select_fusion.1.move0), channel_id=1, source_target_pairs={{0,64},{1,193},{2,66},{3,195},{4,68},{5,197},{6,70},{7,199},{8,72}... | collective-permute-start | bytes 1769480 | tf_op jit(solution)/shard_map/ppermute | solution.py:31
  61.1 1.9 %collective-permute-start.23 = (f32[384,384]{1,0:T(8,128)S(1)}, f32[384,384]{1,0:T(8,128)S(1)}, u32[]{:S(2)}, u32[]{:S(2)}) collective-permute-start(f32[384,384]{1,0:T(8,128)S(1)} %broadcast_select_fusion.1.move0), channel_id=1, source_target_pairs={{0,192},{1,65},{2,194},{3,67},{4,196},{5,69},{6,198},{7,71},{8,200... | collective-permute-start | bytes 1769480 | tf_op jit(solution)/shard_map/ppermute | solution.py:31
  63.1 7.6 %collective-permute-done.21.refs_1_ = f32[384,384]{1,0:T(8,128)S(1)} collective-permute-done((f32[384,384]{1,0:T(8,128)S(1)}, f32[384,384]{1,0:T(8,128)S(1)}, u32[]{:S(2)}, u32[]{:S(2)}) %collective-permute-start.21) | collective-permute-done | bytes 589856 | tf_op jit(solution)/shard_map/ppermute | solution.py:31
  70.7 5.3 %collective-permute-start.22 = (f32[384,384]{1,0:T(8,128)S(1)}, f32[384,384]{1,0:T(8,128)S(1)}, u32[]{:S(2)}, u32[]{:S(2)}) collective-permute-start(f32[384,384]{1,0:T(8,128)S(1)} %collective-permute-done.21.refs_1_), channel_id=1, source_target_pairs={{0,64},{1,193},{2,66},{3,195},{4,68},{5,197},{6,70},{7,199},{8,72}... | collective-permute-start | bytes 1769480 | tf_op jit(solution)/shard_map/ppermute | solution.py:31
  76.0 5.5 %gram.9 = (f32[4,4,136,384]{3,2,1,0:T(8,128)S(1)}, f32[4,4,136,384]{3,2,1,0:T(8,128)S(1)}) custom-call(s32[7]{0:T(128)S(1)} %stack.31.place, f32[8,128]{1,0:T(8,128)S(1)} %get-tuple-element.50.info, f32[16,384]{1,0:T(8,128)S(1)} %get-tuple-element.51.weights, f32[384,384]{1,0:T(8,128)S(1)} %get-tuple-element.52.stay0, ...), custom_call_target="tpu_custom_call" | custom-call | flops 2717908992 | bytes 9437184 | tf_op jit(solution)/shard_map/gram/pallas_call | solution.py:223
  81.6 1.2 collective-permute-done.22.refs_1_
  82.8 1.7 gram.11
  84.8 5.4 %collective-permute-start.25 = (f32[2,4,136,384]{3,2,1,0:T(8,128)S(1)}, f32[2,4,136,384]{3,2,1,0:T(8,128)S(1)}, u32[]{:S(2)}, u32[]{:S(2)}) collective-permute-start(f32[2,4,136,384]{3,2,1,0:T(8,128)S(1)} %get-tuple-element.69), channel_id=1, source_target_pairs={{0,1},{1,0},{2,3},{3,2},{4,5},{5,4},{6,7},{7,6},{8,9},{9,8},{10,11... | collective-permute-start | bytes 5013512 | tf_op jit(solution)/shard_map/ppermute | solution.py:31
  90.1 1.9 %collective-permute-start.24 = (f32[2,4,136,384]{3,2,1,0:T(8,128)S(1)}, f32[2,4,136,384]{3,2,1,0:T(8,128)S(1)}, u32[]{:S(2)}, u32[]{:S(2)}) collective-permute-start(f32[2,4,136,384]{3,2,1,0:T(8,128)S(1)} %get-tuple-element.68), channel_id=1, source_target_pairs={{0,1},{1,0},{2,3},{3,2},{4,5},{5,4},{6,7},{7,6},{8,9},{9,8},{10,11... | collective-permute-start | bytes 5013512 | tf_op jit(solution)/shard_map/ppermute | solution.py:31
  92.1 1.7 gram.10
  94.0 4.4 %collective-permute-start.26 = (f32[2,4,136,384]{3,2,1,0:T(8,128)S(1)}, f32[2,4,136,384]{3,2,1,0:T(8,128)S(1)}, u32[]{:S(2)}, u32[]{:S(2)}) collective-permute-start(f32[2,4,136,384]{3,2,1,0:T(8,128)S(1)} %slice_add_fusion.2), channel_id=1, source_target_pairs={{0,16},{1,49},{2,18},{3,51},{4,20},{5,53},{6,22},{7,55},{8,24},{9,... | collective-permute-start | bytes 5013512 | tf_op jit(solution)/shard_map/ppermute | solution.py:31
  98.4 19.0 %collective-permute-done.26 = f32[2,4,136,384]{3,2,1,0:T(8,128)S(1)} collective-permute-done((f32[2,4,136,384]{3,2,1,0:T(8,128)S(1)}, f32[2,4,136,384]{3,2,1,0:T(8,128)S(1)}, u32[]{:S(2)}, u32[]{:S(2)}) %collective-permute-start.26) | collective-permute-done | bytes 1671200 | tf_op jit(solution)/shard_map/ppermute | solution.py:31
  117.7 2.4 %collective-permute-start.27 = (f32[4,136,384]{2,1,0:T(8,128)S(1)}, f32[4,136,384]{2,1,0:T(8,128)S(1)}, u32[]{:S(2)}, u32[]{:S(2)}) collective-permute-start(f32[4,136,384]{2,1,0:T(8,128)S(1)} %slice_bitcast_fusion.5), channel_id=1, source_target_pairs={{0,48},{1,17},{2,50},{3,19},{4,52},{5,21},{6,54},{7,23},{8,56},{9,... | collective-permute-start | bytes 2506760 | tf_op jit(solution)/shard_map/ppermute | solution.py:31
  120.1 11.2 %collective-permute-done.27 = f32[4,136,384]{2,1,0:T(8,128)S(1)} collective-permute-done((f32[4,136,384]{2,1,0:T(8,128)S(1)}, f32[4,136,384]{2,1,0:T(8,128)S(1)}, u32[]{:S(2)}, u32[]{:S(2)}) %collective-permute-start.27) | collective-permute-done | bytes 835616 | tf_op jit(solution)/shard_map/ppermute | solution.py:31
  131.4 26.7 %collective-permute-start.30 = (f32[136,384]{1,0:T(8,128)S(1)}, f32[136,384]{1,0:T(8,128)S(1)}, u32[]{:S(2)}, u32[]{:S(2)}) collective-permute-start(f32[136,384]{1,0:T(8,128)S(1)} %get-tuple-element.70), channel_id=1, source_target_pairs={{0,4},{1,269},{2,6},{3,271},{4,8},{5,1},{6,10},{7,3},{8,12},{9,5},... | collective-permute-start | bytes 626696 | tf_op jit(solution)/shard_map/ppermute | solution.py:31
  158.1 1.9 %collective-permute-start.29 = (f32[136,384]{1,0:T(8,128)S(1)}, f32[136,384]{1,0:T(8,128)S(1)}, u32[]{:S(2)}, u32[]{:S(2)}) collective-permute-start(f32[136,384]{1,0:T(8,128)S(1)} %get-tuple-element.71), channel_id=1, source_target_pairs={{0,270},{1,271},{2,0},{3,1},{4,2},{5,3},{6,4},{7,5},{8,6},{9,7},{1... | collective-permute-start | bytes 626696 | tf_op jit(solution)/shard_map/ppermute | solution.py:31
  160.1 3.4 %collective-permute-start.28 = (f32[136,384]{1,0:T(8,128)S(1)}, f32[136,384]{1,0:T(8,128)S(1)}, u32[]{:S(2)}, u32[]{:S(2)}) collective-permute-start(f32[136,384]{1,0:T(8,128)S(1)} %get-tuple-element.72), channel_id=1, source_target_pairs={{0,2},{1,3},{2,4},{3,5},{4,6},{5,7},{6,8},{7,9},{8,10},{9,11},{10,... | collective-permute-start | bytes 626696 | tf_op jit(solution)/shard_map/ppermute | solution.py:31
  163.4 2.0 %collective-permute-done.29.above = f32[136,384]{1,0:T(8,128)S(1)} collective-permute-done((f32[136,384]{1,0:T(8,128)S(1)}, f32[136,384]{1,0:T(8,128)S(1)}, u32[]{:S(2)}, u32[]{:S(2)}) %collective-permute-start.29) | collective-permute-done | bytes 208928 | tf_op jit(solution)/shard_map/ppermute | solution.py:31
  165.4 4.4 %collective-permute-done.28.below = f32[136,384]{1,0:T(8,128)S(1)} collective-permute-done((f32[136,384]{1,0:T(8,128)S(1)}, f32[136,384]{1,0:T(8,128)S(1)}, u32[]{:S(2)}, u32[]{:S(2)}) %collective-permute-start.28) | collective-permute-done | bytes 208928 | tf_op jit(solution)/shard_map/ppermute | solution.py:31
  170.5 3.7 %collective-permute-start.31 = (f32[40,384]{1,0:T(8,128)S(1)}, f32[40,384]{1,0:T(8,128)S(1)}, u32[]{:S(2)}, u32[]{:S(2)}) collective-permute-start(f32[40,384]{1,0:T(8,128)S(1)} %get-tuple-element.57), channel_id=1, source_target_pairs={{0,256},{1,257},{2,258},{3,259},{4,260},{5,261},{6,262},{7,263},{8... | collective-permute-start | bytes 184328 | tf_op jit(solution)/shard_map/ppermute | solution.py:31
  174.1 3.3 %collective-permute-start.32 = (f32[40,384]{1,0:T(8,128)S(1)}, f32[40,384]{1,0:T(8,128)S(1)}, u32[]{:S(2)}, u32[]{:S(2)}) collective-permute-start(f32[40,384]{1,0:T(8,128)S(1)} %get-tuple-element.58), channel_id=1, source_target_pairs={{0,264},{1,265},{2,266},{3,267},{4,268},{5,269},{6,270},{7,271},{8... | collective-permute-start | bytes 184328 | tf_op jit(solution)/shard_map/ppermute | solution.py:31
  177.5 9.2 %collective-permute-start.33 = (f32[40,384]{1,0:T(8,128)S(1)}, f32[40,384]{1,0:T(8,128)S(1)}, u32[]{:S(2)}, u32[]{:S(2)}) collective-permute-start(f32[40,384]{1,0:T(8,128)S(1)} %get-tuple-element.59), channel_id=1, source_target_pairs={{0,8},{1,9},{2,10},{3,11},{4,12},{5,13},{6,14},{7,15},{8,0},{9,1},... | collective-permute-start | bytes 184328 | tf_op jit(solution)/shard_map/ppermute | solution.py:31
  186.7 2.5 %collective-permute-done.33.four = f32[40,384]{1,0:T(8,128)S(1)} collective-permute-done((f32[40,384]{1,0:T(8,128)S(1)}, f32[40,384]{1,0:T(8,128)S(1)}, u32[]{:S(2)}, u32[]{:S(2)}) %collective-permute-start.33) | collective-permute-done | bytes 61472 | tf_op jit(solution)/shard_map/ppermute | solution.py:31
  (27 shorter events, 4.1 us)
Async XLA Ops:
  0.8 21.3 %copy-start = (f32[384,1536]{1,0:T(8,128)S(1)}, f32[384,1536]{1,0:T(8,128)}, u32[]{:S(2)}) copy-start(f32[384,1536]{1,0:T(8,128)} %image.3) | copy-start | bytes 7077892
  0.8 21.3 %copy-start.2 = (s32[1024]{0:T(1024)S(1)}, s32[1024]{0:T(1024)}, u32[]{:S(2)}) copy-start(s32[1024]{0:T(1024)} %param.6) | copy-start | bytes 12292
  5.8 32.6 %collective-permute-start.17 = (f32[384,384]{1,0:T(8,128)S(1)}, f32[384,384]{1,0:T(8,128)S(1)}, u32[]{:S(2)}, u32[]{:S(2)}) collective-permute-start(f32[384,384]{1,0:T(8,128)S(1)} %get-tuple-element.48), channel_id=1, source_target_pairs={{0,256},{1,257},{2,258},{3,259},{4,260},{5,261},{6,262},{7,263},{8... | collective-permute-start | bytes 1769480 | tf_op jit(solution)/shard_map/ppermute | solution.py:31
  25.2 17.3 %collective-permute-start.20 = (f32[384,384]{1,0:T(8,128)S(1)}, f32[384,384]{1,0:T(8,128)S(1)}, u32[]{:S(2)}, u32[]{:S(2)}) collective-permute-start(f32[384,384]{1,0:T(8,128)S(1)} %get-tuple-element.52.stay0), channel_id=1, source_target_pairs={{0,128},{1,129},{2,130},{3,131},{4,132},{5,133},{6,134},{7,135},{8... | collective-permute-start | bytes 1769480 | tf_op jit(solution)/shard_map/ppermute | solution.py:31
  30.0 26.5 %collective-permute-start.19 = (f32[384,384]{1,0:T(8,128)S(1)}, f32[384,384]{1,0:T(8,128)S(1)}, u32[]{:S(2)}, u32[]{:S(2)}) collective-permute-start(f32[384,384]{1,0:T(8,128)S(1)} %get-tuple-element.52.stay0), channel_id=1, source_target_pairs={{0,192},{1,65},{2,194},{3,67},{4,196},{5,69},{6,198},{7,71},{8,200... | collective-permute-start | bytes 1769480 | tf_op jit(solution)/shard_map/ppermute | solution.py:31
  32.3 24.1 %collective-permute-start.18 = (f32[384,384]{1,0:T(8,128)S(1)}, f32[384,384]{1,0:T(8,128)S(1)}, u32[]{:S(2)}, u32[]{:S(2)}) collective-permute-start(f32[384,384]{1,0:T(8,128)S(1)} %get-tuple-element.52.stay0), channel_id=1, source_target_pairs={{0,64},{1,193},{2,66},{3,195},{4,68},{5,197},{6,70},{7,199},{8,72}... | collective-permute-start | bytes 1769480 | tf_op jit(solution)/shard_map/ppermute | solution.py:31
  56.5 14.2 %collective-permute-start.21 = (f32[384,384]{1,0:T(8,128)S(1)}, f32[384,384]{1,0:T(8,128)S(1)}, u32[]{:S(2)}, u32[]{:S(2)}) collective-permute-start(f32[384,384]{1,0:T(8,128)S(1)} %broadcast_select_fusion.1.move0), channel_id=1, source_target_pairs={{0,64},{1,193},{2,66},{3,195},{4,68},{5,197},{6,70},{7,199},{8,72}... | collective-permute-start | bytes 1769480 | tf_op jit(solution)/shard_map/ppermute | solution.py:31
  61.1 14.9 %collective-permute-start.23 = (f32[384,384]{1,0:T(8,128)S(1)}, f32[384,384]{1,0:T(8,128)S(1)}, u32[]{:S(2)}, u32[]{:S(2)}) collective-permute-start(f32[384,384]{1,0:T(8,128)S(1)} %broadcast_select_fusion.1.move0), channel_id=1, source_target_pairs={{0,192},{1,65},{2,194},{3,67},{4,196},{5,69},{6,198},{7,71},{8,200... | collective-permute-start | bytes 1769480 | tf_op jit(solution)/shard_map/ppermute | solution.py:31
  70.7 12.1 %collective-permute-start.22 = (f32[384,384]{1,0:T(8,128)S(1)}, f32[384,384]{1,0:T(8,128)S(1)}, u32[]{:S(2)}, u32[]{:S(2)}) collective-permute-start(f32[384,384]{1,0:T(8,128)S(1)} %collective-permute-done.21.refs_1_), channel_id=1, source_target_pairs={{0,64},{1,193},{2,66},{3,195},{4,68},{5,197},{6,70},{7,199},{8,72}... | collective-permute-start | bytes 1769480 | tf_op jit(solution)/shard_map/ppermute | solution.py:31
  84.8 9.0 %collective-permute-start.25 = (f32[2,4,136,384]{3,2,1,0:T(8,128)S(1)}, f32[2,4,136,384]{3,2,1,0:T(8,128)S(1)}, u32[]{:S(2)}, u32[]{:S(2)}) collective-permute-start(f32[2,4,136,384]{3,2,1,0:T(8,128)S(1)} %get-tuple-element.69), channel_id=1, source_target_pairs={{0,1},{1,0},{2,3},{3,2},{4,5},{5,4},{6,7},{7,6},{8,9},{9,8},{10,11... | collective-permute-start | bytes 5013512 | tf_op jit(solution)/shard_map/ppermute | solution.py:31
  90.1 8.2 %collective-permute-start.24 = (f32[2,4,136,384]{3,2,1,0:T(8,128)S(1)}, f32[2,4,136,384]{3,2,1,0:T(8,128)S(1)}, u32[]{:S(2)}, u32[]{:S(2)}) collective-permute-start(f32[2,4,136,384]{3,2,1,0:T(8,128)S(1)} %get-tuple-element.68), channel_id=1, source_target_pairs={{0,1},{1,0},{2,3},{3,2},{4,5},{5,4},{6,7},{7,6},{8,9},{9,8},{10,11... | collective-permute-start | bytes 5013512 | tf_op jit(solution)/shard_map/ppermute | solution.py:31
  94.0 23.4 %collective-permute-start.26 = (f32[2,4,136,384]{3,2,1,0:T(8,128)S(1)}, f32[2,4,136,384]{3,2,1,0:T(8,128)S(1)}, u32[]{:S(2)}, u32[]{:S(2)}) collective-permute-start(f32[2,4,136,384]{3,2,1,0:T(8,128)S(1)} %slice_add_fusion.2), channel_id=1, source_target_pairs={{0,16},{1,49},{2,18},{3,51},{4,20},{5,53},{6,22},{7,55},{8,24},{9,... | collective-permute-start | bytes 5013512 | tf_op jit(solution)/shard_map/ppermute | solution.py:31
  117.7 13.6 %collective-permute-start.27 = (f32[4,136,384]{2,1,0:T(8,128)S(1)}, f32[4,136,384]{2,1,0:T(8,128)S(1)}, u32[]{:S(2)}, u32[]{:S(2)}) collective-permute-start(f32[4,136,384]{2,1,0:T(8,128)S(1)} %slice_bitcast_fusion.5), channel_id=1, source_target_pairs={{0,48},{1,17},{2,50},{3,19},{4,52},{5,21},{6,54},{7,23},{8,56},{9,... | collective-permute-start | bytes 2506760 | tf_op jit(solution)/shard_map/ppermute | solution.py:31
  131.4 32.0 %collective-permute-start.30 = (f32[136,384]{1,0:T(8,128)S(1)}, f32[136,384]{1,0:T(8,128)S(1)}, u32[]{:S(2)}, u32[]{:S(2)}) collective-permute-start(f32[136,384]{1,0:T(8,128)S(1)} %get-tuple-element.70), channel_id=1, source_target_pairs={{0,4},{1,269},{2,6},{3,271},{4,8},{5,1},{6,10},{7,3},{8,12},{9,5},... | collective-permute-start | bytes 626696 | tf_op jit(solution)/shard_map/ppermute | solution.py:31
  158.1 7.3 %collective-permute-start.29 = (f32[136,384]{1,0:T(8,128)S(1)}, f32[136,384]{1,0:T(8,128)S(1)}, u32[]{:S(2)}, u32[]{:S(2)}) collective-permute-start(f32[136,384]{1,0:T(8,128)S(1)} %get-tuple-element.71), channel_id=1, source_target_pairs={{0,270},{1,271},{2,0},{3,1},{4,2},{5,3},{6,4},{7,5},{8,6},{9,7},{1... | collective-permute-start | bytes 626696 | tf_op jit(solution)/shard_map/ppermute | solution.py:31
  160.1 9.8 %collective-permute-start.28 = (f32[136,384]{1,0:T(8,128)S(1)}, f32[136,384]{1,0:T(8,128)S(1)}, u32[]{:S(2)}, u32[]{:S(2)}) collective-permute-start(f32[136,384]{1,0:T(8,128)S(1)} %get-tuple-element.72), channel_id=1, source_target_pairs={{0,2},{1,3},{2,4},{3,5},{4,6},{5,7},{6,8},{7,9},{8,10},{9,11},{10,... | collective-permute-start | bytes 626696 | tf_op jit(solution)/shard_map/ppermute | solution.py:31
  170.5 16.2 %collective-permute-start.31 = (f32[40,384]{1,0:T(8,128)S(1)}, f32[40,384]{1,0:T(8,128)S(1)}, u32[]{:S(2)}, u32[]{:S(2)}) collective-permute-start(f32[40,384]{1,0:T(8,128)S(1)} %get-tuple-element.57), channel_id=1, source_target_pairs={{0,256},{1,257},{2,258},{3,259},{4,260},{5,261},{6,262},{7,263},{8... | collective-permute-start | bytes 184328 | tf_op jit(solution)/shard_map/ppermute | solution.py:31
  174.1 12.6 %collective-permute-start.32 = (f32[40,384]{1,0:T(8,128)S(1)}, f32[40,384]{1,0:T(8,128)S(1)}, u32[]{:S(2)}, u32[]{:S(2)}) collective-permute-start(f32[40,384]{1,0:T(8,128)S(1)} %get-tuple-element.58), channel_id=1, source_target_pairs={{0,264},{1,265},{2,266},{3,267},{4,268},{5,269},{6,270},{7,271},{8... | collective-permute-start | bytes 184328 | tf_op jit(solution)/shard_map/ppermute | solution.py:31
  177.5 11.8 %collective-permute-start.33 = (f32[40,384]{1,0:T(8,128)S(1)}, f32[40,384]{1,0:T(8,128)S(1)}, u32[]{:S(2)}, u32[]{:S(2)}) collective-permute-start(f32[40,384]{1,0:T(8,128)S(1)} %get-tuple-element.59), channel_id=1, source_target_pairs={{0,8},{1,9},{2,10},{3,11},{4,12},{5,13},{6,14},{7,15},{8,0},{9,1},... | collective-permute-start | bytes 184328 | tf_op jit(solution)/shard_map/ppermute | solution.py:31
  191.1 0.6 copy-start.1
